TPU v7x, 256 devices: a whole 4x4x8 slice. The times are simulated.
256 devices in a mesh: member: 8 (over z), space: 32 (over y, x, core).
Axes of the slice: x: 4, y: 4, z: 8, core: 2. Of those that a mesh axis runs over, the one named last changes fastest.
Arguments:
- state: bfloat16 [128, 8, 4, 256, 512], P('member', None, None, 'space'), may hold values from -6 to 6
- wind_east: float32 [8, 4, 256, 512], P(None, None, 'space'), may hold values from 0.1 to 0.45
- wind_north: float32 [8, 4, 256, 512], P(None, None, 'space'), may hold values from -0.45 to 0.45
- obs_col: int32 [32, 8, 512], P('space', 'member'), may hold values from 0 to 16383
- obs_val: float32 [32, 8, 512], P('space', 'member'), may hold values from -6 to 6
- obs_rinv: float32 [32, 8, 512], P('space', 'member'), may hold values from 0.5 to 20
- obs_count: int32 [32, 8], P('space', 'member'), may hold values from 128 to 512, as said below
- loc_class: int32 [32, 8, 3, 512], P('space', 'member'), may hold values from 0 to 3
Outputs:
- analysed: bfloat16 [128, 8, 4, 256, 512], P('member', None, None, 'space')
Inputs may be any that keep to these rules, and one draw needn't show every extreme that they name: `obs_count`: a multiple of 128; some tile holds 512.
All inputs are finite; a program needn't handle non-finite values.
Results may differ from a plain program's by a relative error of at most 0.0066.
Values may be sent and summed in bfloat16 or wider, within the bound.
No kernel may reach another device: no remote copies, remote signals or barrier semaphores. Data moves between devices by JAX's collectives and lax.ppermute only.
A program may use at most 128 MiB of HBM per device.

v0:
```python
import jax
import jax.numpy as jnp
from jax import lax
from jax.sharding import PartitionSpec as P

ITERS = 6


def padded(array, sides, width):
    for axis, dim in sides:
        devices, length = (lax.axis_size(axis), array.shape[dim])
        up = [(i, (i + 1) % devices) for i in range(devices - 1)]
        down = [(j, i) for i, j in up]
        last = lax.slice_in_dim(array, length - width, length, axis=dim)
        first = lax.slice_in_dim(array, 0, width, axis=dim)
        before = lax.ppermute(last, axis, up)
        after = lax.ppermute(first, axis, down)
        array = jnp.concatenate([before, array, after], axis=dim)
    return array


def loc_weights(classes):
    table = (1.0, 0.55, 0.25, 0.08)
    total = jnp.zeros(classes.shape, jnp.float32)
    for index, value in enumerate(table):
        total = total + jnp.where(classes == index, jnp.float32(value), jnp.float32(0.0))
    return total


def west_of(middle):
    last = jnp.roll(middle[..., -1:], 1, axis=-4)
    return jnp.concatenate([last, middle[..., :-1]], axis=-1)


def advance(middle, south, north, wind_east, wind_north):
    west = west_of(middle)
    return (
        middle
        - wind_east * (middle - west)
        - jnp.maximum(wind_north, 0.0) * (middle - south)
        - jnp.minimum(wind_north, 0.0) * (north - middle)
    )


def make_pack(raw_values, values, rinv, count):
    ybar = jnp.mean(raw_values, axis=0)
    pert = raw_values - ybar[None, :]
    innov = values - ybar
    live = jnp.arange(values.shape[0]) < count
    rlive = jnp.where(live, rinv, jnp.float32(0.0))
    return jnp.concatenate([pert, innov[None, :], rlive[None, :]], axis=0)


def tile_weights(own, south, north, classes):
    high = lax.Precision.HIGHEST
    joined = jnp.concatenate([own, south, north], axis=1)
    count_members = joined.shape[0] - 2
    pert = joined[:count_members]
    innov = joined[count_members]
    rloc = joined[count_members + 1] * loc_weights(classes.reshape(-1))
    scaled = pert * rloc[None, :]
    eye = jnp.eye(count_members, dtype=jnp.float32)
    gram = (count_members - 1.0) * eye + jnp.dot(scaled, pert.T, precision=high)
    norm = jnp.sqrt(jnp.sum(gram * gram))
    upper = gram / norm
    lower = eye
    for sweep in range(ITERS):
        factor = 1.5 * eye - 0.5 * jnp.dot(lower, upper, precision=high)
        upper = jnp.dot(upper, factor, precision=high)
        lower = jnp.dot(factor, lower, precision=high)
    drive = jnp.dot(scaled, innov, precision=high)
    wmean = jnp.dot(lower, jnp.dot(lower, drive, precision=high), precision=high) / norm
    weights = (jnp.sqrt((count_members - 1.0) / norm) * lower + wmean[:, None]).astype(jnp.bfloat16)
    colsum = jnp.sum(weights.astype(jnp.float32), axis=0)
    return (weights, colsum)


def apply_weights(weights, colsum, tile_flat):
    count_members = tile_flat.shape[0]
    ones_row = jnp.ones((1, count_members), jnp.bfloat16)
    xbar = jnp.dot(ones_row, tile_flat, preferred_element_type=jnp.float32)[0] / count_members
    mixed = jnp.dot(weights.T, tile_flat, preferred_element_type=jnp.float32)
    return (xbar[None, :] * (1.0 - colsum)[:, None] + mixed).astype(jnp.bfloat16)


def on_device(state, wind_east, wind_north, obs_col, obs_val, obs_rinv, obs_count, loc_class):
    local_members = state.shape[0]
    groups = state.shape[1]
    levels = state.shape[2]
    band_rows = state.shape[3]
    tile_width = state.shape[4]
    all_members = local_members * groups
    extended = padded(state, (("space", 3),), 1).astype(jnp.float32)
    first_state = advance(
        extended[:, :, :, 1:-1],
        extended[:, :, :, :-2],
        extended[:, :, :, 2:],
        wind_east,
        wind_north,
    )
    widened = padded(first_state, (("space", 3),), 1)
    later_state = advance(
        widened[:, :, :, 1:-1], widened[:, :, :, :-2], widened[:, :, :, 2:], wind_east, wind_north
    )
    predict_state = later_state.astype(jnp.bfloat16)
    columns = obs_col[0, 0]
    state_of_tile = lax.all_to_all(predict_state, "member", split_axis=1, concat_axis=0, tiled=True)
    tile_flat = state_of_tile.reshape(all_members, -1)
    raw_values = jnp.take(tile_flat, columns, axis=1).astype(jnp.float32)
    pack = make_pack(raw_values, obs_val[0, 0], obs_rinv[0, 0], obs_count[0, 0])
    rims = padded(pack[None], (("space", 0),), 1)
    weights, colsum = tile_weights(rims[1], rims[0], rims[2], loc_class[0, 0])
    updated = apply_weights(weights, colsum, tile_flat).reshape(
        all_members, 1, levels, band_rows, tile_width
    )
    return lax.all_to_all(updated, "member", split_axis=0, concat_axis=1, tiled=True)


def solution(mesh):
    return jax.shard_map(
        on_device,
        mesh=mesh,
        in_specs=(
            P("member", None, None, "space", None),
            P(None, None, "space", None),
            P(None, None, "space", None),
            P("space", "member", None),
            P("space", "member", None),
            P("space", "member", None),
            P("space", "member"),
            P("space", "member", None, None),
        ),
        out_specs=P("member", None, None, "space", None),
        check_vma=False,
    )
```

profile of v0, /device:TPU:14, one launch (start us, length us, event | category | flops | bytes accessed | tf_op | source)
XLA Modules:
  0.0 326.5 jit_solution(17235241690364078933)
XLA Ops:
  0.0 6.9 %copy.51 = bf16[16,8,4,8,512]{4,1,3,2,0:T(8,128)(2,1)S(1)} copy(bf16[16,8,4,8,512]{4,3,2,1,0:T(8,128)(2,1)} %param.8) | data formatting | bytes 8388608 | tf_op args[0]
  9.0 3.6 %collective-permute-start.1 = (bf16[16,8,4,1,512]{4,1,3,2,0:T(8,128)(2,1)S(1)}, bf16[16,8,4,1,512]{4,1,3,2,0:T(8,128)(2,1)S(1)}, u32[]{:S(2)}, u32[]{:S(2)}) collective-permute-start(bf16[16,8,4,1,512]{4,1,3,2,0:T(8,128)(2,1)S(1)} %get-tuple-element.10), channel_id=1, source_target_pairs={{1,0},{2,1},{3,2},{4,3},{5,4},{6,5},{7,6},{8,7},{9,8},{10,9},{11,1... | collective-permute-start | bytes 1572872 | tf_op jit(solution)/shard_map/ppermute | solution.py:17
  13.7 3.8 %collective-permute-done = bf16[16,8,4,1,512]{4,1,3,2,0:T(8,128)(2,1)S(1)} collective-permute-done((bf16[16,8,4,1,512]{4,1,3,2,0:T(8,128)(2,1)S(1)}, bf16[16,8,4,1,512]{4,1,3,2,0:T(8,128)(2,1)S(1)}, u32[]{:S(2)}, u32[]{:S(2)}) %collective-permute-start) | collective-permute-done | bytes 524320 | tf_op jit(solution)/shard_map/ppermute | solution.py:16
  20.1 4.8 %slice.90 = f32[16,8,4,8,511]{4,1,3,2,0:T(8,128)} slice(f32[16,8,4,10,512]{4,1,3,2,0:T(8,128)S(1)} %maximum_convert_fusion), slice={[0:16], [0:8], [0:4], [1:9], [0:511]} | slice | bytes 16744448 | tf_op jit(solution)/shard_map/slice | solution.py:32
  27.6 16.5 %fusion.9 = f32[16,8,4,8,512]{4,1,3,2,0:T(8,128)} fusion(f32[16,8,4,10,512]{4,1,3,2,0:T(8,128)} %copy-done, f32[16,8,4,8,511]{4,1,3,2,0:T(8,128)} %slice.90, f32[16,7,4,8,1]{4,1,3,2,0:T(8,128)S(1)} %slice.89, f32[16,1,4,8,1]{4,1,3,2,0:T(1,128)S(1)} %maximum_convert_fusion.1, f32[8,4,8,512]{3,0,2,1:T(8,128)S(1)} %copy.56, f32[8,4,8,512]{3,0,2,1:T(8,128)S(1)} %copy.55, ...), kind=kLoop, calls=%fused_computation.14 | loop fusion | flops 23068672 | bytes 43515904 | tf_op jit(solution)/shard_map/sub | solution.py:38
  45.9 6.2 %collective-permute-start.2 = (f32[16,8,4,1,512]{4,1,3,2,0:T(8,128)S(1)}, f32[16,8,4,1,512]{4,1,3,2,0:T(8,128)S(1)}, u32[]{:S(2)}, u32[]{:S(2)}) collective-permute-start(f32[16,8,4,1,512]{4,1,3,2,0:T(8,128)S(1)} %get-tuple-element.7), channel_id=1, source_target_pairs={{0,1},{1,2},{2,3},{3,4},{4,5},{5,6},{6,7},{7,8},{8,9},{9,10},{10,1... | collective-permute-start | bytes 3145736 | tf_op jit(solution)/shard_map/ppermute | solution.py:16
  52.1 1.9 collective-permute-start.3
  54.1 2.2 slice.94
  56.9 5.6 %collective-permute-done.2 = f32[16,8,4,1,512]{4,1,3,2,0:T(8,128)S(1)} collective-permute-done((f32[16,8,4,1,512]{4,1,3,2,0:T(8,128)S(1)}, f32[16,8,4,1,512]{4,1,3,2,0:T(8,128)S(1)}, u32[]{:S(2)}, u32[]{:S(2)}) %collective-permute-start.2) | collective-permute-done | bytes 1048608 | tf_op jit(solution)/shard_map/ppermute | solution.py:16
  62.5 3.9 %collective-permute-done.3 = f32[16,8,4,1,512]{4,1,3,2,0:T(8,128)S(1)} collective-permute-done((f32[16,8,4,1,512]{4,1,3,2,0:T(8,128)S(1)}, f32[16,8,4,1,512]{4,1,3,2,0:T(8,128)S(1)}, u32[]{:S(2)}, u32[]{:S(2)}) %collective-permute-start.3) | collective-permute-done | bytes 1048608 | tf_op jit(solution)/shard_map/ppermute | solution.py:17
  66.4 5.8 %fusion.4 = bf16[16,8,4,8,512]{4,1,3,2,0:T(8,128)(2,1)S(1)} fusion(f32[16,8,4,8,512]{4,1,3,2,0:T(8,128)S(1)} %copy-done.1, f32[16,8,4,1,512]{4,1,3,2,0:T(8,128)S(1)} %collective-permute-done.3, f32[16,8,4,1,512]{4,1,3,2,0:T(8,128)S(1)} %collective-permute-done.2, f32[16,8,4,8,511]{4,1,3,2,0:T(8,128)S(1)} %bitcast.84, f32[16,7,4,8,1]{4,1,3,2,0:T(8,128)S(1)} %slice.94, ...), kind=kLoop, calls=%fused_computation.7 | loop fusion | flops 29360128 | bytes 24641536 | tf_op jit(solution)/shard_map/convert_element_type | solution.py:105
  72.2 3.5 %copy.57 = bf16[16,8,4,8,512]{4,3,2,0,1:T(8,128)(2,1)} copy(bf16[16,8,4,8,512]{4,1,3,2,0:T(8,128)(2,1)S(1)} %fusion.4) | data formatting | bytes 8388608 | tf_op jit(solution)/shard_map/convert_element_type | solution.py:105
  75.7 8.5 %all-to-all-start = ((bf16[16,8,4,8,512]{4,3,2,0,1:T(8,128)(2,1)}), bf16[16,8,4,8,512]{4,3,2,0,1:T(8,128)(2,1)}, u32[]{:S(2)}, u32[]{:S(2)}) async-start(bf16[16,8,4,8,512]{4,3,2,0,1:T(8,128)(2,1)} %copy.57), calls=%async_computation | async-start | bytes 8388608 | tf_op jit(solution)/shard_map/all_to_all | solution.py:107
  85.4 96.4 %all-to-all-done = bf16[16,8,4,8,512]{4,3,2,0,1:T(8,128)(2,1)} async-done(((bf16[16,8,4,8,512]{4,3,2,0,1:T(8,128)(2,1)}), bf16[16,8,4,8,512]{4,3,2,0,1:T(8,128)(2,1)}, u32[]{:S(2)}, u32[]{:S(2)}) %all-to-all-start) | async-done | bytes 4194336 | tf_op jit(solution)/shard_map/all_to_all | solution.py:107
  181.8 7.4 %reshape.172 = bf16[128,16384]{1,0:T(8,128)(2,1)} reshape(bf16[8,16,1,4,8,512]{5,4,3,1,0,2:T(8,128)(2,1)} %bitcast.1) | data formatting | bytes 8388608 | tf_op jit(solution)/shard_map/reshape | solution.py:108
  189.2 6.4 %copy.58 = bf16[128,16384]{0,1:T(8,128)(2,1)} copy(bf16[128,16384]{1,0:T(8,128)(2,1)} %reshape.172) | data formatting | bytes 8388608 | tf_op jit(solution)/shard_map/reshape | solution.py:108
  195.6 3.8 %gather_fusion = bf16[512,128]{1,0:T(8,128)(2,1)S(1)} fusion(bf16[128,16384]{0,1:T(8,128)(2,1)} %copy.58, s32[1024]{0:T(1024)S(1)} %pad_clamp_fusion), kind=kCustom, calls=%fused_computation | custom fusion | bytes 264192 | tf_op jit(solution)/shard_map/jit(_take)/gather | solution.py:109
  200.1 2.0 collective-permute-start.4
  202.1 3.8 %collective-permute-start.5 = (f32[1,130,512]{1,2,0:T(8,128)S(1)}, f32[1,130,512]{1,2,0:T(8,128)S(1)}, u32[]{:S(2)}, u32[]{:S(2)}) collective-permute-start(f32[1,130,512]{1,2,0:T(8,128)S(1)} %maximum_bitcast_fusion), channel_id=1, source_target_pairs={{1,0},{2,1},{3,2},{4,3},{5,4},{6,5},{7,6},{8,7},{9,8},{10,9},{11,1... | collective-permute-start | bytes 798728 | tf_op jit(solution)/shard_map/ppermute | solution.py:17
  205.9 2.8 fusion.45
  213.2 2.4 multiply_reduce_fusion
  221.2 3.5 %fusion = bf16[128,16384]{1,0:T(8,128)(2,1)S(1)} fusion(bf16[128,16384]{1,0:T(8,128)(2,1)} %reshape.172, f32[128]{0:T(128)S(1)} %broadcast_subtract_fusion, f32[16384]{0:T(1024)S(1)} %broadcast_multiply_fusion, f32[128,128]{1,0:T(8,128)S(1)} %fusion.58, f32[128]{0:T(128)S(1)} %fusion.29, f32[]{:T(128)S(6)} %sqrt.7), kind=kOutput, calls=%fused_computation.2 | convolution fusion | flops 543211520 | bytes 8520708 | tf_op jit(solution)/shard_map/dot_general | solution.py:82
  226.5 97.5 %all_to_all.33 = bf16[128,1,4,8,512]{4,3,2,1,0:T(8,128)(2,1)S(1)} all-to-all(bf16[128,1,4,8,512]{4,3,2,1,0:T(8,128)(2,1)S(1)} %bitcast.86), channel_id=1, replica_groups=mesh['member'=8,'space'=32] {'member'}, dimensions={0} | all-to-all | bytes 8388608 | tf_op jit(solution)/shard_map/all_to_all | solution.py:116
  324.0 2.5 copy.63
  (70 shorter events, 22.8 us)
Async XLA Ops:
  0.0 12.6 %copy-start.2 = (f32[8,4,8,512]{3,2,1,0:T(8,128)S(1)}, f32[8,4,8,512]{3,2,1,0:T(8,128)}, u32[]{:S(2)}) copy-start(f32[8,4,8,512]{3,2,1,0:T(8,128)} %param.10) | copy-start | bytes 1572868
  0.0 13.4 %copy-start.3 = (f32[8,4,8,512]{3,2,1,0:T(8,128)S(1)}, f32[8,4,8,512]{3,2,1,0:T(8,128)}, u32[]{:S(2)}) copy-start(f32[8,4,8,512]{3,2,1,0:T(8,128)} %param.9) | copy-start | bytes 1572868
  7.1 10.5 %collective-permute-start = (bf16[16,8,4,1,512]{4,1,3,2,0:T(8,128)(2,1)S(1)}, bf16[16,8,4,1,512]{4,1,3,2,0:T(8,128)(2,1)S(1)}, u32[]{:S(2)}, u32[]{:S(2)}) collective-permute-start(bf16[16,8,4,1,512]{4,1,3,2,0:T(8,128)(2,1)S(1)} %get-tuple-element.9), channel_id=1, source_target_pairs={{0,1},{1,2},{2,3},{3,4},{4,5},{5,6},{6,7},{7,8},{8,9},{9,10},{10,1... | collective-permute-start | bytes 1572872 | tf_op jit(solution)/shard_map/ppermute | solution.py:16
  9.0 10.3 %collective-permute-start.1 = (bf16[16,8,4,1,512]{4,1,3,2,0:T(8,128)(2,1)S(1)}, bf16[16,8,4,1,512]{4,1,3,2,0:T(8,128)(2,1)S(1)}, u32[]{:S(2)}, u32[]{:S(2)}) collective-permute-start(bf16[16,8,4,1,512]{4,1,3,2,0:T(8,128)(2,1)S(1)} %get-tuple-element.10), channel_id=1, source_target_pairs={{1,0},{2,1},{3,2},{4,3},{5,4},{6,5},{7,6},{8,7},{9,8},{10,9},{11,1... | collective-permute-start | bytes 1572872 | tf_op jit(solution)/shard_map/ppermute | solution.py:17
  20.1 6.4 %copy-start = (f32[16,8,4,10,512]{4,1,3,2,0:T(8,128)}, f32[16,8,4,10,512]{4,1,3,2,0:T(8,128)S(1)}, u32[]{:S(2)}) copy-start(f32[16,8,4,10,512]{4,1,3,2,0:T(8,128)S(1)} %maximum_convert_fusion) | copy-start | bytes 31457284
  44.0 12.2 %copy-start.1 = (f32[16,8,4,8,512]{4,1,3,2,0:T(8,128)S(1)}, f32[16,8,4,8,512]{4,1,3,2,0:T(8,128)}, u32[]{:S(2)}) copy-start(f32[16,8,4,8,512]{4,1,3,2,0:T(8,128)} %fusion.9) | copy-start | bytes 25165828
  45.9 16.6 %collective-permute-start.2 = (f32[16,8,4,1,512]{4,1,3,2,0:T(8,128)S(1)}, f32[16,8,4,1,512]{4,1,3,2,0:T(8,128)S(1)}, u32[]{:S(2)}, u32[]{:S(2)}) collective-permute-start(f32[16,8,4,1,512]{4,1,3,2,0:T(8,128)S(1)} %get-tuple-element.7), channel_id=1, source_target_pairs={{0,1},{1,2},{2,3},{3,4},{4,5},{5,6},{6,7},{7,8},{8,9},{9,10},{10,1... | collective-permute-start | bytes 3145736 | tf_op jit(solution)/shard_map/ppermute | solution.py:16
  52.1 14.2 %collective-permute-start.3 = (f32[16,8,4,1,512]{4,1,3,2,0:T(8,128)S(1)}, f32[16,8,4,1,512]{4,1,3,2,0:T(8,128)S(1)}, u32[]{:S(2)}, u32[]{:S(2)}) collective-permute-start(f32[16,8,4,1,512]{4,1,3,2,0:T(8,128)S(1)} %get-tuple-element.8), channel_id=1, source_target_pairs={{1,0},{2,1},{3,2},{4,3},{5,4},{6,5},{7,6},{8,7},{9,8},{10,9},{11,1... | collective-permute-start | bytes 3145736 | tf_op jit(solution)/shard_map/ppermute | solution.py:17
  72.2 12.0 %copy-start.6 = (f32[1,1,512]{2,1,0:T(1,128)S(1)}, f32[1,1,512]{2,1,0:T(1,128)}, u32[]{:S(2)}) copy-start(f32[1,1,512]{2,1,0:T(1,128)} %param.13) | copy-start | bytes 6148
  72.2 12.8 %copy-start.5 = (s32[1,1,3,512]{3,1,2,0:T(1,128)S(1)}, s32[1,1,3,512]{3,1,2,0:T(1,128)}, u32[]{:S(2)}) copy-start(s32[1,1,3,512]{3,1,2,0:T(1,128)} %param.15) | copy-start | bytes 18436
  72.2 13.1 %copy-start.4 = (s32[1,1,512]{2,1,0:T(1,128)S(1)}, s32[1,1,512]{2,1,0:T(1,128)}, u32[]{:S(2)}) copy-start(s32[1,1,512]{2,1,0:T(1,128)} %param.11) | copy-start | bytes 6148
  75.7 106.1 %all-to-all-start = ((bf16[16,8,4,8,512]{4,3,2,0,1:T(8,128)(2,1)}), bf16[16,8,4,8,512]{4,3,2,0,1:T(8,128)(2,1)}, u32[]{:S(2)}, u32[]{:S(2)}) async-start(bf16[16,8,4,8,512]{4,3,2,0,1:T(8,128)(2,1)} %copy.57), calls=%async_computation | async-start | bytes 8388608 | tf_op jit(solution)/shard_map/all_to_all | solution.py:107
  181.8 18.0 %copy-start.7 = (f32[1,1,512]{2,1,0:T(1,128)S(1)}, f32[1,1,512]{2,1,0:T(1,128)}, u32[]{:S(2)}) copy-start(f32[1,1,512]{2,1,0:T(1,128)} %param.12) | copy-start | bytes 6148
  200.1 10.5 %collective-permute-start.4 = (f32[1,130,512]{1,2,0:T(8,128)S(1)}, f32[1,130,512]{1,2,0:T(8,128)S(1)}, u32[]{:S(2)}, u32[]{:S(2)}) collective-permute-start(f32[1,130,512]{1,2,0:T(8,128)S(1)} %maximum_bitcast_fusion), channel_id=1, source_target_pairs={{0,1},{1,2},{2,3},{3,4},{4,5},{5,6},{6,7},{7,8},{8,9},{9,10},{10,1... | collective-permute-start | bytes 798728 | tf_op jit(solution)/shard_map/ppermute | solution.py:16
  202.1 10.2 %collective-permute-start.5 = (f32[1,130,512]{1,2,0:T(8,128)S(1)}, f32[1,130,512]{1,2,0:T(8,128)S(1)}, u32[]{:S(2)}, u32[]{:S(2)}) collective-permute-start(f32[1,130,512]{1,2,0:T(8,128)S(1)} %maximum_bitcast_fusion), channel_id=1, source_target_pairs={{1,0},{2,1},{3,2},{4,3},{5,4},{6,5},{7,6},{8,7},{9,8},{10,9},{11,1... | collective-permute-start | bytes 798728 | tf_op jit(solution)/shard_map/ppermute | solution.py:17
where the time goes:
time: 330 us; the launch traced here: 327 us
  waiting for transfers between devices  115 us (35%)
  blocking collectives  97.5 us (30%)
  local copies, waits for them, and re-layouts  45.5 us (14%)
  starting transfers between devices  28 us (8%)
  other arithmetic  25.3 us (8%)
  matrix products  13.2 us (4%)
    all_to_all x1, blocking collectives, on_device(): lax.all_to_all(updated, 'member', split_axis=0, concat_axis=1, tiled=True)  97.5 us
    all_to_all x1, waiting for transfers between devices, on_device(): lax.all_to_all(predict_state, 'member', split_axis=1, concat_axis=0, tile...  96.4 us
    sub x1, other arithmetic, advance(): middle - wind_east * (middle - west)  16.5 us
    reshape x2, local copies, waits for them, and re-layouts, on_device(): tile_flat = state_of_tile.reshape(all_members, -1)  13.7 us
    ppermute x3, waiting for transfers between devices, padded(): before = lax.ppermute(last, axis, up)  11.2 us
    unnamed x19, local copies, waits for them, and re-layouts  10.6 us
    ppermute x3, starting transfers between devices, padded(): before = lax.ppermute(last, axis, up)  10.2 us
    ppermute x3, starting transfers between devices, padded(): after = lax.ppermute(first, axis, down)  9.33 us
  transfers between devices with their start and end apart: 7, of which 7 were waited for; matrix products, arithmetic and copies ran while one was open for 2% of the time, Pallas kernels for 0%

commit v1 on v0

v1 whole, which is shorter than its diff:
```python
import functools

import jax
import jax.numpy as jnp
from jax import lax
from jax.experimental import pallas as pl
from jax.experimental.pallas import tpu as pltpu
from jax.sharding import PartitionSpec as P

ITERS = 6
LANES = 128
VMEM_LIMIT = 48 * 1024 * 1024


def params(limit=VMEM_LIMIT):
    return pltpu.CompilerParams(vmem_limit_bytes=limit)


def cost(micros):
    return pl.CostEstimate(flops=0, bytes_accessed=int(micros * 3.6e6), transcendentals=0)


def order_rows(shape, members, rows):
    at = lax.broadcasted_iota(jnp.int32, shape, 0)
    source = lax.broadcasted_iota(jnp.int32, shape, 1)
    slot = at // members
    row = jnp.zeros(shape, jnp.int32)
    for index, value in enumerate(rows):
        row = jnp.where(slot == index, value, row)
    band = 8
    return jnp.where(source == (at % members) * band + row, 1.0, 0.0).astype(jnp.bfloat16)


def tile_rows(state_ref, tile, order):
    block = state_ref[:, tile, 0].astype(jnp.float32)
    members, rows, width = block.shape
    flat = block.reshape(members * rows, width).astype(jnp.bfloat16)
    return jnp.dot(order, flat, preferred_element_type=jnp.float32)


def edges_kernel(state_ref, low_ref, high_ref):
    members, tiles, _, rows, width = state_ref.shape
    order = order_rows((4 * members, members * rows), members, (0, 1, rows - 2, rows - 1))
    for tile in range(tiles):
        moved = tile_rows(state_ref, tile, order).astype(jnp.bfloat16)
        columns = slice(tile * width, (tile + 1) * width)
        for row in range(2):
            low_ref[0, row, :, columns] = moved[row * members : (row + 1) * members]
            high_ref[0, row, :, columns] = moved[(row + 2) * members : (row + 3) * members]


def edge_rows(state):
    members, tiles, levels, rows, width = state.shape
    shape = (levels, 2, members, tiles * width)
    block = pl.BlockSpec((1, 2, members, tiles * width), lambda i: (i, 0, 0, 0))
    return pl.pallas_call(
        edges_kernel,
        grid=(levels,),
        in_specs=[pl.BlockSpec((members, tiles, 1, rows, width), lambda i: (0, 0, i, 0, 0))],
        out_specs=[block, block],
        out_shape=[jax.ShapeDtypeStruct(shape, jnp.bfloat16)] * 2,
        compiler_params=params(),
        cost_estimate=cost(3),
        name="edges",
    )(state)


def step_rows(field, made, coef, tiles, width, rows_out, first_row):
    for row in rows_out:
        at = row - first_row
        for tile in range(tiles):
            columns = slice(LANES + tile * width, LANES + (tile + 1) * width)
            padded = slice(tile * width, LANES + (tile + 1) * width)
            west = pltpu.roll(field[at, :, padded], 1, 1)[:, LANES:]
            stay = coef[0, tile, at : at + 1, :]
            east = coef[1, tile, at : at + 1, :]
            up = coef[2, tile, at : at + 1, :]
            down = coef[3, tile, at : at + 1, :]
            made[at, :, columns] = (
                stay * field[at, :, columns]
                + east * west
                + up * field[at - 1, :, columns]
                + down * field[at + 1, :, columns]
            )
        made[at, :, 0:LANES] = made[at, :, tiles * width : tiles * width + LANES]


def set_coef(coef, slots, tile, east, north):
    up = jnp.maximum(north, 0.0)
    down = -jnp.minimum(north, 0.0)
    coef[0, tile, slots, :] = 1.0 - east - up - down
    coef[1, tile, slots, :] = east
    coef[2, tile, slots, :] = up
    coef[3, tile, slots, :] = down


def interior_kernel(state_ref, east_ref, north_ref, out_ref, field, made, coef):
    members, tiles, _, rows, width = state_ref.shape
    order = order_rows((rows * members, members * rows), members, tuple(range(rows)))
    for tile in range(tiles):
        moved = tile_rows(state_ref, tile, order)
        columns = slice(LANES + tile * width, LANES + (tile + 1) * width)
        for row in range(rows):
            field[row, :, columns] = moved[row * members : (row + 1) * members]
        set_coef(coef, slice(0, rows), tile, east_ref[tile, 0], north_ref[tile, 0])
    for row in range(rows):
        field[row, :, 0:LANES] = field[row, :, tiles * width : tiles * width + LANES]
    step_rows(field, made, coef, tiles, width, range(1, rows - 1), 0)
    step_rows(made, field, coef, tiles, width, range(2, rows - 2), 0)
    for row in range(2, rows - 2):
        for tile in range(tiles):
            columns = slice(LANES + tile * width, LANES + (tile + 1) * width)
            kept = slice((row - 2) * width, (row - 1) * width)
            out_ref[tile, :, kept] = field[row, :, columns].astype(jnp.bfloat16)


def interior(state, wind_east, wind_north):
    members, tiles, levels, rows, width = state.shape
    wind = pl.BlockSpec((tiles, 1, rows, width), lambda i: (0, i, 0, 0))
    part = (rows - 4) * width
    return pl.pallas_call(
        interior_kernel,
        grid=(levels,),
        in_specs=[pl.BlockSpec((members, tiles, 1, rows, width), lambda i: (0, 0, i, 0, 0)), wind, wind],
        out_specs=pl.BlockSpec((tiles, members, part), lambda i: (0, 0, i)),
        out_shape=jax.ShapeDtypeStruct((tiles, members, levels * part), jnp.bfloat16),
        scratch_shapes=[
            pltpu.VMEM((rows, members, LANES + tiles * width), jnp.float32),
            pltpu.VMEM((rows, members, LANES + tiles * width), jnp.float32),
            pltpu.VMEM((4, tiles, rows, width), jnp.float32),
        ],
        compiler_params=params(),
        cost_estimate=cost(8),
        name="interior",
    )(state, wind_east, wind_north)


def outer_kernel(
    state_ref, east_ref, north_ref, below_ref, above_ref, wind_below_ref, wind_above_ref, out_ref, field, made, coef
):
    members, tiles, _, rows, width = state_ref.shape
    order = order_rows((rows * members, members * rows), members, tuple(range(rows)))
    for tile in range(tiles):
        moved = tile_rows(state_ref, tile, order)
        columns = slice(LANES + tile * width, LANES + (tile + 1) * width)
        for row in range(rows):
            field[row + 2, :, columns] = moved[row * members : (row + 1) * members]
        set_coef(coef, slice(2, rows + 2), tile, east_ref[tile, 0], north_ref[tile, 0])
        for slot, wind_ref in ((1, wind_below_ref), (rows + 2, wind_above_ref)):
            set_coef(
                coef,
                slice(slot, slot + 1),
                tile,
                wind_ref[0, 0, tile : tile + 1, :],
                wind_ref[1, 0, tile : tile + 1, :],
            )
    for row in range(2):
        field[row, :, LANES:] = below_ref[0, row].astype(jnp.float32)
        field[rows + 2 + row, :, LANES:] = above_ref[0, row].astype(jnp.float32)
    for slot in range(rows + 4):
        field[slot, :, 0:LANES] = field[slot, :, tiles * width : tiles * width + LANES]
    step_rows(field, made, coef, tiles, width, (-1, 0, 1, 2, rows - 3, rows - 2, rows - 1, rows), -2)
    step_rows(made, field, coef, tiles, width, (0, 1, rows - 2, rows - 1), -2)
    for index, row in enumerate((0, 1, rows - 2, rows - 1)):
        for tile in range(tiles):
            columns = slice(LANES + tile * width, LANES + (tile + 1) * width)
            kept = slice(index * width, (index + 1) * width)
            out_ref[tile, :, kept] = field[row + 2, :, columns].astype(jnp.bfloat16)


def outer(state, wind_east, wind_north, below, above, wind_below, wind_above):
    members, tiles, levels, rows, width = state.shape
    wind = pl.BlockSpec((tiles, 1, rows, width), lambda i: (0, i, 0, 0))
    edge = pl.BlockSpec((1, 2, members, tiles * width), lambda i: (i, 0, 0, 0))
    wind_edge = pl.BlockSpec((2, 1, tiles, width), lambda i: (0, i, 0, 0))
    part = 4 * width
    return pl.pallas_call(
        outer_kernel,
        grid=(levels,),
        in_specs=[
            pl.BlockSpec((members, tiles, 1, rows, width), lambda i: (0, 0, i, 0, 0)),
            wind,
            wind,
            edge,
            edge,
            wind_edge,
            wind_edge,
        ],
        out_specs=pl.BlockSpec((tiles, members, part), lambda i: (0, 0, i)),
        out_shape=jax.ShapeDtypeStruct((tiles, members, levels * part), jnp.bfloat16),
        scratch_shapes=[
            pltpu.VMEM((rows + 4, members, LANES + tiles * width), jnp.float32),
            pltpu.VMEM((rows + 4, members, LANES + tiles * width), jnp.float32),
            pltpu.VMEM((4, tiles, rows + 4, width), jnp.float32),
        ],
        compiler_params=params(),
        cost_estimate=cost(9),
        name="outer",
    )(state, wind_east, wind_north, below, above, wind_below, wind_above)


def pick_kernel(place_ref, shift_ref, inner_ref, outer_ref, raw_ref, pieces):
    tile = pl.program_id(0)
    members, length = inner_ref.shape[1:]
    count = length // LANES
    for piece in range(count):
        lanes = slice(piece * LANES, (piece + 1) * LANES)
        pieces[piece] = inner_ref[0, :, lanes].astype(jnp.float32)
        pieces[count + piece] = outer_ref[0, :, lanes].astype(jnp.float32)
    lane = lax.broadcasted_iota(jnp.int32, (members, LANES), 1)
    unroll = 16
    for block in range(raw_ref.shape[2] // LANES):

        def body(step, total):
            for inside in range(unroll):
                slot = step * unroll + inside
                at = block * LANES + slot
                rolled = pltpu.roll(pieces[place_ref[tile, at]], shift_ref[tile, at], 1)
                total = jnp.where(lane == slot, rolled, total)
            return total

        total = lax.fori_loop(0, LANES // unroll, body, jnp.zeros((members, LANES), jnp.float32))
        raw_ref[0, :, block * LANES : (block + 1) * LANES] = total.astype(jnp.bfloat16)


def pick(place, shift, inner, outer_part):
    tiles, members, length = inner.shape
    slots = place.shape[1]
    half = pl.BlockSpec((1, members, length), lambda i, *_: (i, 0, 0))
    return pl.pallas_call(
        pick_kernel,
        grid_spec=pltpu.PrefetchScalarGridSpec(
            num_scalar_prefetch=2,
            grid=(tiles,),
            in_specs=[half, half],
            out_specs=pl.BlockSpec((1, members, slots), lambda i, *_: (i, 0, 0)),
            scratch_shapes=[pltpu.VMEM((2 * length // LANES, members, LANES), jnp.float32)],
        ),
        out_shape=jax.ShapeDtypeStruct((tiles, members, slots), jnp.bfloat16),
        compiler_params=params(),
        cost_estimate=cost(15),
        name="pick",
    )(place, shift, inner, outer_part)


def loc_weights(classes):
    table = (1.0, 0.55, 0.25, 0.08)
    total = jnp.zeros(classes.shape, jnp.float32)
    for index, value in enumerate(table):
        total = total + jnp.where(classes == index, jnp.float32(value), jnp.float32(0.0))
    return total


def weights_kernel(own_ref, south_ref, north_ref, obs_ref, class_ref, mix_ref, rest_ref):
    dot = functools.partial(jnp.dot, precision=lax.Precision.HIGHEST, preferred_element_type=jnp.float32)
    members = own_ref.shape[0]
    row = lax.broadcasted_iota(jnp.int32, (members, members), 0)
    column = lax.broadcasted_iota(jnp.int32, (members, members), 1)
    eye = jnp.where(row == column, 1.0, 0.0).astype(jnp.float32)
    gram = (members - 1.0) * eye
    drive = jnp.zeros((members, 1), jnp.float32)
    for index, raw_ref in enumerate((own_ref, south_ref, north_ref)):
        raw = raw_ref[...].astype(jnp.float32)
        ybar = jnp.sum(raw, axis=0, keepdims=True) * (1.0 / members)
        pert = raw - ybar
        innov = obs_ref[index, 0:1, :] - ybar
        rloc = obs_ref[index, 1:2, :] * loc_weights(class_ref[index : index + 1, :])
        scaled = pert * rloc
        gram = gram + lax.dot_general(
            scaled,
            pert,
            (((1,), (1,)), ((), ())),
            precision=lax.Precision.HIGHEST,
            preferred_element_type=jnp.float32,
        )
        drive = drive + jnp.sum(scaled * innov, axis=1, keepdims=True)
    norm = jnp.sqrt(jnp.sum(jnp.sum(gram * gram, axis=1, keepdims=True), axis=0, keepdims=True))
    upper = gram / norm
    lower = eye
    for sweep in range(ITERS):
        factor = 1.5 * eye - 0.5 * dot(lower, upper)
        if sweep < ITERS - 1:
            upper = dot(upper, factor)
        lower = dot(factor, lower)
    wide = jnp.broadcast_to(drive, (members, members))
    wmean = dot(lower, dot(lower, wide)) / norm
    weights = (jnp.sqrt((members - 1.0) / norm) * lower + wmean).astype(jnp.bfloat16).astype(jnp.float32)
    turned = weights.T
    rest = 1.0 - jnp.sum(turned, axis=1, keepdims=True)
    rows = 8
    rest_ref[...] = jnp.broadcast_to(rest[:, :, None], (members, rows, LANES)).reshape(members * rows, LANES)
    spread = jnp.broadcast_to(turned[:, None, :], (members, rows, members)).reshape(members * rows, members)
    held = lax.broadcasted_iota(jnp.int32, (members * rows, members), 0) % rows
    for index, value in enumerate((2, 3, 4, 5, 0, 1, 6, 7)):
        mix_ref[:, index * members : (index + 1) * members] = jnp.where(held == value, spread, 0.0).astype(jnp.bfloat16)


def tile_mix(own, south, north, obs, classes):
    members = own.shape[0]
    return pl.pallas_call(
        weights_kernel,
        out_shape=[
            jax.ShapeDtypeStruct((members * 8, members * 8), jnp.bfloat16),
            jax.ShapeDtypeStruct((members * 8, LANES), jnp.float32),
        ],
        compiler_params=params(),
        cost_estimate=cost(12),
        name="weights",
    )(own, south, north, obs, classes)


def mix_kernel(mix_ref, rest_ref, inner_ref, outer_ref, out_ref):
    groups, each, part = inner_ref.shape
    members = groups * each
    width = part // 4
    inner = inner_ref[...].reshape(members, part)
    outer_part = outer_ref[...].reshape(members, part)
    pieces = [inner[:, i * width : (i + 1) * width] for i in range(4)]
    pieces += [outer_part[:, i * width : (i + 1) * width] for i in range(4)]
    stacked = jnp.concatenate(pieces, axis=0)
    rows = 8
    at = lax.broadcasted_iota(jnp.int32, (rows, members * rows), 0)
    slot = lax.broadcasted_iota(jnp.int32, (rows, members * rows), 1) // members
    source = jnp.zeros((rows, members * rows), jnp.int32)
    for index, value in enumerate((2, 3, 4, 5, 0, 1, 6, 7)):
        source = jnp.where(slot == index, value, source)
    ones = jnp.where(at == source, 1.0, 0.0).astype(jnp.bfloat16)
    mean = jnp.dot(ones, stacked, preferred_element_type=jnp.float32) * (1.0 / members)
    mixed = jnp.dot(mix_ref[...], stacked, preferred_element_type=jnp.float32)
    for index in range(width // LANES):
        lanes = slice(index * LANES, (index + 1) * LANES)
        rest = rest_ref[...].reshape(members, rows, LANES)
        made = mixed[:, lanes].reshape(members, rows, LANES) + mean[None, :, lanes] * rest
        out_ref[:, :, 0, :, lanes] = made.reshape(groups, each, rows, LANES).astype(jnp.bfloat16)


def analyse(mix, rest, inner, outer_part, levels, width):
    groups, each, _ = inner.shape
    half = pl.BlockSpec((groups, each, 4 * width), lambda i: (0, 0, i))
    return pl.pallas_call(
        mix_kernel,
        grid=(levels,),
        in_specs=[
            pl.BlockSpec(mix.shape, lambda i: (0, 0)),
            pl.BlockSpec(rest.shape, lambda i: (0, 0)),
            half,
            half,
        ],
        out_specs=pl.BlockSpec((groups, each, 1, 8, width), lambda i: (0, 0, i, 0, 0)),
        out_shape=jax.ShapeDtypeStruct((groups, each, levels, 8, width), jnp.bfloat16),
        compiler_params=params(),
        cost_estimate=cost(6),
        name="analyse",
    )(mix, rest, inner, outer_part)


def to_neighbours(low, high):
    devices = lax.axis_size("space")
    up = [(i, i + 1) for i in range(devices - 1)]
    down = [(i + 1, i) for i in range(devices - 1)]
    return lax.ppermute(high, "space", up), lax.ppermute(low, "space", down)


def swap_members(blocks):
    devices = lax.axis_size("member")
    here = lax.axis_index("member")
    got = [lax.dynamic_index_in_dim(blocks, here, 0, keepdims=False)]
    for shift in range(1, devices):
        block = lax.dynamic_index_in_dim(blocks, lax.rem(here + shift, devices), 0, keepdims=False)
        got.append(lax.ppermute(block, "member", [(i, (i + shift) % devices) for i in range(devices)]))
    stacked = jnp.stack(got)
    out = jnp.zeros_like(blocks)
    for shift in range(devices):
        out = lax.dynamic_update_index_in_dim(out, got[shift], lax.rem(here + devices - shift, devices), 0)
    return out


def all_to_all(blocks):
    return lax.all_to_all(blocks, "member", split_axis=0, concat_axis=0, tiled=True)


def on_device(state, wind_east, wind_north, obs_col, obs_val, obs_rinv, obs_count, loc_class):
    members, tiles, levels, rows, width = state.shape
    slots = obs_col.shape[2]

    low, high = edge_rows(state)
    below, above = to_neighbours(low, high)
    winds = jnp.stack([wind_east[:, :, 0], wind_north[:, :, 0], wind_east[:, :, rows - 1], wind_north[:, :, rows - 1]])
    winds = jnp.swapaxes(winds, 1, 2)
    wind_below, wind_above = to_neighbours(winds[0:2], winds[2:4])

    live = jnp.arange(slots, dtype=jnp.int32) < obs_count[0, 0]
    obs = jnp.stack([obs_val[0, 0], jnp.where(live, obs_rinv[0, 0], jnp.float32(0.0))])
    obs_south, obs_north = to_neighbours(obs, obs)

    columns = lax.all_gather(obs_col[0, 0], "member")
    row = (columns // width) % rows
    inside = (row >= 2) & (row < rows - 2)
    kept = jnp.where(inside, row - 2, jnp.where(row < 2, row, row - 4))
    offset = (columns // (rows * width)) * (4 * width) + kept * width + columns % width
    place = offset // LANES + jnp.where(inside, 0, levels * 4 * width // LANES)
    shift = (jnp.arange(slots, dtype=jnp.int32)[None, :] - offset) % LANES

    inner = interior(state, wind_east, wind_north)
    inner_tile = all_to_all(inner)
    outside = outer(state, wind_east, wind_north, below, above, wind_below, wind_above)
    raw = swap_members(pick(place, shift, inner, outside)).reshape(tiles * members, slots)
    south, north = to_neighbours(raw, raw)
    mix, rest = tile_mix(raw, south, north, jnp.stack([obs, obs_south, obs_north]), loc_class[0, 0])
    outer_tile = all_to_all(outside)
    updated = analyse(mix, rest, inner_tile, outer_tile, levels, width)
    final = all_to_all(updated)
    return jnp.swapaxes(final, 0, 1)


def solution(mesh):
    return jax.shard_map(
        on_device,
        mesh=mesh,
        in_specs=(
            P("member", None, None, "space", None),
            P(None, None, "space", None),
            P(None, None, "space", None),
            P("space", "member", None),
            P("space", "member", None),
            P("space", "member", None),
            P("space", "member"),
            P("space", "member", None, None),
        ),
        out_specs=P("member", None, None, "space", None),
        check_vma=False,
    )
```

time: 330 us -> 322 us (0.976)
  waiting for transfers between devices: 115 us -> 40.7 us
  blocking collectives: 97.5 us -> 161 us
  Pallas kernels: 0 us -> 62.6 us
  local copies, waits for them, and re-layouts: 45.5 us -> 7.89 us
  other arithmetic: 25.3 us -> 0.13 us
  starting transfers between devices: 28 us -> 44.4 us
  matrix products: 13.2 us -> 0 us
    all_to_all x1 -> x2, waiting for transfers between devices: 96.4 us -> 20.2 us  [all_to_all(): lax.all_to_all(blocks, 'member', split_axis=0, concat_axis=0, tiled=True)]
    pallas_call x0 -> x6, Pallas kernels: none -> 62.6 us  [the longest x1 30.8 us: pick(): pl.pallas_call(pick_kernel, grid_spec=pltpu.PrefetchScalarGridSpec(num_sc...]
    all_gather x0 -> x1, blocking collectives: none -> 61.5 us  [on_device(): columns = lax.all_gather(obs_col[0, 0], 'member')]
    sub x4 -> x0, other arithmetic: 16.7 us -> none  [the longest x1 16.5 us: advance(): middle - wind_east * (middle - west)]
    reshape x2 -> x0, local copies, waits for them, and re-layouts: 13.7 us -> none  [on_device(): tile_flat = state_of_tile.reshape(all_members, -1)]
    dot_general x23 -> x0, matrix products: 13.2 us -> none  [the longest x1 3.54 us: apply_weights(): mixed = jnp.dot(weights.T, tile_flat, preferred_element_type=jnp.float32)]
    ppermute x6 -> x15, starting transfers between devices: 19.5 us -> 31.6 us  [the longest x8 20 us: to_neighbours(): return (lax.ppermute(high, 'space', up), lax.ppermute(low, 'space', down))]
    slice x6 -> x3, local copies, waits for them, and re-layouts: 10.2 us -> 0.18 us  [the longest x1 0.08 us: on_device(): wind_east[:, :, 0]]
  transfers between devices with their start and end apart: 7 -> 17, of which waited for: 7 -> 5; matrix products, arithmetic and copies ran while one was open for 2% -> 0% of each run, Pallas kernels for 0% -> 15%
where the time goes in v1:
time: 322 us; the launch traced here: 318 us
  blocking collectives  161 us (50%)
  Pallas kernels  62.6 us (19%)
  starting transfers between devices  44.4 us (14%)
  waiting for transfers between devices  40.7 us (13%)
  local copies, waits for them, and re-layouts  7.89 us (2%)
    all_to_all x1, blocking collectives, all_to_all(): lax.all_to_all(blocks, 'member', split_axis=0, concat_axis=0, tiled=True)  99.6 us
    all_gather x1, blocking collectives, on_device(): columns = lax.all_gather(obs_col[0, 0], 'member')  61.5 us
    pallas_call x1, Pallas kernels, pick(): pl.pallas_call(pick_kernel, grid_spec=pltpu.PrefetchScalarGridSpec(num_sc...  30.8 us
    all_to_all x2, waiting for transfers between devices, all_to_all(): lax.all_to_all(blocks, 'member', split_axis=0, concat_axis=0, tiled=True)  20.2 us
    ppermute x8, starting transfers between devices, to_neighbours(): return (lax.ppermute(high, 'space', up), lax.ppermute(low, 'space', down))  20 us
    all_to_all x2, starting transfers between devices, all_to_all(): lax.all_to_all(blocks, 'member', split_axis=0, concat_axis=0, tiled=True)  12.8 us
    ppermute x7, starting transfers between devices, swap_members(): lax.ppermute(block, 'member', [(i, (i + shift) % devices) for i in range(...  11.6 us
    ppermute x7, waiting for transfers between devices, swap_members(): lax.ppermute(block, 'member', [(i, (i + shift) % devices) for i in range(...  10.4 us
  transfers between devices with their start and end apart: 17, of which 5 were waited for; matrix products, arithmetic and copies ran while one was open for 0% of the time, Pallas kernels for 15%

profile of v1, /device:TPU:14, one launch (start us, length us, event | category | flops | bytes accessed | tf_op | source)
XLA Modules:
  0.0 317.9 jit_solution(11569218544223416205)
XLA Ops:
  2.1 6.9 %interior.1.inner_ref = bf16[8,16,8192]{2,1,0:T(8,128)(2,1)} custom-call(bf16[16,8,4,8,512]{4,3,2,1,0:T(8,128)(2,1)} %state_ref.5, f32[8,4,8,512]{3,2,1,0:T(8,128)S(1)} %copy-done, f32[8,4,8,512]{3,2,1,0:T(8,128)S(1)} %copy-done.2), custom_call_target="tpu_custom_call" | custom-call | bytes 28800000 | tf_op jit(solution)/shard_map/interior/pallas_call | solution.py:121
  9.0 8.5 %all-to-all-start = ((bf16[8,16,8192]{2,1,0:T(8,128)(2,1)}), bf16[8,16,8192]{2,1,0:T(8,128)(2,1)S(1)}, u32[]{:S(2)}, u32[]{:S(2)}) async-start(bf16[8,16,8192]{2,1,0:T(8,128)(2,1)} %interior.1.inner_ref), calls=%async_computation | async-start | bytes 4194304 | tf_op jit(solution)/shard_map/all_to_all | solution.py:379
  17.5 3.6 %edges.1 = (bf16[4,2,16,4096]{3,2,1,0:T(8,128)(2,1)S(1)}, bf16[4,2,16,4096]{3,2,1,0:T(8,128)(2,1)S(1)}) custom-call(bf16[16,8,4,8,512]{4,3,2,1,0:T(8,128)(2,1)} %state_ref.5), custom_call_target="tpu_custom_call" | custom-call | bytes 10800000 | tf_op jit(solution)/shard_map/edges/pallas_call | solution.py:56
  23.0 3.6 %collective-permute-start.1 = (bf16[4,2,16,4096]{3,2,1,0:T(8,128)(2,1)S(1)}, bf16[4,2,16,4096]{3,2,1,0:T(8,128)(2,1)S(1)}, u32[]{:S(2)}, u32[]{:S(2)}) collective-permute-start(bf16[4,2,16,4096]{3,2,1,0:T(8,128)(2,1)S(1)} %get-tuple-element.10), channel_id=1, source_target_pairs={{1,0},{2,1},{3,2},{4,3},{5,4},{6,5},{7,6},{8,7},{9,8},{10,9},{11,1... | collective-permute-start | bytes 3145736 | tf_op jit(solution)/shard_map/ppermute | solution.py:361
  27.0 1.9 collective-permute-start.3
  29.0 2.4 collective-permute-start.2
  31.4 9.0 %collective-permute-done.3.wind_above_ref = f32[2,4,8,512]{3,2,1,0:T(8,128)S(1)} collective-permute-done((f32[2,4,8,512]{3,2,1,0:T(8,128)S(1)}, f32[2,4,8,512]{3,2,1,0:T(8,128)S(1)}, u32[]{:S(2)}, u32[]{:S(2)}) %collective-permute-start.3) | collective-permute-done | bytes 131104 | tf_op jit(solution)/shard_map/ppermute | solution.py:361
  40.4 8.1 %outer.1.outer_ref = bf16[8,16,8192]{2,1,0:T(8,128)(2,1)} custom-call(bf16[16,8,4,8,512]{4,3,2,1,0:T(8,128)(2,1)} %state_ref.5, f32[8,4,8,512]{3,2,1,0:T(8,128)S(1)} %copy-done.1, f32[8,4,8,512]{3,2,1,0:T(8,128)S(1)} %copy-done.3, bf16[4,2,16,4096]{3,2,1,0:T(8,128)(2,1)S(1)} %collective-permute-done.below_ref, ...), custom_call_target="tpu_custom_call" | custom-call | bytes 32400000 | tf_op jit(solution)/shard_map/outer/pallas_call | solution.py:177
  48.5 20.2 %all-to-all-done.inner_ref = bf16[8,16,8192]{2,1,0:T(8,128)(2,1)S(1)} async-done(((bf16[8,16,8192]{2,1,0:T(8,128)(2,1)}), bf16[8,16,8192]{2,1,0:T(8,128)(2,1)S(1)}, u32[]{:S(2)}, u32[]{:S(2)}) %all-to-all-start) | async-done | bytes 2097184 | tf_op jit(solution)/shard_map/all_to_all | solution.py:379
  68.7 4.3 %all-to-all-start.1 = ((bf16[8,16,8192]{2,1,0:T(8,128)(2,1)}), bf16[8,16,8192]{2,1,0:T(8,128)(2,1)}, u32[]{:S(2)}, u32[]{:S(2)}) async-start(bf16[8,16,8192]{2,1,0:T(8,128)(2,1)} %outer.1.outer_ref), calls=%async_computation.1 | async-start | bytes 4194304 | tf_op jit(solution)/shard_map/all_to_all | solution.py:379
  73.8 61.5 %all-gather = s32[8,1,512]{2,1,0:T(1,128)S(1)} all-gather(s32[1,1,512]{2,1,0:T(1,128)S(1)} %copy-done.7), channel_id=2, replica_groups=mesh['member'=8,'space'=32] {'member'}, dimensions={0}, use_global_device_ids=true | all-gather | bytes 18432 | tf_op jit(solution)/shard_map/all_gather | solution.py:396
  135.4 30.8 %pick.1 = bf16[8,16,512]{2,1,0:T(8,128)(2,1)S(1)} custom-call(s32[8,512]{1,0:T(8,128)S(1)} %fusion.6.place_ref, s32[8,512]{1,0:T(8,128)S(1)} %get-tuple-element.13.shift_ref, bf16[8,16,8192]{2,1,0:T(8,128)(2,1)} %interior.1.inner_ref, bf16[8,16,8192]{2,1,0:T(8,128)(2,1)} %outer.1.outer_ref), custom_call_target="tpu_custom_call" | custom-call | bytes 54000000 | tf_op jit(solution)/shard_map/pick/pallas_call | solution.py:230
  167.6 2.0 collective-permute-start.10
  169.6 4.0 %collective-permute-start.8 = (bf16[16,512]{1,0:T(8,128)(2,1)S(1)}, bf16[16,512]{1,0:T(8,128)(2,1)S(1)}, u32[]{:S(2)}, u32[]{:S(2)}) collective-permute-start(bf16[16,512]{1,0:T(8,128)(2,1)S(1)} %get-tuple-element.23), channel_id=1, source_target_pairs={{0,160},{32,192},{64,224},{96,0},{128,32},{160,64},{192,96},{224,1... | collective-permute-start | bytes 49160 | tf_op jit(solution)/shard_map/ppermute | solution.py:370
  173.6 2.0 collective-permute-start.7
  177.1 4.3 %collective-permute-done.5 = bf16[16,512]{1,0:T(8,128)(2,1)S(1)} collective-permute-done((bf16[16,512]{1,0:T(8,128)(2,1)S(1)}, bf16[16,512]{1,0:T(8,128)(2,1)S(1)}, u32[]{:S(2)}, u32[]{:S(2)}) %collective-permute-start.5) | collective-permute-done | bytes 16416 | tf_op jit(solution)/shard_map/ppermute | solution.py:370
  182.1 6.1 %collective-permute-done.6 = bf16[16,512]{1,0:T(8,128)(2,1)S(1)} collective-permute-done((bf16[16,512]{1,0:T(8,128)(2,1)S(1)}, bf16[16,512]{1,0:T(8,128)(2,1)S(1)}, u32[]{:S(2)}, u32[]{:S(2)}) %collective-permute-start.6) | collective-permute-done | bytes 16416 | tf_op jit(solution)/shard_map/ppermute | solution.py:370
  190.2 2.4 collective-permute-start.11
  192.7 3.0 collective-permute-start.13
  195.7 2.7 collective-permute-start.14
  199.6 5.5 %weights.1 = (bf16[1024,1024]{1,0:T(8,128)(2,1)S(1)}, f32[1024,128]{1,0:T(8,128)S(1)}) custom-call(bf16[128,512]{1,0:T(8,128)(2,1)S(1)} %bitcast.85, bf16[128,512]{1,0:T(8,128)(2,1)S(1)} %collective-permute-done.11.south_ref, bf16[128,512]{1,0:T(8,128)(2,1)S(1)} %collective-permute-done.12.north_ref, f32[3,2,512]{2,1,0:T(2,128)S(1)} %pad_maximum_fusion.obs_ref, ...), custom_call_target="tpu_custom_call" | custom-call | bytes 43200000 | tf_op jit(solution)/shard_map/weights/pallas_call | solution.py:300
  208.0 7.7 %analyse.1 = bf16[8,16,4,8,512]{4,3,2,1,0:T(8,128)(2,1)} custom-call(bf16[1024,1024]{1,0:T(8,128)(2,1)S(1)} %copy-done.5, f32[1024,128]{1,0:T(8,128)S(1)} %get-tuple-element.12.rest_ref, bf16[8,16,8192]{2,1,0:T(8,128)(2,1)S(1)} %all-to-all-done.inner_ref, bf16[8,16,8192]{2,1,0:T(8,128)(2,1)} %all-to-all-done.1.outer_ref), custom_call_target="tpu_custom_call" | custom-call | bytes 21600000 | tf_op jit(solution)/shard_map/analyse/pallas_call | solution.py:340
  215.7 99.6 %all_to_all.15 = bf16[8,16,4,8,512]{4,3,2,1,0:T(8,128)(2,1)S(1)} all-to-all(bf16[8,16,4,8,512]{4,3,2,1,0:T(8,128)(2,1)} %analyse.1), channel_id=1, replica_groups=mesh['member'=8,'space'=32] {'member'}, dimensions={0} | all-to-all | bytes 8388608 | tf_op jit(solution)/shard_map/all_to_all | solution.py:379
  315.3 2.5 copy.19
  (60 shorter events, 14.1 us)
Async XLA Ops:
  9.0 59.7 %all-to-all-start = ((bf16[8,16,8192]{2,1,0:T(8,128)(2,1)}), bf16[8,16,8192]{2,1,0:T(8,128)(2,1)S(1)}, u32[]{:S(2)}, u32[]{:S(2)}) async-start(bf16[8,16,8192]{2,1,0:T(8,128)(2,1)} %interior.1.inner_ref), calls=%async_computation | async-start | bytes 4194304 | tf_op jit(solution)/shard_map/all_to_all | solution.py:379
  17.5 9.2 %copy-start.1 = (f32[8,4,8,512]{3,2,1,0:T(8,128)S(1)}, f32[8,4,8,512]{3,2,1,0:T(8,128)}, u32[]{:S(2)}) copy-start(f32[8,4,8,512]{3,2,1,0:T(8,128)} %east_ref.3) | copy-start | bytes 1572868
  17.5 9.3 %copy-start.3 = (f32[8,4,8,512]{3,2,1,0:T(8,128)S(1)}, f32[8,4,8,512]{3,2,1,0:T(8,128)}, u32[]{:S(2)}) copy-start(f32[8,4,8,512]{3,2,1,0:T(8,128)} %north_ref.3) | copy-start | bytes 1572868
  21.1 19.3 %collective-permute-start = (bf16[4,2,16,4096]{3,2,1,0:T(8,128)(2,1)S(1)}, bf16[4,2,16,4096]{3,2,1,0:T(8,128)(2,1)S(1)}, u32[]{:S(2)}, u32[]{:S(2)}) collective-permute-start(bf16[4,2,16,4096]{3,2,1,0:T(8,128)(2,1)S(1)} %get-tuple-element.9), channel_id=1, source_target_pairs={{0,1},{1,2},{2,3},{3,4},{4,5},{5,6},{6,7},{7,8},{8,9},{9,10},{10,1... | collective-permute-start | bytes 3145736 | tf_op jit(solution)/shard_map/ppermute | solution.py:361
  23.0 17.4 %collective-permute-start.1 = (bf16[4,2,16,4096]{3,2,1,0:T(8,128)(2,1)S(1)}, bf16[4,2,16,4096]{3,2,1,0:T(8,128)(2,1)S(1)}, u32[]{:S(2)}, u32[]{:S(2)}) collective-permute-start(bf16[4,2,16,4096]{3,2,1,0:T(8,128)(2,1)S(1)} %get-tuple-element.10), channel_id=1, source_target_pairs={{1,0},{2,1},{3,2},{4,3},{5,4},{6,5},{7,6},{8,7},{9,8},{10,9},{11,1... | collective-permute-start | bytes 3145736 | tf_op jit(solution)/shard_map/ppermute | solution.py:361
  27.0 13.3 %collective-permute-start.3 = (f32[2,4,8,512]{3,2,1,0:T(8,128)S(1)}, f32[2,4,8,512]{3,2,1,0:T(8,128)S(1)}, u32[]{:S(2)}, u32[]{:S(2)}) collective-permute-start(f32[2,4,8,512]{3,2,1,0:T(8,128)S(1)} %get-tuple-element.19), channel_id=1, source_target_pairs={{1,0},{2,1},{3,2},{4,3},{5,4},{6,5},{7,6},{8,7},{9,8},{10,9},{11,1... | collective-permute-start | bytes 393224 | tf_op jit(solution)/shard_map/ppermute | solution.py:361
  29.0 11.4 %collective-permute-start.2 = (f32[2,4,8,512]{3,2,1,0:T(8,128)S(1)}, f32[2,4,8,512]{3,2,1,0:T(8,128)S(1)}, u32[]{:S(2)}, u32[]{:S(2)}) collective-permute-start(f32[2,4,8,512]{3,2,1,0:T(8,128)S(1)} %get-tuple-element.20), channel_id=1, source_target_pairs={{0,1},{1,2},{2,3},{3,4},{4,5},{5,6},{6,7},{7,8},{8,9},{9,10},{10,1... | collective-permute-start | bytes 393224 | tf_op jit(solution)/shard_map/ppermute | solution.py:361
  48.5 25.2 %copy-start.7 = (s32[1,1,512]{2,1,0:T(1,128)S(1)}, s32[1,1,512]{2,1,0:T(1,128)}, u32[]{:S(2)}) copy-start(s32[1,1,512]{2,1,0:T(1,128)} %param.11) | copy-start | bytes 6148
  68.7 137.7 %all-to-all-start.1 = ((bf16[8,16,8192]{2,1,0:T(8,128)(2,1)}), bf16[8,16,8192]{2,1,0:T(8,128)(2,1)}, u32[]{:S(2)}, u32[]{:S(2)}) async-start(bf16[8,16,8192]{2,1,0:T(8,128)(2,1)} %outer.1.outer_ref), calls=%async_computation.1 | async-start | bytes 4194304 | tf_op jit(solution)/shard_map/all_to_all | solution.py:379
  135.3 32.3 %copy-start.8 = (f32[1,1,512]{2,1,0:T(1,128)S(1)}, f32[1,1,512]{2,1,0:T(1,128)}, u32[]{:S(2)}) copy-start(f32[1,1,512]{2,1,0:T(1,128)} %param.13) | copy-start | bytes 6148
  135.3 57.3 %copy-start.9 = (f32[1,1,512]{2,1,0:T(1,128)S(1)}, f32[1,1,512]{2,1,0:T(1,128)}, u32[]{:S(2)}) copy-start(f32[1,1,512]{2,1,0:T(1,128)} %param.12) | copy-start | bytes 6148
  135.4 63.1 %copy-start.6 = (s32[1,1,3,512]{3,1,2,0:T(1,128)S(1)}, s32[1,1,3,512]{3,1,2,0:T(1,128)}, u32[]{:S(2)}) copy-start(s32[1,1,3,512]{3,1,2,0:T(1,128)} %param.15) | copy-start | bytes 18436
  166.2 9.4 %collective-permute-start.4 = (bf16[16,512]{1,0:T(8,128)(2,1)S(1)}, bf16[16,512]{1,0:T(8,128)(2,1)S(1)}, u32[]{:S(2)}, u32[]{:S(2)}) collective-permute-start(bf16[16,512]{1,0:T(8,128)(2,1)S(1)} %get-tuple-element.27), channel_id=1, source_target_pairs={{0,32},{32,64},{64,96},{96,128},{128,160},{160,192},{192,224},{224... | collective-permute-start | bytes 49160 | tf_op jit(solution)/shard_map/ppermute | solution.py:370
  167.6 20.7 %collective-permute-start.10 = (bf16[16,512]{1,0:T(8,128)(2,1)S(1)}, bf16[16,512]{1,0:T(8,128)(2,1)S(1)}, u32[]{:S(2)}, u32[]{:S(2)}) collective-permute-start(bf16[16,512]{1,0:T(8,128)(2,1)S(1)} %get-tuple-element.21), channel_id=1, source_target_pairs={{0,224},{32,0},{64,32},{96,64},{128,96},{160,128},{192,160},{224,1... | collective-permute-start | bytes 49160 | tf_op jit(solution)/shard_map/ppermute | solution.py:370
  169.6 18.7 %collective-permute-start.9 = (bf16[16,512]{1,0:T(8,128)(2,1)S(1)}, bf16[16,512]{1,0:T(8,128)(2,1)S(1)}, u32[]{:S(2)}, u32[]{:S(2)}) collective-permute-start(bf16[16,512]{1,0:T(8,128)(2,1)S(1)} %get-tuple-element.22), channel_id=1, source_target_pairs={{0,192},{32,224},{64,0},{96,32},{128,64},{160,96},{192,128},{224,1... | collective-permute-start | bytes 49160 | tf_op jit(solution)/shard_map/ppermute | solution.py:370
  169.6 18.7 %collective-permute-start.8 = (bf16[16,512]{1,0:T(8,128)(2,1)S(1)}, bf16[16,512]{1,0:T(8,128)(2,1)S(1)}, u32[]{:S(2)}, u32[]{:S(2)}) collective-permute-start(bf16[16,512]{1,0:T(8,128)(2,1)S(1)} %get-tuple-element.23), channel_id=1, source_target_pairs={{0,160},{32,192},{64,224},{96,0},{128,32},{160,64},{192,96},{224,1... | collective-permute-start | bytes 49160 | tf_op jit(solution)/shard_map/ppermute | solution.py:370
  173.6 14.7 %collective-permute-start.7 = (bf16[16,512]{1,0:T(8,128)(2,1)S(1)}, bf16[16,512]{1,0:T(8,128)(2,1)S(1)}, u32[]{:S(2)}, u32[]{:S(2)}) collective-permute-start(bf16[16,512]{1,0:T(8,128)(2,1)S(1)} %get-tuple-element.24), channel_id=1, source_target_pairs={{0,128},{32,160},{64,192},{96,224},{128,0},{160,32},{192,64},{224,... | collective-permute-start | bytes 49160 | tf_op jit(solution)/shard_map/ppermute | solution.py:370
  175.6 5.8 %collective-permute-start.5 = (bf16[16,512]{1,0:T(8,128)(2,1)S(1)}, bf16[16,512]{1,0:T(8,128)(2,1)S(1)}, u32[]{:S(2)}, u32[]{:S(2)}) collective-permute-start(bf16[16,512]{1,0:T(8,128)(2,1)S(1)} %get-tuple-element.26), channel_id=1, source_target_pairs={{0,64},{32,96},{64,128},{96,160},{128,192},{160,224},{192,0},{224,... | collective-permute-start | bytes 49160 | tf_op jit(solution)/shard_map/ppermute | solution.py:370
  181.5 6.8 %collective-permute-start.6 = (bf16[16,512]{1,0:T(8,128)(2,1)S(1)}, bf16[16,512]{1,0:T(8,128)(2,1)S(1)}, u32[]{:S(2)}, u32[]{:S(2)}) collective-permute-start(bf16[16,512]{1,0:T(8,128)(2,1)S(1)} %get-tuple-element.25), channel_id=1, source_target_pairs={{0,96},{32,128},{64,160},{96,192},{128,224},{160,0},{192,32},{224,... | collective-permute-start | bytes 49160 | tf_op jit(solution)/shard_map/ppermute | solution.py:370
  188.3 11.3 %collective-permute-start.12 = (bf16[128,512]{1,0:T(8,128)(2,1)S(1)}, bf16[128,512]{1,0:T(8,128)(2,1)S(1)}, u32[]{:S(2)}, u32[]{:S(2)}) collective-permute-start(bf16[128,512]{1,0:T(8,128)(2,1)S(1)} %bitcast.83), channel_id=1, source_target_pairs={{1,0},{2,1},{3,2},{4,3},{5,4},{6,5},{7,6},{8,7},{9,8},{10,9},{11,1... | collective-permute-start | bytes 393224 | tf_op jit(solution)/shard_map/ppermute | solution.py:361
  190.2 9.3 %collective-permute-start.11 = (bf16[128,512]{1,0:T(8,128)(2,1)S(1)}, bf16[128,512]{1,0:T(8,128)(2,1)S(1)}, u32[]{:S(2)}, u32[]{:S(2)}) collective-permute-start(bf16[128,512]{1,0:T(8,128)(2,1)S(1)} %bitcast.84), channel_id=1, source_target_pairs={{0,1},{1,2},{2,3},{3,4},{4,5},{5,6},{6,7},{7,8},{8,9},{9,10},{10,1... | collective-permute-start | bytes 393224 | tf_op jit(solution)/shard_map/ppermute | solution.py:361
  192.7 5.8 %collective-permute-start.13 = (f32[2,512]{1,0:T(2,128)S(1)}, f32[2,512]{1,0:T(2,128)S(1)}, u32[]{:S(2)}, u32[]{:S(2)}) collective-permute-start(f32[2,512]{1,0:T(2,128)S(1)} %get-tuple-element.30), channel_id=1, source_target_pairs={{0,1},{1,2},{2,3},{3,4},{4,5},{5,6},{6,7},{7,8},{8,9},{9,10},{10,1... | collective-permute-start | bytes 12296 | tf_op jit(solution)/shard_map/ppermute | solution.py:361
  195.7 3.9 %collective-permute-start.14 = (f32[2,512]{1,0:T(2,128)S(1)}, f32[2,512]{1,0:T(2,128)S(1)}, u32[]{:S(2)}, u32[]{:S(2)}) collective-permute-start(f32[2,512]{1,0:T(2,128)S(1)} %get-tuple-element.30), channel_id=1, source_target_pairs={{1,0},{2,1},{3,2},{4,3},{5,4},{6,5},{7,6},{8,7},{9,8},{10,9},{11,1... | collective-permute-start | bytes 12296 | tf_op jit(solution)/shard_map/ppermute | solution.py:361
  206.4 1.6 copy-start.5
  (3 other events, 3.4 us)

commit v2 on v1

--- a/solution.py
+++ b/solution.py
@@ -129,7 +129,7 @@
             pltpu.VMEM((rows, members, LANES + tiles * width), jnp.float32),
             pltpu.VMEM((4, tiles, rows, width), jnp.float32),
         ],
-        compiler_params=params(),
+        compiler_params=params(60 * 1024 * 1024),
         cost_estimate=cost(8),
         name="interior",
     )(state, wind_east, wind_north)
@@ -199,48 +199,40 @@
     )(state, wind_east, wind_north, below, above, wind_below, wind_above)
 
 
-def pick_kernel(place_ref, shift_ref, inner_ref, outer_ref, raw_ref, pieces):
-    tile = pl.program_id(0)
+def pick_kernel(place_ref, lane_ref, inner_ref, outer_ref, raw_ref):
     members, length = inner_ref.shape[1:]
+    slots = raw_ref.shape[2]
     count = length // LANES
-    for piece in range(count):
-        lanes = slice(piece * LANES, (piece + 1) * LANES)
-        pieces[piece] = inner_ref[0, :, lanes].astype(jnp.float32)
-        pieces[count + piece] = outer_ref[0, :, lanes].astype(jnp.float32)
-    lane = lax.broadcasted_iota(jnp.int32, (members, LANES), 1)
-    unroll = 16
-    for block in range(raw_ref.shape[2] // LANES):
-
-        def body(step, total):
-            for inside in range(unroll):
-                slot = step * unroll + inside
-                at = block * LANES + slot
-                rolled = pltpu.roll(pieces[place_ref[tile, at]], shift_ref[tile, at], 1)
-                total = jnp.where(lane == slot, rolled, total)
-            return total
-
-        total = lax.fori_loop(0, LANES // unroll, body, jnp.zeros((members, LANES), jnp.float32))
-        raw_ref[0, :, block * LANES : (block + 1) * LANES] = total.astype(jnp.bfloat16)
-
-
-def pick(place, shift, inner, outer_part):
+    at_lane = lax.broadcasted_iota(jnp.int32, (LANES, slots), 0)
+    chosen = jnp.where(at_lane == lane_ref[0], 1.0, 0.0).astype(jnp.bfloat16)
+    place = jnp.broadcast_to(place_ref[0], (members, slots))
+    total = jnp.zeros((members, slots), jnp.float32)
+    together = LANES // members
+    for index, half_ref in enumerate((inner_ref, outer_ref)):
+        for first in range(0, count, together):
+            pieces = [half_ref[0, :, (first + i) * LANES : (first + i + 1) * LANES] for i in range(together)]
+            found = jnp.dot(jnp.concatenate(pieces, axis=0), chosen, preferred_element_type=jnp.float32)
+            for i in range(together):
+                here = place == index * count + first + i
+                total = jnp.where(here, found[i * members : (i + 1) * members], total)
+    raw_ref[0] = total.astype(jnp.bfloat16)
+
+
+def pick(place, lane, inner, outer_part):
     tiles, members, length = inner.shape
-    slots = place.shape[1]
-    half = pl.BlockSpec((1, members, length), lambda i, *_: (i, 0, 0))
+    slots = place.shape[2]
+    half = pl.BlockSpec((1, members, length), lambda i: (i, 0, 0))
+    one = pl.BlockSpec((1, 1, slots), lambda i: (i, 0, 0))
     return pl.pallas_call(
         pick_kernel,
-        grid_spec=pltpu.PrefetchScalarGridSpec(
-            num_scalar_prefetch=2,
-            grid=(tiles,),
-            in_specs=[half, half],
-            out_specs=pl.BlockSpec((1, members, slots), lambda i, *_: (i, 0, 0)),
-            scratch_shapes=[pltpu.VMEM((2 * length // LANES, members, LANES), jnp.float32)],
-        ),
+        grid=(tiles,),
+        in_specs=[one, one, half, half],
+        out_specs=pl.BlockSpec((1, members, slots), lambda i: (i, 0, 0)),
         out_shape=jax.ShapeDtypeStruct((tiles, members, slots), jnp.bfloat16),
         compiler_params=params(),
-        cost_estimate=cost(15),
+        cost_estimate=cost(8),
         name="pick",
-    )(place, shift, inner, outer_part)
+    )(place, lane, inner, outer_part)
 
 
 def loc_weights(classes):
@@ -348,7 +340,7 @@
         ],
         out_specs=pl.BlockSpec((groups, each, 1, 8, width), lambda i: (0, 0, i, 0, 0)),
         out_shape=jax.ShapeDtypeStruct((groups, each, levels, 8, width), jnp.bfloat16),
-        compiler_params=params(),
+        compiler_params=params(60 * 1024 * 1024),
         cost_estimate=cost(6),
         name="analyse",
     )(mix, rest, inner, outer_part)
@@ -361,18 +353,21 @@
     return lax.ppermute(high, "space", up), lax.ppermute(low, "space", down)
 
 
-def swap_members(blocks):
+def partner(value, bit):
+    devices = lax.axis_size("member")
+    return lax.ppermute(value, "member", [(i, i ^ bit) for i in range(devices)])
+
+
+def gather_members(value):
     devices = lax.axis_size("member")
     here = lax.axis_index("member")
-    got = [lax.dynamic_index_in_dim(blocks, here, 0, keepdims=False)]
-    for shift in range(1, devices):
-        block = lax.dynamic_index_in_dim(blocks, lax.rem(here + shift, devices), 0, keepdims=False)
-        got.append(lax.ppermute(block, "member", [(i, (i + shift) % devices) for i in range(devices)]))
-    stacked = jnp.stack(got)
-    out = jnp.zeros_like(blocks)
-    for shift in range(devices):
-        out = lax.dynamic_update_index_in_dim(out, got[shift], lax.rem(here + devices - shift, devices), 0)
-    return out
+    group = devices // 2
+    held = jnp.stack([value] + [partner(value, bit) for bit in range(1, group)])
+    inside = here % group
+    held = jnp.stack([lax.dynamic_index_in_dim(held, inside ^ i, 0, keepdims=False) for i in range(group)])
+    other = partner(held, group)
+    own_first = here < group
+    return jnp.concatenate([jnp.where(own_first, held, other), jnp.where(own_first, other, held)])
 
 
 def all_to_all(blocks):
@@ -382,32 +377,39 @@
 def on_device(state, wind_east, wind_north, obs_col, obs_val, obs_rinv, obs_count, loc_class):
     members, tiles, levels, rows, width = state.shape
     slots = obs_col.shape[2]
+
+    columns = gather_members(obs_col[0, 0])
+    row = (columns // width) % rows
+    inside = (row >= 2) & (row < rows - 2)
+    kept = jnp.where(inside, row - 2, jnp.where(row < 2, row, row - 4))
+    offset = (columns // (rows * width)) * (4 * width) + kept * width + columns % width
+    place = offset // LANES + jnp.where(inside, 0, levels * 4 * width // LANES)
+    lane = offset % LANES
+
+    inner = interior(state, wind_east, wind_north)
+    inner, place, lane, state, wind_east, wind_north, obs_val, obs_rinv = lax.optimization_barrier(
+        (inner, place, lane, state, wind_east, wind_north, obs_val, obs_rinv)
+    )
+    inner_tile = all_to_all(inner)
 
     low, high = edge_rows(state)
     below, above = to_neighbours(low, high)
     winds = jnp.stack([wind_east[:, :, 0], wind_north[:, :, 0], wind_east[:, :, rows - 1], wind_north[:, :, rows - 1]])
     winds = jnp.swapaxes(winds, 1, 2)
     wind_below, wind_above = to_neighbours(winds[0:2], winds[2:4])
-
     live = jnp.arange(slots, dtype=jnp.int32) < obs_count[0, 0]
     obs = jnp.stack([obs_val[0, 0], jnp.where(live, obs_rinv[0, 0], jnp.float32(0.0))])
     obs_south, obs_north = to_neighbours(obs, obs)
-
-    columns = lax.all_gather(obs_col[0, 0], "member")
-    row = (columns // width) % rows
-    inside = (row >= 2) & (row < rows - 2)
-    kept = jnp.where(inside, row - 2, jnp.where(row < 2, row, row - 4))
-    offset = (columns // (rows * width)) * (4 * width) + kept * width + columns % width
-    place = offset // LANES + jnp.where(inside, 0, levels * 4 * width // LANES)
-    shift = (jnp.arange(slots, dtype=jnp.int32)[None, :] - offset) % LANES
-
-    inner = interior(state, wind_east, wind_north)
-    inner_tile = all_to_all(inner)
     outside = outer(state, wind_east, wind_north, below, above, wind_below, wind_above)
-    raw = swap_members(pick(place, shift, inner, outside)).reshape(tiles * members, slots)
+    picked = pick(place[:, None], lane[:, None], inner, outside)
+
+    picked, inner_tile = lax.optimization_barrier((picked, inner_tile))
+    raw = all_to_all(picked)
+    outside, raw = lax.optimization_barrier((outside, raw))
+    outer_tile = all_to_all(outside)
+    raw = raw.reshape(tiles * members, slots)
     south, north = to_neighbours(raw, raw)
     mix, rest = tile_mix(raw, south, north, jnp.stack([obs, obs_south, obs_north]), loc_class[0, 0])
-    outer_tile = all_to_all(outside)
     updated = analyse(mix, rest, inner_tile, outer_tile, levels, width)
     final = all_to_all(updated)
     return jnp.swapaxes(final, 0, 1)

time: 322 us -> 255 us (0.79)
  blocking collectives: 161 us -> 112 us
  Pallas kernels: 62.6 us -> 40.6 us
  waiting for transfers between devices: 40.7 us -> 55.8 us
  starting transfers between devices: 44.4 us -> 38 us
    all_gather x1 -> x0, blocking collectives: 61.5 us -> none  [on_device(): columns = lax.all_gather(obs_col[0, 0], 'member')]
    pallas_call x1, Pallas kernels: 30.8 us -> 7.4 us  [pick(): pl.pallas_call(pick_kernel, grid=(tiles,), in_specs=[one, one, half, half...]
    all_to_all x2, waiting for transfers between devices: 20.2 us -> 41.9 us  [all_to_all(): lax.all_to_all(blocks, 'member', split_axis=0, concat_axis=0, tiled=True)]
    all_to_all x1 -> x2, blocking collectives: 99.6 us -> 112 us  [all_to_all(): lax.all_to_all(blocks, 'member', split_axis=0, concat_axis=0, tiled=True)]
    ppermute x7 -> x4, waiting for transfers between devices: 10.4 us -> 4.13 us  [partner(): return lax.ppermute(value, 'member', [(i, i ^ bit) for i in range(devices)])]
    all_to_all x2, starting transfers between devices: 12.8 us -> 8.1 us  [all_to_all(): lax.all_to_all(blocks, 'member', split_axis=0, concat_axis=0, tiled=True)]
    ppermute x7 -> x4, starting transfers between devices: 11.6 us -> 9.77 us  [partner(): return lax.ppermute(value, 'member', [(i, i ^ bit) for i in range(devices)])]
  transfers between devices with their start and end apart: 17 -> 14, of which waited for: 5 -> 6; matrix products, arithmetic and copies ran while one was open for 0% -> 0% of each run, Pallas kernels for 15% -> 12%
where the time goes in v2:
time: 255 us; the launch traced here: 254 us
  blocking collectives  112 us (44%)
  waiting for transfers between devices  55.8 us (22%)
  Pallas kernels  40.6 us (16%)
  starting transfers between devices  38 us (15%)
  local copies, waits for them, and re-layouts  5.48 us (2%)
    all_to_all x2, blocking collectives, all_to_all(): lax.all_to_all(blocks, 'member', split_axis=0, concat_axis=0, tiled=True)  112 us
    all_to_all x2, waiting for transfers between devices, all_to_all(): lax.all_to_all(blocks, 'member', split_axis=0, concat_axis=0, tiled=True)  41.9 us
    ppermute x8, starting transfers between devices, to_neighbours(): return (lax.ppermute(high, 'space', up), lax.ppermute(low, 'space', down))  20.2 us
    ppermute x4, starting transfers between devices, partner(): return lax.ppermute(value, 'member', [(i, i ^ bit) for i in range(devices)])  9.77 us
    ppermute x8, waiting for transfers between devices, to_neighbours(): return (lax.ppermute(high, 'space', up), lax.ppermute(low, 'space', down))  9.67 us
    pallas_call x1, Pallas kernels, analyse(): pl.pallas_call(mix_kernel, grid=(levels,), in_specs=[pl.BlockSpec(mix.sha...  8.89 us
    pallas_call x1, Pallas kernels, outer(): pl.pallas_call(outer_kernel, grid=(levels,), in_specs=[pl.BlockSpec((memb...  8.16 us
    all_to_all x2, starting transfers between devices, all_to_all(): lax.all_to_all(blocks, 'member', split_axis=0, concat_axis=0, tiled=True)  8.1 us
  transfers between devices with their start and end apart: 14, of which 6 were waited for; matrix products, arithmetic and copies ran while one was open for 0% of the time, Pallas kernels for 12%

profile of v2, /device:TPU:14, one launch (start us, length us, event | category | flops | bytes accessed | tf_op | source)
XLA Modules:
  0.0 253.7 jit_solution(7183650236106296131)
XLA Ops:
  0.0 4.6 %collective-permute-start.2 = (s32[512]{0:T(512)}, s32[512]{0:T(512)S(1)}, u32[]{:S(2)}, u32[]{:S(2)}) collective-permute-start(s32[512]{0:T(512)} %bitcast.39), channel_id=1, source_target_pairs={{0,96},{32,64},{64,32},{96,0},{128,224},{160,192},{192,160},{224,1... | collective-permute-start | bytes 6152 | tf_op jit(solution)/shard_map/ppermute | solution.py:358
  6.4 2.9 %collective-permute-done.1 = s32[512]{0:T(512)S(1)} collective-permute-done((s32[512]{0:T(512)}, s32[512]{0:T(512)S(1)}, u32[]{:S(2)}, u32[]{:S(2)}) %collective-permute-start.1) | collective-permute-done | bytes 2080 | tf_op jit(solution)/shard_map/ppermute | solution.py:358
  10.1 4.6 %collective-permute-start.3 = (s32[4,512]{1,0:T(4,128)S(1)}, s32[4,512]{1,0:T(4,128)S(1)}, u32[]{:S(2)}, u32[]{:S(2)}) collective-permute-start(s32[4,512]{1,0:T(4,128)S(1)} %pad_add_fusion.2), channel_id=1, source_target_pairs={{0,128},{32,160},{64,192},{96,224},{128,0},{160,32},{192,64},{224,... | collective-permute-start | bytes 24584 | tf_op jit(solution)/shard_map/ppermute | solution.py:358
  14.6 7.1 %interior.1.inner_ref = bf16[8,16,8192]{2,1,0:T(8,128)(2,1)} custom-call(bf16[16,8,4,8,512]{4,3,2,1,0:T(8,128)(2,1)} %state_ref.3, f32[8,4,8,512]{3,2,1,0:T(8,128)} %east_ref.2, f32[8,4,8,512]{3,2,1,0:T(8,128)} %north_ref.2), custom_call_target="tpu_custom_call" | custom-call | bytes 28800000 | tf_op jit(solution)/shard_map/interior/pallas_call | solution.py:121
  21.9 3.6 %all-to-all-start = ((bf16[8,16,8192]{2,1,0:T(8,128)(2,1)}), bf16[8,16,8192]{2,1,0:T(8,128)(2,1)S(1)}, u32[]{:S(2)}, u32[]{:S(2)}) async-start(bf16[8,16,8192]{2,1,0:T(8,128)(2,1)} %interior.1.inner_ref), calls=%async_computation | async-start | bytes 4194304 | tf_op jit(solution)/shard_map/all_to_all | solution.py:374
  25.5 3.6 %edges.1 = (bf16[4,2,16,4096]{3,2,1,0:T(8,128)(2,1)S(1)}, bf16[4,2,16,4096]{3,2,1,0:T(8,128)(2,1)S(1)}) custom-call(bf16[16,8,4,8,512]{4,3,2,1,0:T(8,128)(2,1)} %state_ref.3), custom_call_target="tpu_custom_call" | custom-call | bytes 10800000 | tf_op jit(solution)/shard_map/edges/pallas_call | solution.py:56
  29.1 1.9 collective-permute-start.4
  31.0 3.6 %collective-permute-start.5 = (bf16[4,2,16,4096]{3,2,1,0:T(8,128)(2,1)S(1)}, bf16[4,2,16,4096]{3,2,1,0:T(8,128)(2,1)S(1)}, u32[]{:S(2)}, u32[]{:S(2)}) collective-permute-start(bf16[4,2,16,4096]{3,2,1,0:T(8,128)(2,1)S(1)} %get-tuple-element.25), channel_id=1, source_target_pairs={{1,0},{2,1},{3,2},{4,3},{5,4},{6,5},{7,6},{8,7},{9,8},{10,9},{11,1... | collective-permute-start | bytes 3145736 | tf_op jit(solution)/shard_map/ppermute | solution.py:353
  37.3 2.4 collective-permute-start.6
  39.8 8.6 %collective-permute-done.7.wind_above_ref = f32[2,4,8,512]{3,2,1,0:T(8,128)S(1)} collective-permute-done((f32[2,4,8,512]{3,2,1,0:T(8,128)S(1)}, f32[2,4,8,512]{3,2,1,0:T(8,128)S(1)}, u32[]{:S(2)}, u32[]{:S(2)}) %collective-permute-start.7) | collective-permute-done | bytes 131104 | tf_op jit(solution)/shard_map/ppermute | solution.py:353
  48.4 8.2 %outer.1.outer_ref = bf16[8,16,8192]{2,1,0:T(8,128)(2,1)} custom-call(bf16[16,8,4,8,512]{4,3,2,1,0:T(8,128)(2,1)} %state_ref.3, f32[8,4,8,512]{3,2,1,0:T(8,128)S(1)} %copy-done.1, f32[8,4,8,512]{3,2,1,0:T(8,128)S(1)} %copy-done.2, bf16[4,2,16,4096]{3,2,1,0:T(8,128)(2,1)S(1)} %collective-permute-done.4.below_ref, ...), custom_call_target="tpu_custom_call" | custom-call | bytes 32400000 | tf_op jit(solution)/shard_map/outer/pallas_call | solution.py:177
  56.5 7.4 %pick.1 = bf16[8,16,512]{2,1,0:T(8,128)(2,1)S(1)} custom-call(s32[8,1,512]{2,1,0:T(1,128)S(1)} %copy.13.place_ref, s32[8,1,512]{2,1,0:T(1,128)S(1)} %broadcast_in_dim.18.lane_ref, bf16[8,16,8192]{2,1,0:T(8,128)(2,1)S(1)} %copy-done, bf16[8,16,8192]{2,1,0:T(8,128)(2,1)} %outer.1.outer_ref), custom_call_target="tpu_custom_call" | custom-call | bytes 28800000 | tf_op jit(solution)/shard_map/pick/pallas_call | solution.py:226
  64.0 11.6 %all-to-all-done.inner_ref = bf16[8,16,8192]{2,1,0:T(8,128)(2,1)S(1)} async-done(((bf16[8,16,8192]{2,1,0:T(8,128)(2,1)}), bf16[8,16,8192]{2,1,0:T(8,128)(2,1)S(1)}, u32[]{:S(2)}, u32[]{:S(2)}) %all-to-all-start) | async-done | bytes 2097184 | tf_op jit(solution)/shard_map/all_to_all | solution.py:374
  75.5 11.8 %all_to_all.20 = bf16[8,16,512]{2,1,0:T(8,128)(2,1)S(1)} all-to-all(bf16[8,16,512]{2,1,0:T(8,128)(2,1)S(1)} %pick.1), channel_id=1, replica_groups=mesh['member'=8,'space'=32] {'member'}, dimensions={0} | all-to-all | bytes 262144 | tf_op jit(solution)/shard_map/all_to_all | solution.py:374
  87.4 4.5 %all-to-all-start.2 = ((bf16[8,16,8192]{2,1,0:T(8,128)(2,1)}), bf16[8,16,8192]{2,1,0:T(8,128)(2,1)}, u32[]{:S(2)}, u32[]{:S(2)}) async-start(bf16[8,16,8192]{2,1,0:T(8,128)(2,1)} %outer.1.outer_ref), calls=%async_computation.2 | async-start | bytes 4194304 | tf_op jit(solution)/shard_map/all_to_all | solution.py:374
  92.5 1.9 collective-permute-start.9
  94.5 2.4 collective-permute-start.8
  96.9 3.8 %collective-permute-start.10 = (f32[2,512]{1,0:T(2,128)S(1)}, f32[2,512]{1,0:T(2,128)S(1)}, u32[]{:S(2)}, u32[]{:S(2)}) collective-permute-start(f32[2,512]{1,0:T(2,128)S(1)} %get-tuple-element.52), channel_id=1, source_target_pairs={{0,1},{1,2},{2,3},{3,4},{4,5},{5,6},{6,7},{7,8},{8,9},{9,10},{10,1... | collective-permute-start | bytes 12296 | tf_op jit(solution)/shard_map/ppermute | solution.py:353
  100.8 2.1 collective-permute-start.11
  104.0 5.5 %weights.1 = (bf16[1024,1024]{1,0:T(8,128)(2,1)S(1)}, f32[1024,128]{1,0:T(8,128)S(1)}) custom-call(bf16[128,512]{1,0:T(8,128)(2,1)S(1)} %bitcast.32, bf16[128,512]{1,0:T(8,128)(2,1)S(1)} %collective-permute-done.8.south_ref, bf16[128,512]{1,0:T(8,128)(2,1)S(1)} %collective-permute-done.9.north_ref, f32[3,2,512]{2,1,0:T(2,128)S(1)} %pad_maximum_fusion.obs_ref, ...), custom_call_target="tpu_custom_call" | custom-call | bytes 43200000 | tf_op jit(solution)/shard_map/weights/pallas_call | solution.py:292
  111.8 30.4 %all-to-all-done.2.outer_ref = bf16[8,16,8192]{2,1,0:T(8,128)(2,1)} async-done(((bf16[8,16,8192]{2,1,0:T(8,128)(2,1)}), bf16[8,16,8192]{2,1,0:T(8,128)(2,1)}, u32[]{:S(2)}, u32[]{:S(2)}) %all-to-all-start.2) | async-done | bytes 2097184 | tf_op jit(solution)/shard_map/all_to_all | solution.py:374
  142.1 8.9 %analyse.1 = bf16[8,16,4,8,512]{4,3,2,1,0:T(8,128)(2,1)} custom-call(bf16[1024,1024]{1,0:T(8,128)(2,1)} %copy-done.3, f32[1024,128]{1,0:T(8,128)} %copy-done.4, bf16[8,16,8192]{2,1,0:T(8,128)(2,1)} %copy-done.5, bf16[8,16,8192]{2,1,0:T(8,128)(2,1)} %all-to-all-done.2.outer_ref), custom_call_target="tpu_custom_call" | custom-call | bytes 21600000 | tf_op jit(solution)/shard_map/analyse/pallas_call | solution.py:332
  151.0 100.1 %all_to_all.21 = bf16[8,16,4,8,512]{4,3,2,1,0:T(8,128)(2,1)S(1)} all-to-all(bf16[8,16,4,8,512]{4,3,2,1,0:T(8,128)(2,1)} %analyse.1), channel_id=1, replica_groups=mesh['member'=8,'space'=32] {'member'}, dimensions={0} | all-to-all | bytes 8388608 | tf_op jit(solution)/shard_map/all_to_all | solution.py:374
  251.2 2.5 copy.14
  (48 shorter events, 8.6 us)
Async XLA Ops:
  0.0 6.4 %collective-permute-start.2 = (s32[512]{0:T(512)}, s32[512]{0:T(512)S(1)}, u32[]{:S(2)}, u32[]{:S(2)}) collective-permute-start(s32[512]{0:T(512)} %bitcast.39), channel_id=1, source_target_pairs={{0,96},{32,64},{64,32},{96,0},{128,224},{160,192},{192,160},{224,1... | collective-permute-start | bytes 6152 | tf_op jit(solution)/shard_map/ppermute | solution.py:358
  4.6 4.7 %collective-permute-start.1 = (s32[512]{0:T(512)}, s32[512]{0:T(512)S(1)}, u32[]{:S(2)}, u32[]{:S(2)}) collective-permute-start(s32[512]{0:T(512)} %bitcast.40), channel_id=1, source_target_pairs={{0,64},{32,96},{64,0},{96,32},{128,192},{160,224},{192,128},{224,1... | collective-permute-start | bytes 6152 | tf_op jit(solution)/shard_map/ppermute | solution.py:358
  4.6 4.7 %collective-permute-start = (s32[512]{0:T(512)}, s32[512]{0:T(512)S(1)}, u32[]{:S(2)}, u32[]{:S(2)}) collective-permute-start(s32[512]{0:T(512)} %bitcast.41), channel_id=1, source_target_pairs={{0,32},{32,0},{64,96},{96,64},{128,160},{160,128},{192,224},{224,1... | collective-permute-start | bytes 6152 | tf_op jit(solution)/shard_map/ppermute | solution.py:358
  10.1 11.7 %collective-permute-start.3 = (s32[4,512]{1,0:T(4,128)S(1)}, s32[4,512]{1,0:T(4,128)S(1)}, u32[]{:S(2)}, u32[]{:S(2)}) collective-permute-start(s32[4,512]{1,0:T(4,128)S(1)} %pad_add_fusion.2), channel_id=1, source_target_pairs={{0,128},{32,160},{64,192},{96,224},{128,0},{160,32},{192,64},{224,... | collective-permute-start | bytes 24584 | tf_op jit(solution)/shard_map/ppermute | solution.py:358
  21.9 53.7 %all-to-all-start = ((bf16[8,16,8192]{2,1,0:T(8,128)(2,1)}), bf16[8,16,8192]{2,1,0:T(8,128)(2,1)S(1)}, u32[]{:S(2)}, u32[]{:S(2)}) async-start(bf16[8,16,8192]{2,1,0:T(8,128)(2,1)} %interior.1.inner_ref), calls=%async_computation | async-start | bytes 4194304 | tf_op jit(solution)/shard_map/all_to_all | solution.py:374
  25.5 9.2 %copy-start.1 = (f32[8,4,8,512]{3,2,1,0:T(8,128)S(1)}, f32[8,4,8,512]{3,2,1,0:T(8,128)}, u32[]{:S(2)}) copy-start(f32[8,4,8,512]{3,2,1,0:T(8,128)} %east_ref.2) | copy-start | bytes 1572868
  25.5 9.5 %copy-start.2 = (f32[8,4,8,512]{3,2,1,0:T(8,128)S(1)}, f32[8,4,8,512]{3,2,1,0:T(8,128)}, u32[]{:S(2)}) copy-start(f32[8,4,8,512]{3,2,1,0:T(8,128)} %north_ref.2) | copy-start | bytes 1572868
  29.1 19.3 %collective-permute-start.4 = (bf16[4,2,16,4096]{3,2,1,0:T(8,128)(2,1)S(1)}, bf16[4,2,16,4096]{3,2,1,0:T(8,128)(2,1)S(1)}, u32[]{:S(2)}, u32[]{:S(2)}) collective-permute-start(bf16[4,2,16,4096]{3,2,1,0:T(8,128)(2,1)S(1)} %get-tuple-element.24), channel_id=1, source_target_pairs={{0,1},{1,2},{2,3},{3,4},{4,5},{5,6},{6,7},{7,8},{8,9},{9,10},{10,1... | collective-permute-start | bytes 3145736 | tf_op jit(solution)/shard_map/ppermute | solution.py:353
  31.0 17.4 %collective-permute-start.5 = (bf16[4,2,16,4096]{3,2,1,0:T(8,128)(2,1)S(1)}, bf16[4,2,16,4096]{3,2,1,0:T(8,128)(2,1)S(1)}, u32[]{:S(2)}, u32[]{:S(2)}) collective-permute-start(bf16[4,2,16,4096]{3,2,1,0:T(8,128)(2,1)S(1)} %get-tuple-element.25), channel_id=1, source_target_pairs={{1,0},{2,1},{3,2},{4,3},{5,4},{6,5},{7,6},{8,7},{9,8},{10,9},{11,1... | collective-permute-start | bytes 3145736 | tf_op jit(solution)/shard_map/ppermute | solution.py:353
  35.4 13.0 %collective-permute-start.7 = (f32[2,4,8,512]{3,2,1,0:T(8,128)S(1)}, f32[2,4,8,512]{3,2,1,0:T(8,128)S(1)}, u32[]{:S(2)}, u32[]{:S(2)}) collective-permute-start(f32[2,4,8,512]{3,2,1,0:T(8,128)S(1)} %get-tuple-element.43), channel_id=1, source_target_pairs={{1,0},{2,1},{3,2},{4,3},{5,4},{6,5},{7,6},{8,7},{9,8},{10,9},{11,1... | collective-permute-start | bytes 393224 | tf_op jit(solution)/shard_map/ppermute | solution.py:353
  37.3 11.0 %collective-permute-start.6 = (f32[2,4,8,512]{3,2,1,0:T(8,128)S(1)}, f32[2,4,8,512]{3,2,1,0:T(8,128)S(1)}, u32[]{:S(2)}, u32[]{:S(2)}) collective-permute-start(f32[2,4,8,512]{3,2,1,0:T(8,128)S(1)} %get-tuple-element.44), channel_id=1, source_target_pairs={{0,1},{1,2},{2,3},{3,4},{4,5},{5,6},{6,7},{7,8},{8,9},{9,10},{10,1... | collective-permute-start | bytes 393224 | tf_op jit(solution)/shard_map/ppermute | solution.py:353
  39.8 16.7 %copy-start = (bf16[8,16,8192]{2,1,0:T(8,128)(2,1)S(1)}, bf16[8,16,8192]{2,1,0:T(8,128)(2,1)}, u32[]{:S(2)}) copy-start(bf16[8,16,8192]{2,1,0:T(8,128)(2,1)} %interior.1.inner_ref) | copy-start | bytes 6291460
  75.5 11.9 %copy-start.5 = (bf16[8,16,8192]{2,1,0:T(8,128)(2,1)}, bf16[8,16,8192]{2,1,0:T(8,128)(2,1)S(1)}, u32[]{:S(2)}) copy-start(bf16[8,16,8192]{2,1,0:T(8,128)(2,1)S(1)} %all-to-all-done.inner_ref) | copy-start | bytes 6291460
  87.4 5.2 %copy-start.7 = (f32[1,1,512]{2,1,0:T(1,128)S(1)}, f32[1,1,512]{2,1,0:T(1,128)}, u32[]{:S(2)}) copy-start(f32[1,1,512]{2,1,0:T(1,128)} %param.13) | copy-start | bytes 6148
  87.4 9.5 %copy-start.8 = (f32[1,1,512]{2,1,0:T(1,128)S(1)}, f32[1,1,512]{2,1,0:T(1,128)}, u32[]{:S(2)}) copy-start(f32[1,1,512]{2,1,0:T(1,128)} %param.12) | copy-start | bytes 6148
  87.4 15.5 %copy-start.6 = (s32[1,1,3,512]{3,1,2,0:T(1,128)S(1)}, s32[1,1,3,512]{3,1,2,0:T(1,128)}, u32[]{:S(2)}) copy-start(s32[1,1,3,512]{3,1,2,0:T(1,128)} %param.15) | copy-start | bytes 18436
  87.4 54.8 %all-to-all-start.2 = ((bf16[8,16,8192]{2,1,0:T(8,128)(2,1)}), bf16[8,16,8192]{2,1,0:T(8,128)(2,1)}, u32[]{:S(2)}, u32[]{:S(2)}) async-start(bf16[8,16,8192]{2,1,0:T(8,128)(2,1)} %outer.1.outer_ref), calls=%async_computation.2 | async-start | bytes 4194304 | tf_op jit(solution)/shard_map/all_to_all | solution.py:374
  92.5 11.5 %collective-permute-start.9 = (bf16[128,512]{1,0:T(8,128)(2,1)S(1)}, bf16[128,512]{1,0:T(8,128)(2,1)S(1)}, u32[]{:S(2)}, u32[]{:S(2)}) collective-permute-start(bf16[128,512]{1,0:T(8,128)(2,1)S(1)} %bitcast.30), channel_id=1, source_target_pairs={{1,0},{2,1},{3,2},{4,3},{5,4},{6,5},{7,6},{8,7},{9,8},{10,9},{11,1... | collective-permute-start | bytes 393224 | tf_op jit(solution)/shard_map/ppermute | solution.py:353
  94.5 9.5 %collective-permute-start.8 = (bf16[128,512]{1,0:T(8,128)(2,1)S(1)}, bf16[128,512]{1,0:T(8,128)(2,1)S(1)}, u32[]{:S(2)}, u32[]{:S(2)}) collective-permute-start(bf16[128,512]{1,0:T(8,128)(2,1)S(1)} %bitcast.31), channel_id=1, source_target_pairs={{0,1},{1,2},{2,3},{3,4},{4,5},{5,6},{6,7},{7,8},{8,9},{9,10},{10,1... | collective-permute-start | bytes 393224 | tf_op jit(solution)/shard_map/ppermute | solution.py:353
  96.9 6.0 %collective-permute-start.10 = (f32[2,512]{1,0:T(2,128)S(1)}, f32[2,512]{1,0:T(2,128)S(1)}, u32[]{:S(2)}, u32[]{:S(2)}) collective-permute-start(f32[2,512]{1,0:T(2,128)S(1)} %get-tuple-element.52), channel_id=1, source_target_pairs={{0,1},{1,2},{2,3},{3,4},{4,5},{5,6},{6,7},{7,8},{8,9},{9,10},{10,1... | collective-permute-start | bytes 12296 | tf_op jit(solution)/shard_map/ppermute | solution.py:353
  100.8 3.2 %collective-permute-start.11 = (f32[2,512]{1,0:T(2,128)S(1)}, f32[2,512]{1,0:T(2,128)S(1)}, u32[]{:S(2)}, u32[]{:S(2)}) collective-permute-start(f32[2,512]{1,0:T(2,128)S(1)} %get-tuple-element.52), channel_id=1, source_target_pairs={{1,0},{2,1},{3,2},{4,3},{5,4},{6,5},{7,6},{8,7},{9,8},{10,9},{11,1... | collective-permute-start | bytes 12296 | tf_op jit(solution)/shard_map/ppermute | solution.py:353
  109.5 1.4 copy-start.3
  110.9 0.9 copy-start.4

commit v3 on v2

--- a/solution.py
+++ b/solution.py
@@ -193,46 +193,58 @@
             pltpu.VMEM((rows + 4, members, LANES + tiles * width), jnp.float32),
             pltpu.VMEM((4, tiles, rows + 4, width), jnp.float32),
         ],
-        compiler_params=params(),
+        compiler_params=params(60 * 1024 * 1024),
         cost_estimate=cost(9),
         name="outer",
     )(state, wind_east, wind_north, below, above, wind_below, wind_above)
 
 
-def pick_kernel(place_ref, lane_ref, inner_ref, outer_ref, raw_ref):
-    members, length = inner_ref.shape[1:]
-    slots = raw_ref.shape[2]
-    count = length // LANES
+def pick_kernel(steps, place_ref, lane_ref, part_ref, *refs):
+    before_ref, raw_ref, total = refs if len(refs) == 3 else (None, *refs)
+    groups, each, length = part_ref.shape
+    members, slots = raw_ref.shape
+    step = pl.program_id(0)
     at_lane = lax.broadcasted_iota(jnp.int32, (LANES, slots), 0)
-    chosen = jnp.where(at_lane == lane_ref[0], 1.0, 0.0).astype(jnp.bfloat16)
-    place = jnp.broadcast_to(place_ref[0], (members, slots))
-    total = jnp.zeros((members, slots), jnp.float32)
-    together = LANES // members
-    for index, half_ref in enumerate((inner_ref, outer_ref)):
-        for first in range(0, count, together):
-            pieces = [half_ref[0, :, (first + i) * LANES : (first + i + 1) * LANES] for i in range(together)]
-            found = jnp.dot(jnp.concatenate(pieces, axis=0), chosen, preferred_element_type=jnp.float32)
-            for i in range(together):
-                here = place == index * count + first + i
-                total = jnp.where(here, found[i * members : (i + 1) * members], total)
-    raw_ref[0] = total.astype(jnp.bfloat16)
-
-
-def pick(place, lane, inner, outer_part):
-    tiles, members, length = inner.shape
-    slots = place.shape[2]
-    half = pl.BlockSpec((1, members, length), lambda i: (i, 0, 0))
-    one = pl.BlockSpec((1, 1, slots), lambda i: (i, 0, 0))
-    return pl.pallas_call(
-        pick_kernel,
-        grid=(tiles,),
-        in_specs=[one, one, half, half],
-        out_specs=pl.BlockSpec((1, members, slots), lambda i: (i, 0, 0)),
-        out_shape=jax.ShapeDtypeStruct((tiles, members, slots), jnp.bfloat16),
-        compiler_params=params(),
-        cost_estimate=cost(8),
+
+    @pl.when(step == 0)
+    def _():
+        if before_ref is None:
+            total[...] = jnp.zeros(total.shape, jnp.float32)
+        else:
+            total[...] = before_ref[...].astype(jnp.float32)
+
+    here = place_ref[...] - step * (length // LANES)
+    pieces = []
+    for piece in range(length // LANES):
+        wanted = jnp.where(here == piece, lane_ref[...], -1)
+        pieces.append(jnp.where(at_lane == wanted, 1.0, 0.0).astype(jnp.bfloat16))
+    flat = part_ref[...].reshape(members, length)
+    total[...] += jnp.dot(flat, jnp.concatenate(pieces, axis=0), preferred_element_type=jnp.float32)
+
+    @pl.when(step == steps - 1)
+    def _():
+        raw_ref[...] = total[...].astype(jnp.bfloat16)
+
+
+def pick(place, lane, part, before=None):
+    groups, each, length = part.shape
+    slots = place.shape[1]
+    members = groups * each
+    steps = 8
+    row = pl.BlockSpec((1, slots), lambda i: (0, 0))
+    whole = pl.BlockSpec((members, slots), lambda i: (0, 0))
+    return pl.pallas_call(
+        functools.partial(pick_kernel, steps),
+        grid=(steps,),
+        in_specs=[row, row, pl.BlockSpec((groups, each, length // steps), lambda i: (0, 0, i))]
+        + ([] if before is None else [whole]),
+        out_specs=whole,
+        scratch_shapes=[pltpu.VMEM((members, slots), jnp.float32)],
+        out_shape=jax.ShapeDtypeStruct((members, slots), jnp.bfloat16),
+        compiler_params=params(59 * 1024 * 1024),
+        cost_estimate=cost(4),
         name="pick",
-    )(place, lane, inner, outer_part)
+    )(place, lane, part, *([] if before is None else [before]))
 
 
 def loc_weights(classes):
@@ -243,107 +255,156 @@
     return total
 
 
-def weights_kernel(own_ref, south_ref, north_ref, obs_ref, class_ref, mix_ref, rest_ref):
-    dot = functools.partial(jnp.dot, precision=lax.Precision.HIGHEST, preferred_element_type=jnp.float32)
-    members = own_ref.shape[0]
+def halves_of(value):
+    high = value.astype(jnp.bfloat16)
+    return high, (value - high.astype(jnp.float32)).astype(jnp.bfloat16)
+
+
+def product(left, right, turned=False):
+    over = (((1,), (1 if turned else 0,)), ((), ()))
+    dot = functools.partial(lax.dot_general, dimension_numbers=over, preferred_element_type=jnp.float32)
+    (a, b), (c, d) = halves_of(left), halves_of(right)
+    return dot(a, c) + (dot(a, d) + dot(b, c))
+
+
+def gram_of(raw, value, rinv, classes):
+    ybar = jnp.sum(raw, axis=0, keepdims=True) * (1.0 / raw.shape[0])
+    pert = raw - ybar
+    innov = value - ybar
+    scaled = pert * (rinv * loc_weights(classes))
+    return product(scaled, pert, turned=True), jnp.sum(scaled * innov, axis=1, keepdims=True)
+
+
+def own_kernel(raw_ref, obs_ref, class_ref, gram_ref, drive_ref):
+    gram, drive = gram_of(raw_ref[...].astype(jnp.float32), obs_ref[0:1, :], obs_ref[1:2, :], class_ref[0:1, :])
+    gram_ref[...] = gram
+    drive_ref[...] = jnp.broadcast_to(drive, gram.shape)
+
+
+def own_gram(raw, obs, classes):
+    members = raw.shape[0]
+    return pl.pallas_call(
+        own_kernel,
+        out_shape=[jax.ShapeDtypeStruct((members, members), jnp.float32)] * 2,
+        compiler_params=params(),
+        cost_estimate=cost(2),
+        name="own",
+    )(raw, obs, classes)
+
+
+ROWS_INNER = (2, 3, 4, 5)
+ROWS_OUTER = (0, 1, 6, 7)
+ROWS = 8
+PAIR = 8
+
+
+def is_inner(slot):
+    return (slot >= 2) & (slot <= 5)
+
+
+def set_weights(gram, drive, mix_refs, rest_refs):
+    members = gram.shape[0]
     row = lax.broadcasted_iota(jnp.int32, (members, members), 0)
     column = lax.broadcasted_iota(jnp.int32, (members, members), 1)
     eye = jnp.where(row == column, 1.0, 0.0).astype(jnp.float32)
-    gram = (members - 1.0) * eye
-    drive = jnp.zeros((members, 1), jnp.float32)
-    for index, raw_ref in enumerate((own_ref, south_ref, north_ref)):
-        raw = raw_ref[...].astype(jnp.float32)
-        ybar = jnp.sum(raw, axis=0, keepdims=True) * (1.0 / members)
-        pert = raw - ybar
-        innov = obs_ref[index, 0:1, :] - ybar
-        rloc = obs_ref[index, 1:2, :] * loc_weights(class_ref[index : index + 1, :])
-        scaled = pert * rloc
-        gram = gram + lax.dot_general(
-            scaled,
-            pert,
-            (((1,), (1,)), ((), ())),
-            precision=lax.Precision.HIGHEST,
-            preferred_element_type=jnp.float32,
-        )
-        drive = drive + jnp.sum(scaled * innov, axis=1, keepdims=True)
+    gram = gram + (members - 1.0) * eye
     norm = jnp.sqrt(jnp.sum(jnp.sum(gram * gram, axis=1, keepdims=True), axis=0, keepdims=True))
     upper = gram / norm
     lower = eye
     for sweep in range(ITERS):
-        factor = 1.5 * eye - 0.5 * dot(lower, upper)
+        factor = 1.5 * eye - 0.5 * (upper if sweep == 0 else product(lower, upper))
         if sweep < ITERS - 1:
-            upper = dot(upper, factor)
-        lower = dot(factor, lower)
-    wide = jnp.broadcast_to(drive, (members, members))
-    wmean = dot(lower, dot(lower, wide)) / norm
+            upper = product(upper, factor)
+        lower = factor if sweep == 0 else product(factor, lower)
+    wmean = product(lower, product(lower, drive)) / norm
     weights = (jnp.sqrt((members - 1.0) / norm) * lower + wmean).astype(jnp.bfloat16).astype(jnp.float32)
-    turned = weights.T
-    rest = 1.0 - jnp.sum(turned, axis=1, keepdims=True)
-    rows = 8
-    rest_ref[...] = jnp.broadcast_to(rest[:, :, None], (members, rows, LANES)).reshape(members * rows, LANES)
-    spread = jnp.broadcast_to(turned[:, None, :], (members, rows, members)).reshape(members * rows, members)
-    held = lax.broadcasted_iota(jnp.int32, (members * rows, members), 0) % rows
-    for index, value in enumerate((2, 3, 4, 5, 0, 1, 6, 7)):
-        mix_ref[:, index * members : (index + 1) * members] = jnp.where(held == value, spread, 0.0).astype(jnp.bfloat16)
-
-
-def tile_mix(own, south, north, obs, classes):
-    members = own.shape[0]
-    return pl.pallas_call(
-        weights_kernel,
-        out_shape=[
-            jax.ShapeDtypeStruct((members * 8, members * 8), jnp.bfloat16),
-            jax.ShapeDtypeStruct((members * 8, LANES), jnp.float32),
-        ],
-        compiler_params=params(),
-        cost_estimate=cost(12),
-        name="weights",
-    )(own, south, north, obs, classes)
-
-
-def mix_kernel(mix_ref, rest_ref, inner_ref, outer_ref, out_ref):
+    turned = weights.T.astype(jnp.bfloat16)
+    shape = (members * ROWS // 2, members)
+    at = lax.broadcasted_iota(jnp.int32, shape, 0)
+    slot = at % ROWS
+    pair = at // ROWS
+    low = (pair // PAIR) * (2 * PAIR) + pair % PAIR
+    member = lax.broadcasted_iota(jnp.int32, shape, 1)
+
+    def spread(which):
+        chosen = jnp.where(member == which, 1.0, 0.0).astype(jnp.bfloat16)
+        return jnp.dot(chosen, turned, preferred_element_type=jnp.float32)
+
+    first, second = spread(low), spread(low + PAIR)
+    for index, value in enumerate((first, second)):
+        rest = 1.0 - jnp.sum(value, axis=1, keepdims=True)
+        rest_refs[index] = jnp.broadcast_to(rest, shape).reshape(members // 2, ROWS, members)
+    for index, rows in enumerate((ROWS_INNER, ROWS_OUTER)):
+        home = is_inner(slot) if rows == ROWS_INNER else ~is_inner(slot)
+        row = jnp.where(home, slot, (slot + 4) % ROWS)
+        value = jnp.where(home, first, second)
+        for place, wanted in enumerate(rows):
+            columns = slice(place * members, (place + 1) * members)
+            mix_refs[index, :, columns] = jnp.where(row == wanted, value, 0.0).astype(jnp.bfloat16)
+
+
+def analyse_kernel(gram_ref, drive_ref, south_ref, north_ref, obs_ref, class_ref, inner_ref, outer_ref, out_ref, mix, rest):
+    @pl.when(pl.program_id(0) == 0)
+    def _():
+        gram, drive = gram_ref[...], drive_ref[...]
+        for index, raw_ref in ((1, south_ref), (2, north_ref)):
+            more, push = gram_of(
+                raw_ref[...].astype(jnp.float32),
+                obs_ref[2 * index : 2 * index + 1, :],
+                obs_ref[2 * index + 1 : 2 * index + 2, :],
+                class_ref[index : index + 1, :],
+            )
+            gram, drive = gram + more, drive + push
+        set_weights(gram, drive, mix, rest)
+
     groups, each, part = inner_ref.shape
     members = groups * each
     width = part // 4
-    inner = inner_ref[...].reshape(members, part)
-    outer_part = outer_ref[...].reshape(members, part)
-    pieces = [inner[:, i * width : (i + 1) * width] for i in range(4)]
-    pieces += [outer_part[:, i * width : (i + 1) * width] for i in range(4)]
-    stacked = jnp.concatenate(pieces, axis=0)
-    rows = 8
-    at = lax.broadcasted_iota(jnp.int32, (rows, members * rows), 0)
-    slot = lax.broadcasted_iota(jnp.int32, (rows, members * rows), 1) // members
-    source = jnp.zeros((rows, members * rows), jnp.int32)
-    for index, value in enumerate((2, 3, 4, 5, 0, 1, 6, 7)):
-        source = jnp.where(slot == index, value, source)
-    ones = jnp.where(at == source, 1.0, 0.0).astype(jnp.bfloat16)
-    mean = jnp.dot(ones, stacked, preferred_element_type=jnp.float32) * (1.0 / members)
-    mixed = jnp.dot(mix_ref[...], stacked, preferred_element_type=jnp.float32)
+    at = lax.broadcasted_iota(jnp.int32, (ROWS, members * 4), 0)
+    slot = lax.broadcasted_iota(jnp.int32, (ROWS, members * 4), 1) // members
+    mean = jnp.zeros((ROWS, width), jnp.float32)
+    mixed = []
+    for index, (part_ref, rows) in enumerate(((inner_ref, ROWS_INNER), (outer_ref, ROWS_OUTER))):
+        flat = part_ref[...].reshape(members, part)
+        stacked = jnp.concatenate([flat[:, i * width : (i + 1) * width] for i in range(4)], axis=0)
+        source = jnp.zeros(at.shape, jnp.int32)
+        for place, value in enumerate(rows):
+            source = jnp.where(slot == place, value, source)
+        ones = jnp.where(at == source, 1.0, 0.0).astype(jnp.bfloat16)
+        mean = mean + jnp.dot(ones, stacked, preferred_element_type=jnp.float32)
+        mixed.append(jnp.dot(mix[index], stacked, preferred_element_type=jnp.float32))
+    mean = mean * (1.0 / members)
+    shape = (members // 2, ROWS, LANES)
+    home = is_inner(lax.broadcasted_iota(jnp.int32, shape, 1))
     for index in range(width // LANES):
         lanes = slice(index * LANES, (index + 1) * LANES)
-        rest = rest_ref[...].reshape(members, rows, LANES)
-        made = mixed[:, lanes].reshape(members, rows, LANES) + mean[None, :, lanes] * rest
-        out_ref[:, :, 0, :, lanes] = made.reshape(groups, each, rows, LANES).astype(jnp.bfloat16)
-
-
-def analyse(mix, rest, inner, outer_part, levels, width):
+        inner, outside = (value[:, lanes].reshape(shape) for value in mixed)
+        low = jnp.where(home, inner, outside) + mean[None, :, lanes] * rest[0]
+        high = pltpu.roll(jnp.where(home, outside, inner), 4, 1) + mean[None, :, lanes] * rest[1]
+        half = (groups, PAIR, ROWS, LANES)
+        out_ref[:, 0:PAIR, 0, :, lanes] = low.reshape(half).astype(jnp.bfloat16)
+        out_ref[:, PAIR : 2 * PAIR, 0, :, lanes] = high.reshape(half).astype(jnp.bfloat16)
+
+
+def analyse(gram, drive, south, north, obs, classes, inner, outer_part, levels, width):
     groups, each, _ = inner.shape
+    members = groups * each
     half = pl.BlockSpec((groups, each, 4 * width), lambda i: (0, 0, i))
-    return pl.pallas_call(
-        mix_kernel,
+    small = [gram, drive, south, north, obs, classes]
+    return pl.pallas_call(
+        analyse_kernel,
         grid=(levels,),
-        in_specs=[
-            pl.BlockSpec(mix.shape, lambda i: (0, 0)),
-            pl.BlockSpec(rest.shape, lambda i: (0, 0)),
-            half,
-            half,
-        ],
+        in_specs=[pl.BlockSpec(a.shape, lambda i: (0, 0)) for a in small] + [half, half],
         out_specs=pl.BlockSpec((groups, each, 1, 8, width), lambda i: (0, 0, i, 0, 0)),
         out_shape=jax.ShapeDtypeStruct((groups, each, levels, 8, width), jnp.bfloat16),
-        compiler_params=params(60 * 1024 * 1024),
-        cost_estimate=cost(6),
+        scratch_shapes=[
+            pltpu.VMEM((2, members * ROWS // 2, members * 4), jnp.bfloat16),
+            pltpu.VMEM((2, members // 2, ROWS, members), jnp.float32),
+        ],
+        compiler_params=params(59 * 1024 * 1024),
+        cost_estimate=cost(12),
         name="analyse",
-    )(mix, rest, inner, outer_part)
+    )(*small, inner, outer_part)
 
 
 def to_neighbours(low, high):
@@ -353,23 +414,6 @@
     return lax.ppermute(high, "space", up), lax.ppermute(low, "space", down)
 
 
-def partner(value, bit):
-    devices = lax.axis_size("member")
-    return lax.ppermute(value, "member", [(i, i ^ bit) for i in range(devices)])
-
-
-def gather_members(value):
-    devices = lax.axis_size("member")
-    here = lax.axis_index("member")
-    group = devices // 2
-    held = jnp.stack([value] + [partner(value, bit) for bit in range(1, group)])
-    inside = here % group
-    held = jnp.stack([lax.dynamic_index_in_dim(held, inside ^ i, 0, keepdims=False) for i in range(group)])
-    other = partner(held, group)
-    own_first = here < group
-    return jnp.concatenate([jnp.where(own_first, held, other), jnp.where(own_first, other, held)])
-
-
 def all_to_all(blocks):
     return lax.all_to_all(blocks, "member", split_axis=0, concat_axis=0, tiled=True)
 
@@ -378,17 +422,9 @@
     members, tiles, levels, rows, width = state.shape
     slots = obs_col.shape[2]
 
-    columns = gather_members(obs_col[0, 0])
-    row = (columns // width) % rows
-    inside = (row >= 2) & (row < rows - 2)
-    kept = jnp.where(inside, row - 2, jnp.where(row < 2, row, row - 4))
-    offset = (columns // (rows * width)) * (4 * width) + kept * width + columns % width
-    place = offset // LANES + jnp.where(inside, 0, levels * 4 * width // LANES)
-    lane = offset % LANES
-
     inner = interior(state, wind_east, wind_north)
-    inner, place, lane, state, wind_east, wind_north, obs_val, obs_rinv = lax.optimization_barrier(
-        (inner, place, lane, state, wind_east, wind_north, obs_val, obs_rinv)
+    inner, state, wind_east, wind_north, obs_val, obs_rinv = lax.optimization_barrier(
+        (inner, state, wind_east, wind_north, obs_val, obs_rinv)
     )
     inner_tile = all_to_all(inner)
 
@@ -401,16 +437,22 @@
     obs = jnp.stack([obs_val[0, 0], jnp.where(live, obs_rinv[0, 0], jnp.float32(0.0))])
     obs_south, obs_north = to_neighbours(obs, obs)
     outside = outer(state, wind_east, wind_north, below, above, wind_below, wind_above)
-    picked = pick(place[:, None], lane[:, None], inner, outside)
-
-    picked, inner_tile = lax.optimization_barrier((picked, inner_tile))
-    raw = all_to_all(picked)
-    outside, raw = lax.optimization_barrier((outside, raw))
+
+    columns = obs_col[0]
+    row = (columns // width) % rows
+    inside = (row >= 2) & (row < rows - 2)
+    kept = jnp.where(inside, row - 2, jnp.where(row < 2, row, row - 4))
+    offset = (columns // (rows * width)) * (4 * width) + kept * width + columns % width
+    place, lane = offset // LANES, offset % LANES
+
+    outside, obs_south, obs_north, inner_tile = lax.optimization_barrier((outside, obs_south, obs_north, inner_tile))
     outer_tile = all_to_all(outside)
-    raw = raw.reshape(tiles * members, slots)
+    raw = pick(jnp.where(inside, place, -1), lane, inner_tile)
+    raw = pick(jnp.where(inside, -1, place), lane, outer_tile, raw)
     south, north = to_neighbours(raw, raw)
-    mix, rest = tile_mix(raw, south, north, jnp.stack([obs, obs_south, obs_north]), loc_class[0, 0])
-    updated = analyse(mix, rest, inner_tile, outer_tile, levels, width)
+    gram, drive = own_gram(raw, obs, loc_class[0, 0])
+    all_obs = jnp.concatenate([obs, obs_south, obs_north])
+    updated = analyse(gram, drive, south, north, all_obs, loc_class[0, 0], inner_tile, outer_tile, levels, width)
     final = all_to_all(updated)
     return jnp.swapaxes(final, 0, 1)
 

time: 255 us -> 251 us (0.984)
  blocking collectives: 112 us -> 100 us
  waiting for transfers between devices: 55.8 us -> 59.8 us
    all_to_all x2, waiting for transfers between devices: 41.9 us -> 54.1 us  [all_to_all(): lax.all_to_all(blocks, 'member', split_axis=0, concat_axis=0, tiled=True)]
    all_to_all x2 -> x1, blocking collectives: 112 us -> 100 us  [all_to_all(): lax.all_to_all(blocks, 'member', split_axis=0, concat_axis=0, tiled=True)]
    ppermute x4 -> x0, starting transfers between devices: 9.77 us -> none  [partner(): return lax.ppermute(value, 'member', [(i, i ^ bit) for i in range(devices)])]
    all_to_all x2, starting transfers between devices: 8.1 us -> 12.9 us  [all_to_all(): lax.all_to_all(blocks, 'member', split_axis=0, concat_axis=0, tiled=True)]
    ppermute x4 -> x0, waiting for transfers between devices: 4.13 us -> none  [partner(): return lax.ppermute(value, 'member', [(i, i ^ bit) for i in range(devices)])]
    ppermute x8, waiting for transfers between devices: 9.67 us -> 5.73 us  [to_neighbours(): return (lax.ppermute(high, 'space', up), lax.ppermute(low, 'space', down))]
    ppermute x8, starting transfers between devices: 20.2 us -> 23.4 us  [to_neighbours(): return (lax.ppermute(high, 'space', up), lax.ppermute(low, 'space', down))]
    pallas_call x3 -> x4, Pallas kernels: 21.8 us -> 23.4 us  [the longest x2 12.4 us: pick(): pl.pallas_call(functools.partial(pick_kernel, steps), grid=(steps,), in_s...]
  transfers between devices with their start and end apart: 14 -> 10, of which waited for: 6 -> 4; matrix products, arithmetic and copies ran while one was open for 0% -> 1% of each run, Pallas kernels for 12% -> 7%
where the time goes in v3:
time: 251 us; the launch traced here: 249 us
  blocking collectives  100 us (40%)
  waiting for transfers between devices  59.8 us (24%)
  Pallas kernels  42.5 us (17%)
  starting transfers between devices  36.4 us (15%)
  local copies, waits for them, and re-layouts  7.04 us (3%)
    all_to_all x1, blocking collectives, all_to_all(): lax.all_to_all(blocks, 'member', split_axis=0, concat_axis=0, tiled=True)  100 us
    all_to_all x2, waiting for transfers between devices, all_to_all(): lax.all_to_all(blocks, 'member', split_axis=0, concat_axis=0, tiled=True)  54.1 us
    ppermute x8, starting transfers between devices, to_neighbours(): return (lax.ppermute(high, 'space', up), lax.ppermute(low, 'space', down))  23.4 us
    all_to_all x2, starting transfers between devices, all_to_all(): lax.all_to_all(blocks, 'member', split_axis=0, concat_axis=0, tiled=True)  12.9 us
    pallas_call x2, Pallas kernels, pick(): pl.pallas_call(functools.partial(pick_kernel, steps), grid=(steps,), in_s...  12.4 us
    pallas_call x1, Pallas kernels, analyse(): pl.pallas_call(analyse_kernel, grid=(levels,), in_specs=[pl.BlockSpec(a.s...  10.6 us
    pallas_call x1, Pallas kernels, outer(): pl.pallas_call(outer_kernel, grid=(levels,), in_specs=[pl.BlockSpec((memb...  8.5 us
    pallas_call x1, Pallas kernels, interior(): pl.pallas_call(interior_kernel, grid=(levels,), in_specs=[pl.BlockSpec((m...  7.11 us
  transfers between devices with their start and end apart: 10, of which 4 were waited for; matrix products, arithmetic and copies ran while one was open for 1% of the time, Pallas kernels for 7%

profile of v3, /device:TPU:14, one launch (start us, length us, event | category | flops | bytes accessed | tf_op | source)
XLA Modules:
  0.0 248.9 jit_solution(1470625366599622658)
XLA Ops:
  0.0 7.1 %interior.1 = bf16[8,16,8192]{2,1,0:T(8,128)(2,1)} custom-call(bf16[16,8,4,8,512]{4,3,2,1,0:T(8,128)(2,1)} %state_ref.3, f32[8,4,8,512]{3,2,1,0:T(8,128)} %east_ref.2, f32[8,4,8,512]{3,2,1,0:T(8,128)} %north_ref.2), custom_call_target="tpu_custom_call" | custom-call | bytes 28800000 | tf_op jit(solution)/shard_map/interior/pallas_call | solution.py:121
  7.1 8.6 %all-to-all-start = ((bf16[8,16,8192]{2,1,0:T(8,128)(2,1)}), bf16[8,16,8192]{2,1,0:T(8,128)(2,1)S(1)}, u32[]{:S(2)}, u32[]{:S(2)}) async-start(bf16[8,16,8192]{2,1,0:T(8,128)(2,1)} %interior.1), calls=%async_computation | async-start | bytes 4194304 | tf_op jit(solution)/shard_map/all_to_all | solution.py:418
  15.7 3.5 %edges.1 = (bf16[4,2,16,4096]{3,2,1,0:T(8,128)(2,1)S(1)}, bf16[4,2,16,4096]{3,2,1,0:T(8,128)(2,1)S(1)}) custom-call(bf16[16,8,4,8,512]{4,3,2,1,0:T(8,128)(2,1)} %state_ref.3), custom_call_target="tpu_custom_call" | custom-call | bytes 10800000 | tf_op jit(solution)/shard_map/edges/pallas_call | solution.py:56
  19.2 1.9 collective-permute-start
  21.2 3.6 %collective-permute-start.1 = (bf16[4,2,16,4096]{3,2,1,0:T(8,128)(2,1)S(1)}, bf16[4,2,16,4096]{3,2,1,0:T(8,128)(2,1)}, u32[]{:S(2)}, u32[]{:S(2)}) collective-permute-start(bf16[4,2,16,4096]{3,2,1,0:T(8,128)(2,1)S(1)} %get-tuple-element.23), channel_id=1, source_target_pairs={{1,0},{2,1},{3,2},{4,3},{5,4},{6,5},{7,6},{8,7},{9,8},{10,9},{11,1... | collective-permute-start | bytes 3145736 | tf_op jit(solution)/shard_map/ppermute | solution.py:414
  25.5 1.9 collective-permute-start.3
  27.5 2.4 collective-permute-start.2
  30.6 3.2 %collective-permute-start.5 = (f32[2,512]{1,0:T(2,128)S(1)}, f32[2,512]{1,0:T(2,128)S(1)}, u32[]{:S(2)}, u32[]{:S(2)}) collective-permute-start(f32[2,512]{1,0:T(2,128)S(1)} %pad_maximum_fusion.1.obs_ref), channel_id=1, source_target_pairs={{1,0},{2,1},{3,2},{4,3},{5,4},{6,5},{7,6},{8,7},{9,8},{10,9},{11,1... | collective-permute-start | bytes 12296 | tf_op jit(solution)/shard_map/ppermute | solution.py:414
  33.7 4.8 %collective-permute-done.3.wind_above_ref = f32[2,4,8,512]{3,2,1,0:T(8,128)S(1)} collective-permute-done((f32[2,4,8,512]{3,2,1,0:T(8,128)S(1)}, f32[2,4,8,512]{3,2,1,0:T(8,128)S(1)}, u32[]{:S(2)}, u32[]{:S(2)}) %collective-permute-start.3) | collective-permute-done | bytes 131104 | tf_op jit(solution)/shard_map/ppermute | solution.py:414
  38.5 6.1 %collective-permute-start.4 = (f32[2,512]{1,0:T(2,128)S(1)}, f32[2,512]{1,0:T(2,128)S(1)}, u32[]{:S(2)}, u32[]{:S(2)}) collective-permute-start(f32[2,512]{1,0:T(2,128)S(1)} %pad_maximum_fusion.1.obs_ref), channel_id=1, source_target_pairs={{0,1},{1,2},{2,3},{3,4},{4,5},{5,6},{6,7},{7,8},{8,9},{9,10},{10,1... | collective-permute-start | bytes 12296 | tf_op jit(solution)/shard_map/ppermute | solution.py:414
  44.6 1.0 copy-done.7
  45.7 8.5 %outer.1 = bf16[8,16,8192]{2,1,0:T(8,128)(2,1)} custom-call(bf16[16,8,4,8,512]{4,3,2,1,0:T(8,128)(2,1)} %state_ref.3, f32[8,4,8,512]{3,2,1,0:T(8,128)} %east_ref.2, f32[8,4,8,512]{3,2,1,0:T(8,128)} %north_ref.2, bf16[4,2,16,4096]{3,2,1,0:T(8,128)(2,1)} %copy-done.7, bf16[4,2,16,4096]{3,2,1,0:T(8,128)(2,1)} %collective-permute-done.1.above_ref, ...), custom_call_target="tpu_custom_call" | custom-call | bytes 32400000 | tf_op jit(solution)/shard_map/outer/pallas_call | solution.py:177
  54.2 12.7 %all-to-all-done.part_ref.inner_ref = bf16[8,16,8192]{2,1,0:T(8,128)(2,1)S(1)} async-done(((bf16[8,16,8192]{2,1,0:T(8,128)(2,1)}), bf16[8,16,8192]{2,1,0:T(8,128)(2,1)S(1)}, u32[]{:S(2)}, u32[]{:S(2)}) %all-to-all-start) | async-done | bytes 2097184 | tf_op jit(solution)/shard_map/all_to_all | solution.py:418
  66.9 4.3 %all-to-all-start.1 = ((bf16[8,16,8192]{2,1,0:T(8,128)(2,1)}), bf16[8,16,8192]{2,1,0:T(8,128)(2,1)}, u32[]{:S(2)}, u32[]{:S(2)}) async-start(bf16[8,16,8192]{2,1,0:T(8,128)(2,1)} %outer.1), calls=%async_computation.1 | async-start | bytes 4194304 | tf_op jit(solution)/shard_map/all_to_all | solution.py:418
  72.5 6.2 %pick.2.refs_0_ = bf16[128,512]{1,0:T(8,128)(2,1)} custom-call(s32[1,512]{1,0:T(1,128)} %get-tuple-element.33.place_ref, s32[1,512]{1,0:T(1,128)} %get-tuple-element.44.lane_ref, bf16[8,16,8192]{2,1,0:T(8,128)(2,1)} %copy-done.4), custom_call_target="tpu_custom_call" | custom-call | bytes 14400000 | tf_op jit(solution)/shard_map/pick/pallas_call | solution.py:236
  78.7 41.3 %all-to-all-done.1.part_ref.outer_ref = bf16[8,16,8192]{2,1,0:T(8,128)(2,1)} async-done(((bf16[8,16,8192]{2,1,0:T(8,128)(2,1)}), bf16[8,16,8192]{2,1,0:T(8,128)(2,1)}, u32[]{:S(2)}, u32[]{:S(2)}) %all-to-all-start.1) | async-done | bytes 2097184 | tf_op jit(solution)/shard_map/all_to_all | solution.py:418
  120.1 6.2 %pick.3.raw_ref = bf16[128,512]{1,0:T(8,128)(2,1)} custom-call(s32[1,512]{1,0:T(1,128)} %get-tuple-element.45.place_ref, s32[1,512]{1,0:T(1,128)} %get-tuple-element.44.lane_ref, bf16[8,16,8192]{2,1,0:T(8,128)(2,1)} %all-to-all-done.1.part_ref.outer_ref, bf16[128,512]{1,0:T(8,128)(2,1)} %pick.2.refs_0_), custom_call_target="tpu_custom_call" | custom-call | bytes 14400000 | tf_op jit(solution)/shard_map/pick/pallas_call | solution.py:236
  126.3 1.9 collective-permute-start.7
  128.2 2.4 collective-permute-start.6
  131.3 0.9 copy-done
  133.8 0.9 collective-permute-done.6.south_ref
  135.4 10.6 %analyse.1 = bf16[8,16,4,8,512]{4,3,2,1,0:T(8,128)(2,1)} custom-call(f32[128,128]{1,0:T(8,128)} %copy-done.2, f32[128,128]{1,0:T(8,128)} %copy-done.3, bf16[128,512]{1,0:T(8,128)(2,1)} %copy-done.11, bf16[128,512]{1,0:T(8,128)(2,1)} %copy-done.10, f32[6,512]{1,0:T(8,128)} %pad_maximum_fusion.obs_ref, s32[3,512]{1,0:T(4,128)} %bitcast.41, ...), custom_call_target="tpu_custom_call" | custom-call | bytes 43200000 | tf_op jit(solution)/shard_map/analyse/pallas_call | solution.py:394
  146.0 100.4 %all_to_all.15 = bf16[8,16,4,8,512]{4,3,2,1,0:T(8,128)(2,1)S(1)} all-to-all(bf16[8,16,4,8,512]{4,3,2,1,0:T(8,128)(2,1)} %analyse.1), channel_id=1, replica_groups=mesh['member'=8,'space'=32] {'member'}, dimensions={0} | all-to-all | bytes 8388608 | tf_op jit(solution)/shard_map/all_to_all | solution.py:418
  246.4 2.5 %copy.13 = bf16[16,8,4,8,512]{4,3,2,1,0:T(8,128)(2,1)} copy(bf16[16,8,4,8,512]{4,3,2,0,1:T(8,128)(2,1)S(1)} %bitcast.42) | data formatting | bytes 8388608 | tf_op jit(solution)/shard_map/transpose | solution.py:457
  (49 shorter events, 4.8 us)
Async XLA Ops:
  7.1 17.7 %copy-start.5 = (f32[8,4,8,512]{3,2,1,0:T(8,128)S(1)}, f32[8,4,8,512]{3,2,1,0:T(8,128)}, u32[]{:S(2)}) copy-start(f32[8,4,8,512]{3,2,1,0:T(8,128)} %east_ref.2) | copy-start | bytes 1572868
  7.1 18.0 %copy-start.6 = (f32[8,4,8,512]{3,2,1,0:T(8,128)S(1)}, f32[8,4,8,512]{3,2,1,0:T(8,128)}, u32[]{:S(2)}) copy-start(f32[8,4,8,512]{3,2,1,0:T(8,128)} %north_ref.2) | copy-start | bytes 1572868
  7.1 59.8 %all-to-all-start = ((bf16[8,16,8192]{2,1,0:T(8,128)(2,1)}), bf16[8,16,8192]{2,1,0:T(8,128)(2,1)S(1)}, u32[]{:S(2)}, u32[]{:S(2)}) async-start(bf16[8,16,8192]{2,1,0:T(8,128)(2,1)} %interior.1), calls=%async_computation | async-start | bytes 4194304 | tf_op jit(solution)/shard_map/all_to_all | solution.py:418
  15.7 14.8 %copy-start.15 = (f32[1,1,512]{2,1,0:T(1,128)S(1)}, f32[1,1,512]{2,1,0:T(1,128)}, u32[]{:S(2)}) copy-start(f32[1,1,512]{2,1,0:T(1,128)} %param.13) | copy-start | bytes 6148
  15.7 14.8 %copy-start.12 = (f32[1,1,512]{2,1,0:T(1,128)S(1)}, f32[1,1,512]{2,1,0:T(1,128)}, u32[]{:S(2)}) copy-start(f32[1,1,512]{2,1,0:T(1,128)} %param.12) | copy-start | bytes 6148
  19.2 25.4 %collective-permute-start = (bf16[4,2,16,4096]{3,2,1,0:T(8,128)(2,1)S(1)}, bf16[4,2,16,4096]{3,2,1,0:T(8,128)(2,1)S(1)}, u32[]{:S(2)}, u32[]{:S(2)}) collective-permute-start(bf16[4,2,16,4096]{3,2,1,0:T(8,128)(2,1)S(1)} %get-tuple-element.22), channel_id=1, source_target_pairs={{0,1},{1,2},{2,3},{3,4},{4,5},{5,6},{6,7},{7,8},{8,9},{9,10},{10,1... | collective-permute-start | bytes 3145736 | tf_op jit(solution)/shard_map/ppermute | solution.py:414
  21.2 24.5 %collective-permute-start.1 = (bf16[4,2,16,4096]{3,2,1,0:T(8,128)(2,1)S(1)}, bf16[4,2,16,4096]{3,2,1,0:T(8,128)(2,1)}, u32[]{:S(2)}, u32[]{:S(2)}) collective-permute-start(bf16[4,2,16,4096]{3,2,1,0:T(8,128)(2,1)S(1)} %get-tuple-element.23), channel_id=1, source_target_pairs={{1,0},{2,1},{3,2},{4,3},{5,4},{6,5},{7,6},{8,7},{9,8},{10,9},{11,1... | collective-permute-start | bytes 3145736 | tf_op jit(solution)/shard_map/ppermute | solution.py:414
  25.5 13.0 %collective-permute-start.3 = (f32[2,4,8,512]{3,2,1,0:T(8,128)S(1)}, f32[2,4,8,512]{3,2,1,0:T(8,128)S(1)}, u32[]{:S(2)}, u32[]{:S(2)}) collective-permute-start(f32[2,4,8,512]{3,2,1,0:T(8,128)S(1)} %get-tuple-element.42), channel_id=1, source_target_pairs={{1,0},{2,1},{3,2},{4,3},{5,4},{6,5},{7,6},{8,7},{9,8},{10,9},{11,1... | collective-permute-start | bytes 393224 | tf_op jit(solution)/shard_map/ppermute | solution.py:414
  27.5 17.1 %collective-permute-start.2 = (f32[2,4,8,512]{3,2,1,0:T(8,128)S(1)}, f32[2,4,8,512]{3,2,1,0:T(8,128)S(1)}, u32[]{:S(2)}, u32[]{:S(2)}) collective-permute-start(f32[2,4,8,512]{3,2,1,0:T(8,128)S(1)} %get-tuple-element.43), channel_id=1, source_target_pairs={{0,1},{1,2},{2,3},{3,4},{4,5},{5,6},{6,7},{7,8},{8,9},{9,10},{10,1... | collective-permute-start | bytes 393224 | tf_op jit(solution)/shard_map/ppermute | solution.py:414
  30.6 23.6 %collective-permute-start.5 = (f32[2,512]{1,0:T(2,128)S(1)}, f32[2,512]{1,0:T(2,128)S(1)}, u32[]{:S(2)}, u32[]{:S(2)}) collective-permute-start(f32[2,512]{1,0:T(2,128)S(1)} %pad_maximum_fusion.1.obs_ref), channel_id=1, source_target_pairs={{1,0},{2,1},{3,2},{4,3},{5,4},{6,5},{7,6},{8,7},{9,8},{10,9},{11,1... | collective-permute-start | bytes 12296 | tf_op jit(solution)/shard_map/ppermute | solution.py:414
  38.5 7.1 %copy-start.8 = (f32[2,4,8,512]{3,2,1,0:T(8,128)}, f32[2,4,8,512]{3,2,1,0:T(8,128)S(1)}, u32[]{:S(2)}) copy-start(f32[2,4,8,512]{3,2,1,0:T(8,128)S(1)} %collective-permute-done.3.wind_above_ref) | copy-start | bytes 393220
  38.5 15.7 %collective-permute-start.4 = (f32[2,512]{1,0:T(2,128)S(1)}, f32[2,512]{1,0:T(2,128)S(1)}, u32[]{:S(2)}, u32[]{:S(2)}) collective-permute-start(f32[2,512]{1,0:T(2,128)S(1)} %pad_maximum_fusion.1.obs_ref), channel_id=1, source_target_pairs={{0,1},{1,2},{2,3},{3,4},{4,5},{5,6},{6,7},{7,8},{8,9},{9,10},{10,1... | collective-permute-start | bytes 12296 | tf_op jit(solution)/shard_map/ppermute | solution.py:414
  44.6 1.1 copy-start.9
  44.6 1.0 copy-start.7
  54.2 17.1 %copy-start.14 = (s32[1,1,512]{2,1,0:T(1,128)S(1)}, s32[1,1,512]{2,1,0:T(1,128)}, u32[]{:S(2)}) copy-start(s32[1,1,512]{2,1,0:T(1,128)} %param.11) | copy-start | bytes 6148
  54.2 76.5 %copy-start.13 = (s32[1,1,3,512]{3,1,2,0:T(1,128)S(1)}, s32[1,1,3,512]{3,1,2,0:T(1,128)}, u32[]{:S(2)}) copy-start(s32[1,1,3,512]{3,1,2,0:T(1,128)} %param.15) | copy-start | bytes 18436
  66.9 5.6 %copy-start.4 = (bf16[8,16,8192]{2,1,0:T(8,128)(2,1)}, bf16[8,16,8192]{2,1,0:T(8,128)(2,1)S(1)}, u32[]{:S(2)}) copy-start(bf16[8,16,8192]{2,1,0:T(8,128)(2,1)S(1)} %all-to-all-done.part_ref.inner_ref) | copy-start | bytes 6291460
  66.9 53.1 %all-to-all-start.1 = ((bf16[8,16,8192]{2,1,0:T(8,128)(2,1)}), bf16[8,16,8192]{2,1,0:T(8,128)(2,1)}, u32[]{:S(2)}, u32[]{:S(2)}) async-start(bf16[8,16,8192]{2,1,0:T(8,128)(2,1)} %outer.1), calls=%async_computation.1 | async-start | bytes 4194304 | tf_op jit(solution)/shard_map/all_to_all | solution.py:418
  126.3 7.5 %collective-permute-start.7 = (bf16[128,512]{1,0:T(8,128)(2,1)}, bf16[128,512]{1,0:T(8,128)(2,1)S(1)}, u32[]{:S(2)}, u32[]{:S(2)}) collective-permute-start(bf16[128,512]{1,0:T(8,128)(2,1)} %pick.3.raw_ref), channel_id=1, source_target_pairs={{1,0},{2,1},{3,2},{4,3},{5,4},{6,5},{7,6},{8,7},{9,8},{10,9},{11,1... | collective-permute-start | bytes 393224 | tf_op jit(solution)/shard_map/ppermute | solution.py:414
  128.2 6.5 %collective-permute-start.6 = (bf16[128,512]{1,0:T(8,128)(2,1)}, bf16[128,512]{1,0:T(8,128)(2,1)S(1)}, u32[]{:S(2)}, u32[]{:S(2)}) collective-permute-start(bf16[128,512]{1,0:T(8,128)(2,1)} %pick.3.raw_ref), channel_id=1, source_target_pairs={{0,1},{1,2},{2,3},{3,4},{4,5},{5,6},{6,7},{7,8},{8,9},{9,10},{10,1... | collective-permute-start | bytes 393224 | tf_op jit(solution)/shard_map/ppermute | solution.py:414
  130.7 4.1 %copy-start.1 = (s32[1,1,3,512]{3,2,1,0:T(4,128)}, s32[1,1,3,512]{3,2,1,0:T(4,128)S(1)}, u32[]{:S(2)}) copy-start(s32[1,1,3,512]{3,2,1,0:T(4,128)S(1)} %copy.16) | copy-start | bytes 18436
  131.3 0.9 copy-start
  133.8 1.0 copy-start.10
  134.7 0.7 copy-start.11
  (2 other events, 1.3 us)

commit v4 on v3

--- a/solution.py
+++ b/solution.py
@@ -9,7 +9,8 @@
 
 ITERS = 6
 LANES = 128
-VMEM_LIMIT = 48 * 1024 * 1024
+VMEM_LIMIT = 20 * 1024 * 1024
+LEAVE_ROOM = 20 * 1024 * 1024
 
 
 def params(limit=VMEM_LIMIT):
@@ -193,55 +194,45 @@
             pltpu.VMEM((rows + 4, members, LANES + tiles * width), jnp.float32),
             pltpu.VMEM((4, tiles, rows + 4, width), jnp.float32),
         ],
-        compiler_params=params(60 * 1024 * 1024),
+        compiler_params=params(),
         cost_estimate=cost(9),
         name="outer",
     )(state, wind_east, wind_north, below, above, wind_below, wind_above)
 
 
-def pick_kernel(steps, place_ref, lane_ref, part_ref, *refs):
-    before_ref, raw_ref, total = refs if len(refs) == 3 else (None, *refs)
+def pick_kernel(span, place_ref, lane_ref, part_ref, *refs):
+    before_ref, raw_ref = refs if len(refs) == 2 else (None, *refs)
     groups, each, length = part_ref.shape
-    members, slots = raw_ref.shape
-    step = pl.program_id(0)
-    at_lane = lax.broadcasted_iota(jnp.int32, (LANES, slots), 0)
-
-    @pl.when(step == 0)
-    def _():
-        if before_ref is None:
-            total[...] = jnp.zeros(total.shape, jnp.float32)
-        else:
-            total[...] = before_ref[...].astype(jnp.float32)
-
-    here = place_ref[...] - step * (length // LANES)
-    pieces = []
-    for piece in range(length // LANES):
-        wanted = jnp.where(here == piece, lane_ref[...], -1)
-        pieces.append(jnp.where(at_lane == wanted, 1.0, 0.0).astype(jnp.bfloat16))
-    flat = part_ref[...].reshape(members, length)
-    total[...] += jnp.dot(flat, jnp.concatenate(pieces, axis=0), preferred_element_type=jnp.float32)
-
-    @pl.when(step == steps - 1)
-    def _():
-        raw_ref[...] = total[...].astype(jnp.bfloat16)
-
-
-def pick(place, lane, part, before=None):
+    slots = raw_ref.shape[1]
+    at_lane = lax.broadcasted_iota(jnp.int32, (span, slots), 0)
+    chosen = jnp.where(at_lane == lane_ref[...], 1.0, 0.0).astype(jnp.bfloat16)
+    place = jnp.broadcast_to(place_ref[...], (each, slots))
+    together = LANES // each
+    for group in range(groups):
+        members = slice(group * each, (group + 1) * each)
+        total = jnp.zeros((each, slots), jnp.float32) if before_ref is None else before_ref[members].astype(jnp.float32)
+        for first in range(0, length // span, together):
+            pieces = [part_ref[group, :, (first + i) * span : (first + i + 1) * span] for i in range(together)]
+            found = jnp.dot(jnp.concatenate(pieces, axis=0), chosen, preferred_element_type=jnp.float32)
+            for i in range(together):
+                total = jnp.where(place == first + i, found[i * each : (i + 1) * each], total)
+        raw_ref[members] = total.astype(jnp.bfloat16)
+
+
+def pick(place, lane, part, span, before=None):
     groups, each, length = part.shape
     slots = place.shape[1]
-    members = groups * each
-    steps = 8
+    steps = 2
     row = pl.BlockSpec((1, slots), lambda i: (0, 0))
-    whole = pl.BlockSpec((members, slots), lambda i: (0, 0))
+    some = pl.BlockSpec((groups // steps * each, slots), lambda i: (i, 0))
     return pl.pallas_call(
-        functools.partial(pick_kernel, steps),
+        functools.partial(pick_kernel, span),
         grid=(steps,),
-        in_specs=[row, row, pl.BlockSpec((groups, each, length // steps), lambda i: (0, 0, i))]
-        + ([] if before is None else [whole]),
-        out_specs=whole,
-        scratch_shapes=[pltpu.VMEM((members, slots), jnp.float32)],
-        out_shape=jax.ShapeDtypeStruct((members, slots), jnp.bfloat16),
-        compiler_params=params(59 * 1024 * 1024),
+        in_specs=[row, row, pl.BlockSpec((groups // steps, each, length), lambda i: (i, 0, 0))]
+        + ([] if before is None else [some]),
+        out_specs=some,
+        out_shape=jax.ShapeDtypeStruct((groups * each, slots), jnp.bfloat16),
+        compiler_params=params(LEAVE_ROOM),
         cost_estimate=cost(4),
         name="pick",
     )(place, lane, part, *([] if before is None else [before]))
@@ -273,23 +264,6 @@
     innov = value - ybar
     scaled = pert * (rinv * loc_weights(classes))
     return product(scaled, pert, turned=True), jnp.sum(scaled * innov, axis=1, keepdims=True)
-
-
-def own_kernel(raw_ref, obs_ref, class_ref, gram_ref, drive_ref):
-    gram, drive = gram_of(raw_ref[...].astype(jnp.float32), obs_ref[0:1, :], obs_ref[1:2, :], class_ref[0:1, :])
-    gram_ref[...] = gram
-    drive_ref[...] = jnp.broadcast_to(drive, gram.shape)
-
-
-def own_gram(raw, obs, classes):
-    members = raw.shape[0]
-    return pl.pallas_call(
-        own_kernel,
-        out_shape=[jax.ShapeDtypeStruct((members, members), jnp.float32)] * 2,
-        compiler_params=params(),
-        cost_estimate=cost(2),
-        name="own",
-    )(raw, obs, classes)
 
 
 ROWS_INNER = (2, 3, 4, 5)
@@ -343,11 +317,11 @@
             mix_refs[index, :, columns] = jnp.where(row == wanted, value, 0.0).astype(jnp.bfloat16)
 
 
-def analyse_kernel(gram_ref, drive_ref, south_ref, north_ref, obs_ref, class_ref, inner_ref, outer_ref, out_ref, mix, rest):
+def analyse_kernel(own_ref, south_ref, north_ref, obs_ref, class_ref, inner_ref, outer_ref, out_ref, mix, rest):
     @pl.when(pl.program_id(0) == 0)
     def _():
-        gram, drive = gram_ref[...], drive_ref[...]
-        for index, raw_ref in ((1, south_ref), (2, north_ref)):
+        gram = drive = 0.0
+        for index, raw_ref in enumerate((own_ref, south_ref, north_ref)):
             more, push = gram_of(
                 raw_ref[...].astype(jnp.float32),
                 obs_ref[2 * index : 2 * index + 1, :],
@@ -355,7 +329,7 @@
                 class_ref[index : index + 1, :],
             )
             gram, drive = gram + more, drive + push
-        set_weights(gram, drive, mix, rest)
+        set_weights(gram, jnp.broadcast_to(drive, gram.shape), mix, rest)
 
     groups, each, part = inner_ref.shape
     members = groups * each
@@ -386,11 +360,11 @@
         out_ref[:, PAIR : 2 * PAIR, 0, :, lanes] = high.reshape(half).astype(jnp.bfloat16)
 
 
-def analyse(gram, drive, south, north, obs, classes, inner, outer_part, levels, width):
+def analyse(raw, south, north, obs, classes, inner, outer_part, levels, width):
     groups, each, _ = inner.shape
     members = groups * each
     half = pl.BlockSpec((groups, each, 4 * width), lambda i: (0, 0, i))
-    small = [gram, drive, south, north, obs, classes]
+    small = [raw, south, north, obs, classes]
     return pl.pallas_call(
         analyse_kernel,
         grid=(levels,),
@@ -401,7 +375,7 @@
             pltpu.VMEM((2, members * ROWS // 2, members * 4), jnp.bfloat16),
             pltpu.VMEM((2, members // 2, ROWS, members), jnp.float32),
         ],
-        compiler_params=params(59 * 1024 * 1024),
+        compiler_params=params(LEAVE_ROOM),
         cost_estimate=cost(12),
         name="analyse",
     )(*small, inner, outer_part)
@@ -443,16 +417,16 @@
     inside = (row >= 2) & (row < rows - 2)
     kept = jnp.where(inside, row - 2, jnp.where(row < 2, row, row - 4))
     offset = (columns // (rows * width)) * (4 * width) + kept * width + columns % width
-    place, lane = offset // LANES, offset % LANES
-
-    outside, obs_south, obs_north, inner_tile = lax.optimization_barrier((outside, obs_south, obs_north, inner_tile))
+    span = 2 * LANES
+    place, lane = offset // span, offset % span
+
+    all_obs = jnp.concatenate([obs, obs_south, obs_north])
+    outside, all_obs, inner_tile = lax.optimization_barrier((outside, all_obs, inner_tile))
     outer_tile = all_to_all(outside)
-    raw = pick(jnp.where(inside, place, -1), lane, inner_tile)
-    raw = pick(jnp.where(inside, -1, place), lane, outer_tile, raw)
+    raw = pick(jnp.where(inside, place, -1), lane, inner_tile, span)
+    raw = pick(jnp.where(inside, -1, place), lane, outer_tile, span, raw)
     south, north = to_neighbours(raw, raw)
-    gram, drive = own_gram(raw, obs, loc_class[0, 0])
-    all_obs = jnp.concatenate([obs, obs_south, obs_north])
-    updated = analyse(gram, drive, south, north, all_obs, loc_class[0, 0], inner_tile, outer_tile, levels, width)
+    updated = analyse(raw, south, north, all_obs, loc_class[0, 0], inner_tile, outer_tile, levels, width)
     final = all_to_all(updated)
     return jnp.swapaxes(final, 0, 1)
 

time: 251 us -> 242 us (0.964)
  Pallas kernels: 42.5 us -> 28.9 us
  waiting for transfers between devices: 59.8 us -> 69.8 us
    pallas_call x3 -> x2, Pallas kernels: 12.7 us -> 4.19 us  [pick(): pl.pallas_call(functools.partial(pick_kernel, span), grid=(steps,), in_sp...]
    all_to_all x2, waiting for transfers between devices: 54.1 us -> 60.4 us  [all_to_all(): lax.all_to_all(blocks, 'member', split_axis=0, concat_axis=0, tiled=True)]
    ppermute x8, waiting for transfers between devices: 5.73 us -> 9.47 us  [to_neighbours(): return (lax.ppermute(high, 'space', up), lax.ppermute(low, 'space', down))]
  transfers between devices with their start and end apart: 10 -> 10, of which waited for: 4 -> 6; matrix products, arithmetic and copies ran while one was open for 1% -> 0% of each run, Pallas kernels for 7% -> 4%
where the time goes in v4:
time: 242 us; the launch traced here: 241 us
  blocking collectives  98.2 us (41%)
  waiting for transfers between devices  69.8 us (29%)
  starting transfers between devices  36.4 us (15%)
  Pallas kernels  28.9 us (12%)
  local copies, waits for them, and re-layouts  6.69 us (3%)
    all_to_all x1, blocking collectives, all_to_all(): lax.all_to_all(blocks, 'member', split_axis=0, concat_axis=0, tiled=True)  98.2 us
    all_to_all x2, waiting for transfers between devices, all_to_all(): lax.all_to_all(blocks, 'member', split_axis=0, concat_axis=0, tiled=True)  60.4 us
    ppermute x8, starting transfers between devices, to_neighbours(): return (lax.ppermute(high, 'space', up), lax.ppermute(low, 'space', down))  23.4 us
    all_to_all x2, starting transfers between devices, all_to_all(): lax.all_to_all(blocks, 'member', split_axis=0, concat_axis=0, tiled=True)  12.9 us
    ppermute x8, waiting for transfers between devices, to_neighbours(): return (lax.ppermute(high, 'space', up), lax.ppermute(low, 'space', down))  9.47 us
    pallas_call x1, Pallas kernels, analyse(): pl.pallas_call(analyse_kernel, grid=(levels,), in_specs=[pl.BlockSpec(a.s...  9.36 us
    pallas_call x1, Pallas kernels, interior(): pl.pallas_call(interior_kernel, grid=(levels,), in_specs=[pl.BlockSpec((m...  7.08 us
    pallas_call x1, Pallas kernels, outer(): pl.pallas_call(outer_kernel, grid=(levels,), in_specs=[pl.BlockSpec((memb...  6.66 us
  transfers between devices with their start and end apart: 10, of which 6 were waited for; matrix products, arithmetic and copies ran while one was open for 0% of the time, Pallas kernels for 4%

profile of v4, /device:TPU:14, one launch (start us, length us, event | category | flops | bytes accessed | tf_op | source)
XLA Modules:
  0.0 241.1 jit_solution(14870149115514734992)
XLA Ops:
  0.0 7.1 %interior.1 = bf16[8,16,8192]{2,1,0:T(8,128)(2,1)} custom-call(bf16[16,8,4,8,512]{4,3,2,1,0:T(8,128)(2,1)} %state_ref.3, f32[8,4,8,512]{3,2,1,0:T(8,128)} %east_ref.2, f32[8,4,8,512]{3,2,1,0:T(8,128)} %north_ref.2), custom_call_target="tpu_custom_call" | custom-call | bytes 28800000 | tf_op jit(solution)/shard_map/interior/pallas_call | solution.py:122
  7.1 8.6 %all-to-all-start = ((bf16[8,16,8192]{2,1,0:T(8,128)(2,1)}), bf16[8,16,8192]{2,1,0:T(8,128)(2,1)S(1)}, u32[]{:S(2)}, u32[]{:S(2)}) async-start(bf16[8,16,8192]{2,1,0:T(8,128)(2,1)} %interior.1), calls=%async_computation | async-start | bytes 4194304 | tf_op jit(solution)/shard_map/all_to_all | solution.py:392
  15.7 2.2 copy-done
  17.9 1.6 edges.1
  19.5 1.9 collective-permute-start
  21.4 3.6 %collective-permute-start.1 = (bf16[4,2,16,4096]{3,2,1,0:T(8,128)(2,1)S(1)}, bf16[4,2,16,4096]{3,2,1,0:T(8,128)(2,1)S(1)}, u32[]{:S(2)}, u32[]{:S(2)}) collective-permute-start(bf16[4,2,16,4096]{3,2,1,0:T(8,128)(2,1)S(1)} %get-tuple-element.20), channel_id=1, source_target_pairs={{1,0},{2,1},{3,2},{4,3},{5,4},{6,5},{7,6},{8,7},{9,8},{10,9},{11,1... | collective-permute-start | bytes 3145736 | tf_op jit(solution)/shard_map/ppermute | solution.py:388
  25.8 1.9 collective-permute-start.3
  27.7 2.4 collective-permute-start.2
  30.8 3.2 %collective-permute-start.5 = (f32[2,512]{1,0:T(2,128)S(1)}, f32[2,512]{1,0:T(2,128)S(1)}, u32[]{:S(2)}, u32[]{:S(2)}) collective-permute-start(f32[2,512]{1,0:T(2,128)S(1)} %pad_maximum_fusion.1), channel_id=1, source_target_pairs={{1,0},{2,1},{3,2},{4,3},{5,4},{6,5},{7,6},{8,7},{9,8},{10,9},{11,1... | collective-permute-start | bytes 12296 | tf_op jit(solution)/shard_map/ppermute | solution.py:388
  34.0 4.8 %collective-permute-done.5 = f32[2,512]{1,0:T(2,128)S(1)} collective-permute-done((f32[2,512]{1,0:T(2,128)S(1)}, f32[2,512]{1,0:T(2,128)S(1)}, u32[]{:S(2)}, u32[]{:S(2)}) %collective-permute-start.5) | collective-permute-done | bytes 4128 | tf_op jit(solution)/shard_map/ppermute | solution.py:388
  38.8 6.1 %collective-permute-start.4 = (f32[2,512]{1,0:T(2,128)S(1)}, f32[2,512]{1,0:T(2,128)S(1)}, u32[]{:S(2)}, u32[]{:S(2)}) collective-permute-start(f32[2,512]{1,0:T(2,128)S(1)} %pad_maximum_fusion.1), channel_id=1, source_target_pairs={{0,1},{1,2},{2,3},{3,4},{4,5},{5,6},{6,7},{7,8},{8,9},{9,10},{10,1... | collective-permute-start | bytes 12296 | tf_op jit(solution)/shard_map/ppermute | solution.py:388
  45.7 6.7 %outer.1 = bf16[8,16,8192]{2,1,0:T(8,128)(2,1)S(1)} custom-call(bf16[16,8,4,8,512]{4,3,2,1,0:T(8,128)(2,1)S(1)} %copy-done, f32[8,4,8,512]{3,2,1,0:T(8,128)S(1)} %copy-done.2, f32[8,4,8,512]{3,2,1,0:T(8,128)S(1)} %copy-done.3, bf16[4,2,16,4096]{3,2,1,0:T(8,128)(2,1)S(1)} %collective-permute-done.below_ref, ...), custom_call_target="tpu_custom_call" | custom-call | bytes 32400000 | tf_op jit(solution)/shard_map/outer/pallas_call | solution.py:178
  52.4 1.3 copy-done.1
  53.7 13.2 %all-to-all-done.part_ref.inner_ref = bf16[8,16,8192]{2,1,0:T(8,128)(2,1)S(1)} async-done(((bf16[8,16,8192]{2,1,0:T(8,128)(2,1)}), bf16[8,16,8192]{2,1,0:T(8,128)(2,1)S(1)}, u32[]{:S(2)}, u32[]{:S(2)}) %all-to-all-start) | async-done | bytes 2097184 | tf_op jit(solution)/shard_map/all_to_all | solution.py:392
  66.9 4.4 %all-to-all-start.1 = ((bf16[8,16,8192]{2,1,0:T(8,128)(2,1)}), bf16[8,16,8192]{2,1,0:T(8,128)(2,1)}, u32[]{:S(2)}, u32[]{:S(2)}) async-start(bf16[8,16,8192]{2,1,0:T(8,128)(2,1)} %copy-done.1), calls=%async_computation.1 | async-start | bytes 4194304 | tf_op jit(solution)/shard_map/all_to_all | solution.py:392
  71.3 1.5 pick.2.refs_0_
  72.8 47.2 %all-to-all-done.1.part_ref.outer_ref = bf16[8,16,8192]{2,1,0:T(8,128)(2,1)} async-done(((bf16[8,16,8192]{2,1,0:T(8,128)(2,1)}), bf16[8,16,8192]{2,1,0:T(8,128)(2,1)}, u32[]{:S(2)}, u32[]{:S(2)}) %all-to-all-start.1) | async-done | bytes 2097184 | tf_op jit(solution)/shard_map/all_to_all | solution.py:392
  120.0 2.7 %pick.3.own_ref = bf16[128,512]{1,0:T(8,128)(2,1)S(1)} custom-call(s32[1,512]{1,0:T(1,128)S(1)} %get-tuple-element.39.place_ref, s32[1,512]{1,0:T(1,128)S(1)} %get-tuple-element.38.lane_ref, bf16[8,16,8192]{2,1,0:T(8,128)(2,1)} %all-to-all-done.1.part_ref.outer_ref, bf16[128,512]{1,0:T(8,128)(2,1)S(1)} %pick.2.refs_0_), custom_call_target="tpu_custom_call" | custom-call | bytes 14400000 | tf_op jit(solution)/shard_map/pick/pallas_call | solution.py:228
  122.7 1.9 collective-permute-start.7
  124.7 2.4 collective-permute-start.6
  127.2 3.8 %collective-permute-done.6.south_ref = bf16[128,512]{1,0:T(8,128)(2,1)S(1)} collective-permute-done((bf16[128,512]{1,0:T(8,128)(2,1)S(1)}, bf16[128,512]{1,0:T(8,128)(2,1)S(1)}, u32[]{:S(2)}, u32[]{:S(2)}) %collective-permute-start.6) | collective-permute-done | bytes 131104 | tf_op jit(solution)/shard_map/ppermute | solution.py:388
  131.0 9.4 %analyse.1 = bf16[8,16,4,8,512]{4,3,2,1,0:T(8,128)(2,1)S(1)} custom-call(bf16[128,512]{1,0:T(8,128)(2,1)S(1)} %pick.3.own_ref, bf16[128,512]{1,0:T(8,128)(2,1)S(1)} %collective-permute-done.6.south_ref, bf16[128,512]{1,0:T(8,128)(2,1)S(1)} %collective-permute-done.7.north_ref, f32[6,512]{1,0:T(8,128)S(1)} %pad_maximum_fusion.obs_ref, s32[3,512]{1,0:T(4,128)S(1)} %bitcast.40, ...), custom_call_target="tpu_custom_call" | custom-call | bytes 43200000 | tf_op jit(solution)/shard_map/analyse/pallas_call | solution.py:368
  140.3 98.2 %all_to_all.15 = bf16[8,16,4,8,512]{4,3,2,1,0:T(8,128)(2,1)S(1)} all-to-all(bf16[8,16,4,8,512]{4,3,2,1,0:T(8,128)(2,1)S(1)} %analyse.1), channel_id=1, replica_groups=mesh['member'=8,'space'=32] {'member'}, dimensions={0} | all-to-all | bytes 8388608 | tf_op jit(solution)/shard_map/all_to_all | solution.py:392
  238.6 2.5 %copy.13 = bf16[16,8,4,8,512]{4,3,2,1,0:T(8,128)(2,1)} copy(bf16[16,8,4,8,512]{4,3,2,0,1:T(8,128)(2,1)S(1)} %bitcast.41) | data formatting | bytes 8388608 | tf_op jit(solution)/shard_map/transpose | solution.py:431
  (32 shorter events, 1.7 us)
Async XLA Ops:
  7.1 18.0 %copy-start.2 = (f32[8,4,8,512]{3,2,1,0:T(8,128)S(1)}, f32[8,4,8,512]{3,2,1,0:T(8,128)}, u32[]{:S(2)}) copy-start(f32[8,4,8,512]{3,2,1,0:T(8,128)} %east_ref.2) | copy-start | bytes 1572868
  7.1 18.3 %copy-start.3 = (f32[8,4,8,512]{3,2,1,0:T(8,128)S(1)}, f32[8,4,8,512]{3,2,1,0:T(8,128)}, u32[]{:S(2)}) copy-start(f32[8,4,8,512]{3,2,1,0:T(8,128)} %north_ref.2) | copy-start | bytes 1572868
  7.1 59.8 %all-to-all-start = ((bf16[8,16,8192]{2,1,0:T(8,128)(2,1)}), bf16[8,16,8192]{2,1,0:T(8,128)(2,1)S(1)}, u32[]{:S(2)}, u32[]{:S(2)}) async-start(bf16[8,16,8192]{2,1,0:T(8,128)(2,1)} %interior.1), calls=%async_computation | async-start | bytes 4194304 | tf_op jit(solution)/shard_map/all_to_all | solution.py:392
  15.7 2.2 copy-start
  17.9 12.9 %copy-start.7 = (f32[1,1,512]{2,1,0:T(1,128)S(1)}, f32[1,1,512]{2,1,0:T(1,128)}, u32[]{:S(2)}) copy-start(f32[1,1,512]{2,1,0:T(1,128)} %param.13) | copy-start | bytes 6148
  17.9 12.9 %copy-start.4 = (f32[1,1,512]{2,1,0:T(1,128)S(1)}, f32[1,1,512]{2,1,0:T(1,128)}, u32[]{:S(2)}) copy-start(f32[1,1,512]{2,1,0:T(1,128)} %param.12) | copy-start | bytes 6148
  19.5 26.2 %collective-permute-start = (bf16[4,2,16,4096]{3,2,1,0:T(8,128)(2,1)S(1)}, bf16[4,2,16,4096]{3,2,1,0:T(8,128)(2,1)S(1)}, u32[]{:S(2)}, u32[]{:S(2)}) collective-permute-start(bf16[4,2,16,4096]{3,2,1,0:T(8,128)(2,1)S(1)} %get-tuple-element.19), channel_id=1, source_target_pairs={{0,1},{1,2},{2,3},{3,4},{4,5},{5,6},{6,7},{7,8},{8,9},{9,10},{10,1... | collective-permute-start | bytes 3145736 | tf_op jit(solution)/shard_map/ppermute | solution.py:388
  21.4 24.3 %collective-permute-start.1 = (bf16[4,2,16,4096]{3,2,1,0:T(8,128)(2,1)S(1)}, bf16[4,2,16,4096]{3,2,1,0:T(8,128)(2,1)S(1)}, u32[]{:S(2)}, u32[]{:S(2)}) collective-permute-start(bf16[4,2,16,4096]{3,2,1,0:T(8,128)(2,1)S(1)} %get-tuple-element.20), channel_id=1, source_target_pairs={{1,0},{2,1},{3,2},{4,3},{5,4},{6,5},{7,6},{8,7},{9,8},{10,9},{11,1... | collective-permute-start | bytes 3145736 | tf_op jit(solution)/shard_map/ppermute | solution.py:388
  25.8 19.9 %collective-permute-start.3 = (f32[2,4,8,512]{3,2,1,0:T(8,128)S(1)}, f32[2,4,8,512]{3,2,1,0:T(8,128)S(1)}, u32[]{:S(2)}, u32[]{:S(2)}) collective-permute-start(f32[2,4,8,512]{3,2,1,0:T(8,128)S(1)} %get-tuple-element.36), channel_id=1, source_target_pairs={{1,0},{2,1},{3,2},{4,3},{5,4},{6,5},{7,6},{8,7},{9,8},{10,9},{11,1... | collective-permute-start | bytes 393224 | tf_op jit(solution)/shard_map/ppermute | solution.py:388
  27.7 18.0 %collective-permute-start.2 = (f32[2,4,8,512]{3,2,1,0:T(8,128)S(1)}, f32[2,4,8,512]{3,2,1,0:T(8,128)S(1)}, u32[]{:S(2)}, u32[]{:S(2)}) collective-permute-start(f32[2,4,8,512]{3,2,1,0:T(8,128)S(1)} %get-tuple-element.37), channel_id=1, source_target_pairs={{0,1},{1,2},{2,3},{3,4},{4,5},{5,6},{6,7},{7,8},{8,9},{9,10},{10,1... | collective-permute-start | bytes 393224 | tf_op jit(solution)/shard_map/ppermute | solution.py:388
  30.8 8.0 %collective-permute-start.5 = (f32[2,512]{1,0:T(2,128)S(1)}, f32[2,512]{1,0:T(2,128)S(1)}, u32[]{:S(2)}, u32[]{:S(2)}) collective-permute-start(f32[2,512]{1,0:T(2,128)S(1)} %pad_maximum_fusion.1), channel_id=1, source_target_pairs={{1,0},{2,1},{3,2},{4,3},{5,4},{6,5},{7,6},{8,7},{9,8},{10,9},{11,1... | collective-permute-start | bytes 12296 | tf_op jit(solution)/shard_map/ppermute | solution.py:388
  38.8 6.9 %collective-permute-start.4 = (f32[2,512]{1,0:T(2,128)S(1)}, f32[2,512]{1,0:T(2,128)S(1)}, u32[]{:S(2)}, u32[]{:S(2)}) collective-permute-start(f32[2,512]{1,0:T(2,128)S(1)} %pad_maximum_fusion.1), channel_id=1, source_target_pairs={{0,1},{1,2},{2,3},{3,4},{4,5},{5,6},{6,7},{7,8},{8,9},{9,10},{10,1... | collective-permute-start | bytes 12296 | tf_op jit(solution)/shard_map/ppermute | solution.py:388
  52.4 1.3 copy-start.1
  53.7 17.5 %copy-start.6 = (s32[1,1,512]{2,1,0:T(1,128)S(1)}, s32[1,1,512]{2,1,0:T(1,128)}, u32[]{:S(2)}) copy-start(s32[1,1,512]{2,1,0:T(1,128)} %param.11) | copy-start | bytes 6148
  53.7 73.4 %copy-start.5 = (s32[1,1,3,512]{3,1,2,0:T(1,128)S(1)}, s32[1,1,3,512]{3,1,2,0:T(1,128)}, u32[]{:S(2)}) copy-start(s32[1,1,3,512]{3,1,2,0:T(1,128)} %param.15) | copy-start | bytes 18436
  66.9 53.1 %all-to-all-start.1 = ((bf16[8,16,8192]{2,1,0:T(8,128)(2,1)}), bf16[8,16,8192]{2,1,0:T(8,128)(2,1)}, u32[]{:S(2)}, u32[]{:S(2)}) async-start(bf16[8,16,8192]{2,1,0:T(8,128)(2,1)} %copy-done.1), calls=%async_computation.1 | async-start | bytes 4194304 | tf_op jit(solution)/shard_map/all_to_all | solution.py:392
  122.7 4.4 %collective-permute-start.7 = (bf16[128,512]{1,0:T(8,128)(2,1)S(1)}, bf16[128,512]{1,0:T(8,128)(2,1)S(1)}, u32[]{:S(2)}, u32[]{:S(2)}) collective-permute-start(bf16[128,512]{1,0:T(8,128)(2,1)S(1)} %pick.3.own_ref), channel_id=1, source_target_pairs={{1,0},{2,1},{3,2},{4,3},{5,4},{6,5},{7,6},{8,7},{9,8},{10,9},{11,1... | collective-permute-start | bytes 393224 | tf_op jit(solution)/shard_map/ppermute | solution.py:388
  124.7 6.3 %collective-permute-start.6 = (bf16[128,512]{1,0:T(8,128)(2,1)S(1)}, bf16[128,512]{1,0:T(8,128)(2,1)S(1)}, u32[]{:S(2)}, u32[]{:S(2)}) collective-permute-start(bf16[128,512]{1,0:T(8,128)(2,1)S(1)} %pick.3.own_ref), channel_id=1, source_target_pairs={{0,1},{1,2},{2,3},{3,4},{4,5},{5,6},{6,7},{7,8},{8,9},{9,10},{10,1... | collective-permute-start | bytes 393224 | tf_op jit(solution)/shard_map/ppermute | solution.py:388

commit v5 on v4

--- a/solution.py
+++ b/solution.py
@@ -9,8 +9,8 @@
 
 ITERS = 6
 LANES = 128
-VMEM_LIMIT = 20 * 1024 * 1024
-LEAVE_ROOM = 20 * 1024 * 1024
+VMEM_LIMIT = 14 * 1024 * 1024
+LEAVE_ROOM = 14 * 1024 * 1024
 
 
 def params(limit=VMEM_LIMIT):
@@ -255,7 +255,8 @@
     over = (((1,), (1 if turned else 0,)), ((), ()))
     dot = functools.partial(lax.dot_general, dimension_numbers=over, preferred_element_type=jnp.float32)
     (a, b), (c, d) = halves_of(left), halves_of(right)
-    return dot(a, c) + (dot(a, d) + dot(b, c))
+    axis = 1 if turned else 0
+    return dot(jnp.concatenate([a, a, b], axis=1), jnp.concatenate([c, d, c], axis=axis))
 
 
 def gram_of(raw, value, rinv, classes):
@@ -337,7 +338,7 @@
     at = lax.broadcasted_iota(jnp.int32, (ROWS, members * 4), 0)
     slot = lax.broadcasted_iota(jnp.int32, (ROWS, members * 4), 1) // members
     mean = jnp.zeros((ROWS, width), jnp.float32)
-    mixed = []
+    held = []
     for index, (part_ref, rows) in enumerate(((inner_ref, ROWS_INNER), (outer_ref, ROWS_OUTER))):
         flat = part_ref[...].reshape(members, part)
         stacked = jnp.concatenate([flat[:, i * width : (i + 1) * width] for i in range(4)], axis=0)
@@ -346,19 +347,22 @@
             source = jnp.where(slot == place, value, source)
         ones = jnp.where(at == source, 1.0, 0.0).astype(jnp.bfloat16)
         mean = mean + jnp.dot(ones, stacked, preferred_element_type=jnp.float32)
-        mixed.append(jnp.dot(mix[index], stacked, preferred_element_type=jnp.float32))
+        held.append(stacked)
     mean = mean * (1.0 / members)
-    shape = (members // 2, ROWS, LANES)
+    wide = 2 * LANES
+    shape = (members // 2, ROWS, wide)
     home = is_inner(lax.broadcasted_iota(jnp.int32, shape, 1))
-    for index in range(width // LANES):
-        lanes = slice(index * LANES, (index + 1) * LANES)
-        inner, outside = (value[:, lanes].reshape(shape) for value in mixed)
-        low = jnp.where(home, inner, outside) + mean[None, :, lanes] * rest[0]
-        high = pltpu.roll(jnp.where(home, outside, inner), 4, 1) + mean[None, :, lanes] * rest[1]
-        half = (groups, PAIR, ROWS, LANES)
+    rests = [jnp.concatenate([rest[i]] * (wide // LANES), axis=2) for i in range(2)]
+    for start in range(0, width, wide):
+        lanes = slice(start, start + wide)
+        inner, outside = (
+            jnp.dot(mix[i], held[i][:, lanes], preferred_element_type=jnp.float32).reshape(shape) for i in range(2)
+        )
+        low = jnp.where(home, inner, outside) + mean[None, :, lanes] * rests[0]
+        high = pltpu.roll(jnp.where(home, outside, inner), 4, 1) + mean[None, :, lanes] * rests[1]
+        half = (groups, PAIR, ROWS, wide)
         out_ref[:, 0:PAIR, 0, :, lanes] = low.reshape(half).astype(jnp.bfloat16)
         out_ref[:, PAIR : 2 * PAIR, 0, :, lanes] = high.reshape(half).astype(jnp.bfloat16)
-
 
 def analyse(raw, south, north, obs, classes, inner, outer_part, levels, width):
     groups, each, _ = inner.shape

time: 242 us -> 241 us (level)
  no operation moved by 1% of the time
where the time goes in v5:
time: 241 us; the launch traced here: 240 us
  blocking collectives  98.2 us (41%)
  waiting for transfers between devices  69.8 us (29%)
  starting transfers between devices  36.4 us (15%)
  Pallas kernels  27.9 us (12%)
  local copies, waits for them, and re-layouts  6.69 us (3%)
    all_to_all x1, blocking collectives, all_to_all(): lax.all_to_all(blocks, 'member', split_axis=0, concat_axis=0, tiled=True)  98.2 us
    all_to_all x2, waiting for transfers between devices, all_to_all(): lax.all_to_all(blocks, 'member', split_axis=0, concat_axis=0, tiled=True)  60.4 us
    ppermute x8, starting transfers between devices, to_neighbours(): return (lax.ppermute(high, 'space', up), lax.ppermute(low, 'space', down))  23.4 us
    all_to_all x2, starting transfers between devices, all_to_all(): lax.all_to_all(blocks, 'member', split_axis=0, concat_axis=0, tiled=True)  12.9 us
    ppermute x8, waiting for transfers between devices, to_neighbours(): return (lax.ppermute(high, 'space', up), lax.ppermute(low, 'space', down))  9.47 us
    pallas_call x1, Pallas kernels, analyse(): pl.pallas_call(analyse_kernel, grid=(levels,), in_specs=[pl.BlockSpec(a.s...  8.4 us
    pallas_call x1, Pallas kernels, interior(): pl.pallas_call(interior_kernel, grid=(levels,), in_specs=[pl.BlockSpec((m...  7.08 us
    pallas_call x1, Pallas kernels, outer(): pl.pallas_call(outer_kernel, grid=(levels,), in_specs=[pl.BlockSpec((memb...  6.66 us
  transfers between devices with their start and end apart: 10, of which 6 were waited for; matrix products, arithmetic and copies ran while one was open for 0% of the time, Pallas kernels for 4%

profile of v5, /device:TPU:14, one launch (start us, length us, event | category | flops | bytes accessed | tf_op | source)
XLA Modules:
  0.0 240.1 jit_solution(570550169938400118)
XLA Ops:
  0.0 7.1 %interior.1 = bf16[8,16,8192]{2,1,0:T(8,128)(2,1)} custom-call(bf16[16,8,4,8,512]{4,3,2,1,0:T(8,128)(2,1)} %state_ref.3, f32[8,4,8,512]{3,2,1,0:T(8,128)} %east_ref.2, f32[8,4,8,512]{3,2,1,0:T(8,128)} %north_ref.2), custom_call_target="tpu_custom_call" | custom-call | bytes 28800000 | tf_op jit(solution)/shard_map/interior/pallas_call | solution.py:122
  7.1 8.6 %all-to-all-start = ((bf16[8,16,8192]{2,1,0:T(8,128)(2,1)}), bf16[8,16,8192]{2,1,0:T(8,128)(2,1)S(1)}, u32[]{:S(2)}, u32[]{:S(2)}) async-start(bf16[8,16,8192]{2,1,0:T(8,128)(2,1)} %interior.1), calls=%async_computation | async-start | bytes 4194304 | tf_op jit(solution)/shard_map/all_to_all | solution.py:396
  15.7 2.2 copy-done
  17.9 1.6 edges.1
  19.5 1.9 collective-permute-start
  21.4 3.6 %collective-permute-start.1 = (bf16[4,2,16,4096]{3,2,1,0:T(8,128)(2,1)S(1)}, bf16[4,2,16,4096]{3,2,1,0:T(8,128)(2,1)S(1)}, u32[]{:S(2)}, u32[]{:S(2)}) collective-permute-start(bf16[4,2,16,4096]{3,2,1,0:T(8,128)(2,1)S(1)} %get-tuple-element.20), channel_id=1, source_target_pairs={{1,0},{2,1},{3,2},{4,3},{5,4},{6,5},{7,6},{8,7},{9,8},{10,9},{11,1... | collective-permute-start | bytes 3145736 | tf_op jit(solution)/shard_map/ppermute | solution.py:392
  25.8 1.9 collective-permute-start.3
  27.7 2.4 %collective-permute-start.2 = (f32[2,4,8,512]{3,2,1,0:T(8,128)S(1)}, f32[2,4,8,512]{3,2,1,0:T(8,128)S(1)}, u32[]{:S(2)}, u32[]{:S(2)}) collective-permute-start(f32[2,4,8,512]{3,2,1,0:T(8,128)S(1)} %get-tuple-element.37), channel_id=1, source_target_pairs={{0,1},{1,2},{2,3},{3,4},{4,5},{5,6},{6,7},{7,8},{8,9},{9,10},{10,1... | collective-permute-start | bytes 393224 | tf_op jit(solution)/shard_map/ppermute | solution.py:392
  30.8 3.2 %collective-permute-start.5 = (f32[2,512]{1,0:T(2,128)S(1)}, f32[2,512]{1,0:T(2,128)S(1)}, u32[]{:S(2)}, u32[]{:S(2)}) collective-permute-start(f32[2,512]{1,0:T(2,128)S(1)} %pad_maximum_fusion.1), channel_id=1, source_target_pairs={{1,0},{2,1},{3,2},{4,3},{5,4},{6,5},{7,6},{8,7},{9,8},{10,9},{11,1... | collective-permute-start | bytes 12296 | tf_op jit(solution)/shard_map/ppermute | solution.py:392
  34.0 4.8 %collective-permute-done.5 = f32[2,512]{1,0:T(2,128)S(1)} collective-permute-done((f32[2,512]{1,0:T(2,128)S(1)}, f32[2,512]{1,0:T(2,128)S(1)}, u32[]{:S(2)}, u32[]{:S(2)}) %collective-permute-start.5) | collective-permute-done | bytes 4128 | tf_op jit(solution)/shard_map/ppermute | solution.py:392
  38.8 6.1 %collective-permute-start.4 = (f32[2,512]{1,0:T(2,128)S(1)}, f32[2,512]{1,0:T(2,128)S(1)}, u32[]{:S(2)}, u32[]{:S(2)}) collective-permute-start(f32[2,512]{1,0:T(2,128)S(1)} %pad_maximum_fusion.1), channel_id=1, source_target_pairs={{0,1},{1,2},{2,3},{3,4},{4,5},{5,6},{6,7},{7,8},{8,9},{9,10},{10,1... | collective-permute-start | bytes 12296 | tf_op jit(solution)/shard_map/ppermute | solution.py:392
  45.7 6.7 %outer.1 = bf16[8,16,8192]{2,1,0:T(8,128)(2,1)S(1)} custom-call(bf16[16,8,4,8,512]{4,3,2,1,0:T(8,128)(2,1)S(1)} %copy-done, f32[8,4,8,512]{3,2,1,0:T(8,128)S(1)} %copy-done.2, f32[8,4,8,512]{3,2,1,0:T(8,128)S(1)} %copy-done.3, bf16[4,2,16,4096]{3,2,1,0:T(8,128)(2,1)S(1)} %collective-permute-done.below_ref, ...), custom_call_target="tpu_custom_call" | custom-call | bytes 32400000 | tf_op jit(solution)/shard_map/outer/pallas_call | solution.py:178
  52.4 1.3 copy-done.1
  53.7 13.2 %all-to-all-done.part_ref.inner_ref = bf16[8,16,8192]{2,1,0:T(8,128)(2,1)S(1)} async-done(((bf16[8,16,8192]{2,1,0:T(8,128)(2,1)}), bf16[8,16,8192]{2,1,0:T(8,128)(2,1)S(1)}, u32[]{:S(2)}, u32[]{:S(2)}) %all-to-all-start) | async-done | bytes 2097184 | tf_op jit(solution)/shard_map/all_to_all | solution.py:396
  66.9 4.4 %all-to-all-start.1 = ((bf16[8,16,8192]{2,1,0:T(8,128)(2,1)}), bf16[8,16,8192]{2,1,0:T(8,128)(2,1)}, u32[]{:S(2)}, u32[]{:S(2)}) async-start(bf16[8,16,8192]{2,1,0:T(8,128)(2,1)} %copy-done.1), calls=%async_computation.1 | async-start | bytes 4194304 | tf_op jit(solution)/shard_map/all_to_all | solution.py:396
  71.3 1.5 pick.2.refs_0_
  72.8 47.2 %all-to-all-done.1.part_ref.outer_ref = bf16[8,16,8192]{2,1,0:T(8,128)(2,1)} async-done(((bf16[8,16,8192]{2,1,0:T(8,128)(2,1)}), bf16[8,16,8192]{2,1,0:T(8,128)(2,1)}, u32[]{:S(2)}, u32[]{:S(2)}) %all-to-all-start.1) | async-done | bytes 2097184 | tf_op jit(solution)/shard_map/all_to_all | solution.py:396
  120.0 2.7 %pick.3.own_ref = bf16[128,512]{1,0:T(8,128)(2,1)S(1)} custom-call(s32[1,512]{1,0:T(1,128)S(1)} %get-tuple-element.39.place_ref, s32[1,512]{1,0:T(1,128)S(1)} %get-tuple-element.38.lane_ref, bf16[8,16,8192]{2,1,0:T(8,128)(2,1)} %all-to-all-done.1.part_ref.outer_ref, bf16[128,512]{1,0:T(8,128)(2,1)S(1)} %pick.2.refs_0_), custom_call_target="tpu_custom_call" | custom-call | bytes 14400000 | tf_op jit(solution)/shard_map/pick/pallas_call | solution.py:228
  122.7 1.9 collective-permute-start.7
  124.7 2.4 %collective-permute-start.6 = (bf16[128,512]{1,0:T(8,128)(2,1)S(1)}, bf16[128,512]{1,0:T(8,128)(2,1)S(1)}, u32[]{:S(2)}, u32[]{:S(2)}) collective-permute-start(bf16[128,512]{1,0:T(8,128)(2,1)S(1)} %pick.3.own_ref), channel_id=1, source_target_pairs={{0,1},{1,2},{2,3},{3,4},{4,5},{5,6},{6,7},{7,8},{8,9},{9,10},{10,1... | collective-permute-start | bytes 393224 | tf_op jit(solution)/shard_map/ppermute | solution.py:392
  127.2 3.8 %collective-permute-done.6.south_ref = bf16[128,512]{1,0:T(8,128)(2,1)S(1)} collective-permute-done((bf16[128,512]{1,0:T(8,128)(2,1)S(1)}, bf16[128,512]{1,0:T(8,128)(2,1)S(1)}, u32[]{:S(2)}, u32[]{:S(2)}) %collective-permute-start.6) | collective-permute-done | bytes 131104 | tf_op jit(solution)/shard_map/ppermute | solution.py:392
  131.0 8.4 %analyse.1 = bf16[8,16,4,8,512]{4,3,2,1,0:T(8,128)(2,1)S(1)} custom-call(bf16[128,512]{1,0:T(8,128)(2,1)S(1)} %pick.3.own_ref, bf16[128,512]{1,0:T(8,128)(2,1)S(1)} %collective-permute-done.6.south_ref, bf16[128,512]{1,0:T(8,128)(2,1)S(1)} %collective-permute-done.7.north_ref, f32[6,512]{1,0:T(8,128)S(1)} %pad_maximum_fusion.obs_ref, s32[3,512]{1,0:T(4,128)S(1)} %bitcast.40, ...), custom_call_target="tpu_custom_call" | custom-call | bytes 43200000 | tf_op jit(solution)/shard_map/analyse/pallas_call | solution.py:372
  139.4 98.2 %all_to_all.15 = bf16[8,16,4,8,512]{4,3,2,1,0:T(8,128)(2,1)S(1)} all-to-all(bf16[8,16,4,8,512]{4,3,2,1,0:T(8,128)(2,1)S(1)} %analyse.1), channel_id=1, replica_groups=mesh['member'=8,'space'=32] {'member'}, dimensions={0} | all-to-all | bytes 8388608 | tf_op jit(solution)/shard_map/all_to_all | solution.py:396
  237.6 2.5 %copy.13 = bf16[16,8,4,8,512]{4,3,2,1,0:T(8,128)(2,1)} copy(bf16[16,8,4,8,512]{4,3,2,0,1:T(8,128)(2,1)S(1)} %bitcast.41) | data formatting | bytes 8388608 | tf_op jit(solution)/shard_map/transpose | solution.py:435
  (32 shorter events, 1.7 us)
Async XLA Ops:
  7.1 18.0 %copy-start.2 = (f32[8,4,8,512]{3,2,1,0:T(8,128)S(1)}, f32[8,4,8,512]{3,2,1,0:T(8,128)}, u32[]{:S(2)}) copy-start(f32[8,4,8,512]{3,2,1,0:T(8,128)} %east_ref.2) | copy-start | bytes 1572868
  7.1 18.3 %copy-start.3 = (f32[8,4,8,512]{3,2,1,0:T(8,128)S(1)}, f32[8,4,8,512]{3,2,1,0:T(8,128)}, u32[]{:S(2)}) copy-start(f32[8,4,8,512]{3,2,1,0:T(8,128)} %north_ref.2) | copy-start | bytes 1572868
  7.1 59.8 %all-to-all-start = ((bf16[8,16,8192]{2,1,0:T(8,128)(2,1)}), bf16[8,16,8192]{2,1,0:T(8,128)(2,1)S(1)}, u32[]{:S(2)}, u32[]{:S(2)}) async-start(bf16[8,16,8192]{2,1,0:T(8,128)(2,1)} %interior.1), calls=%async_computation | async-start | bytes 4194304 | tf_op jit(solution)/shard_map/all_to_all | solution.py:396
  15.7 2.2 copy-start
  17.9 12.9 %copy-start.7 = (f32[1,1,512]{2,1,0:T(1,128)S(1)}, f32[1,1,512]{2,1,0:T(1,128)}, u32[]{:S(2)}) copy-start(f32[1,1,512]{2,1,0:T(1,128)} %param.13) | copy-start | bytes 6148
  17.9 12.9 %copy-start.4 = (f32[1,1,512]{2,1,0:T(1,128)S(1)}, f32[1,1,512]{2,1,0:T(1,128)}, u32[]{:S(2)}) copy-start(f32[1,1,512]{2,1,0:T(1,128)} %param.12) | copy-start | bytes 6148
  19.5 26.2 %collective-permute-start = (bf16[4,2,16,4096]{3,2,1,0:T(8,128)(2,1)S(1)}, bf16[4,2,16,4096]{3,2,1,0:T(8,128)(2,1)S(1)}, u32[]{:S(2)}, u32[]{:S(2)}) collective-permute-start(bf16[4,2,16,4096]{3,2,1,0:T(8,128)(2,1)S(1)} %get-tuple-element.19), channel_id=1, source_target_pairs={{0,1},{1,2},{2,3},{3,4},{4,5},{5,6},{6,7},{7,8},{8,9},{9,10},{10,1... | collective-permute-start | bytes 3145736 | tf_op jit(solution)/shard_map/ppermute | solution.py:392
  21.4 24.3 %collective-permute-start.1 = (bf16[4,2,16,4096]{3,2,1,0:T(8,128)(2,1)S(1)}, bf16[4,2,16,4096]{3,2,1,0:T(8,128)(2,1)S(1)}, u32[]{:S(2)}, u32[]{:S(2)}) collective-permute-start(bf16[4,2,16,4096]{3,2,1,0:T(8,128)(2,1)S(1)} %get-tuple-element.20), channel_id=1, source_target_pairs={{1,0},{2,1},{3,2},{4,3},{5,4},{6,5},{7,6},{8,7},{9,8},{10,9},{11,1... | collective-permute-start | bytes 3145736 | tf_op jit(solution)/shard_map/ppermute | solution.py:392
  25.8 19.9 %collective-permute-start.3 = (f32[2,4,8,512]{3,2,1,0:T(8,128)S(1)}, f32[2,4,8,512]{3,2,1,0:T(8,128)S(1)}, u32[]{:S(2)}, u32[]{:S(2)}) collective-permute-start(f32[2,4,8,512]{3,2,1,0:T(8,128)S(1)} %get-tuple-element.36), channel_id=1, source_target_pairs={{1,0},{2,1},{3,2},{4,3},{5,4},{6,5},{7,6},{8,7},{9,8},{10,9},{11,1... | collective-permute-start | bytes 393224 | tf_op jit(solution)/shard_map/ppermute | solution.py:392
  27.7 18.0 %collective-permute-start.2 = (f32[2,4,8,512]{3,2,1,0:T(8,128)S(1)}, f32[2,4,8,512]{3,2,1,0:T(8,128)S(1)}, u32[]{:S(2)}, u32[]{:S(2)}) collective-permute-start(f32[2,4,8,512]{3,2,1,0:T(8,128)S(1)} %get-tuple-element.37), channel_id=1, source_target_pairs={{0,1},{1,2},{2,3},{3,4},{4,5},{5,6},{6,7},{7,8},{8,9},{9,10},{10,1... | collective-permute-start | bytes 393224 | tf_op jit(solution)/shard_map/ppermute | solution.py:392
  30.8 8.0 %collective-permute-start.5 = (f32[2,512]{1,0:T(2,128)S(1)}, f32[2,512]{1,0:T(2,128)S(1)}, u32[]{:S(2)}, u32[]{:S(2)}) collective-permute-start(f32[2,512]{1,0:T(2,128)S(1)} %pad_maximum_fusion.1), channel_id=1, source_target_pairs={{1,0},{2,1},{3,2},{4,3},{5,4},{6,5},{7,6},{8,7},{9,8},{10,9},{11,1... | collective-permute-start | bytes 12296 | tf_op jit(solution)/shard_map/ppermute | solution.py:392
  38.8 6.9 %collective-permute-start.4 = (f32[2,512]{1,0:T(2,128)S(1)}, f32[2,512]{1,0:T(2,128)S(1)}, u32[]{:S(2)}, u32[]{:S(2)}) collective-permute-start(f32[2,512]{1,0:T(2,128)S(1)} %pad_maximum_fusion.1), channel_id=1, source_target_pairs={{0,1},{1,2},{2,3},{3,4},{4,5},{5,6},{6,7},{7,8},{8,9},{9,10},{10,1... | collective-permute-start | bytes 12296 | tf_op jit(solution)/shard_map/ppermute | solution.py:392
  52.4 1.3 copy-start.1
  53.7 17.5 %copy-start.6 = (s32[1,1,512]{2,1,0:T(1,128)S(1)}, s32[1,1,512]{2,1,0:T(1,128)}, u32[]{:S(2)}) copy-start(s32[1,1,512]{2,1,0:T(1,128)} %param.11) | copy-start | bytes 6148
  53.7 73.4 %copy-start.5 = (s32[1,1,3,512]{3,1,2,0:T(1,128)S(1)}, s32[1,1,3,512]{3,1,2,0:T(1,128)}, u32[]{:S(2)}) copy-start(s32[1,1,3,512]{3,1,2,0:T(1,128)} %param.15) | copy-start | bytes 18436
  66.9 53.1 %all-to-all-start.1 = ((bf16[8,16,8192]{2,1,0:T(8,128)(2,1)}), bf16[8,16,8192]{2,1,0:T(8,128)(2,1)}, u32[]{:S(2)}, u32[]{:S(2)}) async-start(bf16[8,16,8192]{2,1,0:T(8,128)(2,1)} %copy-done.1), calls=%async_computation.1 | async-start | bytes 4194304 | tf_op jit(solution)/shard_map/all_to_all | solution.py:396
  122.7 4.4 %collective-permute-start.7 = (bf16[128,512]{1,0:T(8,128)(2,1)S(1)}, bf16[128,512]{1,0:T(8,128)(2,1)S(1)}, u32[]{:S(2)}, u32[]{:S(2)}) collective-permute-start(bf16[128,512]{1,0:T(8,128)(2,1)S(1)} %pick.3.own_ref), channel_id=1, source_target_pairs={{1,0},{2,1},{3,2},{4,3},{5,4},{6,5},{7,6},{8,7},{9,8},{10,9},{11,1... | collective-permute-start | bytes 393224 | tf_op jit(solution)/shard_map/ppermute | solution.py:392
  124.7 6.3 %collective-permute-start.6 = (bf16[128,512]{1,0:T(8,128)(2,1)S(1)}, bf16[128,512]{1,0:T(8,128)(2,1)S(1)}, u32[]{:S(2)}, u32[]{:S(2)}) collective-permute-start(bf16[128,512]{1,0:T(8,128)(2,1)S(1)} %pick.3.own_ref), channel_id=1, source_target_pairs={{0,1},{1,2},{2,3},{3,4},{4,5},{5,6},{6,7},{7,8},{8,9},{9,10},{10,1... | collective-permute-start | bytes 393224 | tf_op jit(solution)/shard_map/ppermute | solution.py:392
